TPU v7x, 256 devices: a whole 4x4x8 slice. The times are simulated.
256 devices in a mesh: dp: 16 (over x, y), replica: 16 (over z, core).
Axes of the slice: x: 4, y: 4, z: 8, core: 2. Of those that a mesh axis runs over, the one named last changes fastest.
Arguments:
- picture_probes: bfloat16 [8192, 32, 256], P(('dp', 'replica')), may hold values from -2 to 2
- caption_vectors: bfloat16 [8192, 256], P(('dp', 'replica')), may hold values from -2 to 2
- chosen_slot_per_match: int32 [8192, 8192], P(('dp', 'replica')), may hold values from 0 to 31
- softmax_heat: float32 [1], replicated, may hold values from 0.05 to 0.1
Outputs:
- query_grads: float32 [8192, 32, 256], P(('dp', 'replica'))
- text_grads: float32 [8192, 256], P(('dp', 'replica'))
All inputs are finite; a program needn't handle non-finite values.
Results may differ from a plain program's by a relative error of at most 0.00105.
The roundings to bfloat16 on the way count: a program that leaves them out, or rounds other values in their place, can miss the bound.
Values may be sent and summed in bfloat16 or wider, within the bound.
No kernel may reach another device: no remote copies, remote signals or barrier semaphores. Data moves between devices by JAX's collectives and lax.ppermute only.
A program may use at most 64 MiB of HBM per device.

v0:
```python
import math

import jax
import jax.numpy as jnp
from jax import lax
from jax.sharding import PartitionSpec as P

EPS = 1e-06


def pick_query(dense, index, levels):
    hit = index[:, None, :] == levels[None, :, None]
    return jnp.sum(jnp.where(hit, dense, 0.0), axis=1)


def normalized_rows(values):
    wide = values.astype(jnp.float32)
    scale = lax.rsqrt(jnp.sum(wide * wide, axis=-1, keepdims=True) + EPS)
    return (wide * scale, scale)


def shards(picture_probes, caption_vectors, chosen_slot_per_match, softmax_heat):
    rows, count, width = picture_probes.shape
    query_normalized, q_scale = normalized_rows(picture_probes)
    t_unit, t_scale = normalized_rows(caption_vectors)
    q_half = query_normalized.astype(jnp.bfloat16)
    text_halved = t_unit.astype(jnp.bfloat16)
    all_text = lax.all_gather(text_halved, ("dp", "replica"), axis=0, tiled=True)
    total = all_text.shape[0]
    levels = jnp.arange(count, dtype=jnp.int32)
    reciprocal_length = 1.0 / softmax_heat[0]
    block = math.gcd(total, 1024)
    nblocks = total // block

    def similarity_increment(step, s_one):
        start = step * block
        piece = lax.dynamic_slice_in_dim(all_text, start, block, 0)
        dense = jnp.einsum("iqd,jd->iqj", q_half, piece, preferred_element_type=jnp.float32)
        fwd = lax.dynamic_slice_in_dim(chosen_slot_per_match, start, block, 1)
        return lax.dynamic_update_slice_in_dim(s_one, pick_query(dense, fwd, levels), start, 1)

    s_one = lax.fori_loop(0, nblocks, similarity_increment, jnp.zeros((rows, total), jnp.float32))
    e_one = jnp.exp(s_one * reciprocal_length)
    p_one = e_one / jnp.sum(e_one, axis=1, keepdims=True)
    running_sums = lax.psum(jnp.sum(e_one, axis=0), ("dp", "replica"))
    p_two = e_one / running_sums[None, :]
    first = lax.axis_index(("dp", "replica")) * rows
    diagonal = (
        jnp.arange(total, dtype=jnp.int32)[None, :]
        == (first + jnp.arange(rows, dtype=jnp.int32))[:, None]
    )
    target = jnp.where(diagonal, 0.9, 0.0) + 0.1 / total
    g_one = (p_one - target) * (0.5 * reciprocal_length)
    g_two = (p_two - target) * (0.5 * reciprocal_length)
    g_both = g_one + g_two

    def grad_step(step, carry):
        dq_acc, dt_all = carry
        start = step * block
        piece = lax.dynamic_slice_in_dim(all_text, start, block, 0)
        fwd = lax.dynamic_slice_in_dim(chosen_slot_per_match, start, block, 1)
        grad_piece = lax.dynamic_slice_in_dim(g_both, start, block, 1)
        mix = jnp.where(fwd[:, None, :] == levels[None, :, None], grad_piece[:, None, :], 0.0)
        mix = mix.astype(jnp.bfloat16)
        dq_acc = dq_acc + jnp.einsum("iqj,jd->iqd", mix, piece, preferred_element_type=jnp.float32)
        term = jnp.einsum("iqj,iqd->jd", mix, q_half, preferred_element_type=jnp.float32)
        dt_all = lax.dynamic_update_slice_in_dim(dt_all, term, start, 0)
        return (dq_acc, dt_all)

    dq_half, dt_all = lax.fori_loop(
        0,
        nblocks,
        grad_step,
        (jnp.zeros((rows, count, width), jnp.float32), jnp.zeros((total, width), jnp.float32)),
    )
    dt_half = lax.psum_scatter(dt_all, ("dp", "replica"), scatter_dimension=0, tiled=True)
    query_grads = (
        dq_half - query_normalized * jnp.sum(query_normalized * dq_half, axis=-1, keepdims=True)
    ) * q_scale
    text_grads = (dt_half - t_unit * jnp.sum(t_unit * dt_half, axis=-1, keepdims=True)) * t_scale
    return (query_grads, text_grads)


def solution(mesh):
    placed = (
        P(("dp", "replica"), None, None),
        P(("dp", "replica"), None),
        P(("dp", "replica"), None),
        P(),
    )
    return jax.shard_map(
        shards,
        mesh=mesh,
        in_specs=placed,
        out_specs=(P(("dp", "replica"), None, None), P(("dp", "replica"), None)),
        check_vma=False,
    )
```

profile of v0, /device:TPU:32, one launch (start us, length us, event | category | flops | bytes accessed | tf_op | source)
XLA Modules:
  0.0 1550.3 jit_solution(10129338185893090817)
XLA Ops:
  12.8 116.2 %all-gather.2.cloned.1.call-done = bf16[8192,256]{1,0:T(8,128)(2,1)} async-done(((bf16[32,256]{1,0:T(8,128)(2,1)}), bf16[8192,256]{1,0:T(8,128)(2,1)}) %all-gather.2.cloned.1.call-update) | async-done | bytes 4194320 | tf_op jit(solution)/shard_map/all_gather | solution.py:28
  129.0 23.2 %while.30 = (s32[]{:T(128)}, f32[32,8192]{1,0:T(8,128)S(1)}, s32[32,8192]{1,0:T(8,128)}, bf16[8192,256]{1,0:T(8,128)(2,1)}, bf16[32,32,256]{2,1,0:T(8,128)(2,1)S...) while((s32[]{:T(128)}, f32[32,8192]{1,0:T(8,128)S(1)}, s32[32,8192]{1,0:T(8,128)}, ...), condition=%wide.region_4.5_spmd.clone, body=%wide.region_2.4_spmd.clone.sunk | while | flops 539983872 | bytes 1835159 | solution.py:42
  130.0 1.9 fusion.54
  132.9 1.9 fusion.54
  135.8 1.9 fusion.54
  138.7 1.9 fusion.54
  141.6 1.9 fusion.54
  144.5 1.9 fusion.54
  147.4 1.9 fusion.54
  150.3 1.9 fusion.54
  152.6 76.3 %psum.7 = f32[8192]{0:T(1024)S(1)} all-reduce(f32[8192]{0:T(1024)S(1)} %get-tuple-element.293), channel_id=1, replica_groups=mesh['dp'=16,'replica'=16] {'dp','replica'}, use_global_device_ids=true, to_apply=%region_7.8 | all-reduce | flops 8192 | bytes 65536 | tf_op jit(solution)/shard_map/psum | solution.py:45
  229.4 3.8 broadcast_in_dim.71
  233.1 38.6 %while.31 = (s32[]{:T(128)}, f32[32,32,256]{2,1,0:T(8,128)S(1)}, f32[8192,256]{1,0:T(8,128)}, s32[32,8192]{1,0:T(8,128)}, bf16[32,8192]{1,0:T(8,128)(2,1)S(1)}, ...) while((s32[]{:T(128)}, f32[32,32,256]{2,1,0:T(8,128)S(1)}, ...), condition=%wide.region_9.10_spmd.clone, body=%wide.region_8.9_spmd.clone.sunk | while | flops 1078460416 | bytes 4980925 | solution.py:70
  234.0 2.1 fusion.57
  236.2 1.7 fusion.58
  238.9 2.1 fusion.57
  241.0 1.8 fusion.58
  243.7 2.1 fusion.57
  245.9 1.7 fusion.58
  248.5 2.1 fusion.57
  250.7 1.7 fusion.58
  253.4 2.1 fusion.57
  255.5 1.7 fusion.58
  258.2 2.1 fusion.57
  260.3 1.8 fusion.58
  263.0 2.1 fusion.57
  265.2 1.8 fusion.58
  267.8 2.1 fusion.57
  270.0 1.7 fusion.58
  272.8 6.2 fusion.27
  279.0 1262.1 %reduce-scatter.2.cloned.1.call-done = f32[32,256]{1,0:T(8,128)} async-done(((f32[8192,256]{1,0:T(8,128)}), f32[32,256]{1,0:T(8,128)}) %reduce-scatter.2.cloned.1.call-update) | async-done | bytes 32784 | tf_op jit(solution)/shard_map/reduce_scatter | solution.py:76
  1542.0 1.5 fusion.41
  (52 shorter events, 22.5 us)
Async XLA Ops:
  7.2 121.8 %all-gather.2.cloned.1.call-start = ((), (), s32[]{:S(2)}) async-start(), calls=%async_computation.1 | async-start | bytes 4210688 | tf_op jit(solution)/shard_map/all_gather | solution.py:28
  9.5 1531.6 %reduce-scatter.2.cloned.1.call-start = ((), (), s32[]{:S(2)}) async-start(), calls=%async_computation.2 | async-start | bytes 8421376 | tf_op jit(solution)/shard_map/reduce_scatter | solution.py:76
  271.7 1.0 copy-start
  271.7 1269.3 %copy-start.1 = (bf16[32,256]{1,0:T(8,128)(2,1)S(1)}, bf16[32,256]{1,0:T(8,128)(2,1)}, u32[]{:S(2)}) copy-start(bf16[32,256]{1,0:T(8,128)(2,1)} %param.9) | copy-start | bytes 49156
Sparse Core Ops, SparseCore 0:
  12.3 116.6 all-gather.1
  271.9 1269.1 reduce-scatter.1
where the time goes:
time: 1560 us; the launch traced here: 1550 us
  waiting for transfers between devices  1380 us (88%)
  blocking collectives  76.3 us (5%)
  matrix products  46.6 us (3%)
  local copies, waits for them, and re-layouts  19.7 us (1%)
    reduce_scatter x1, waiting for transfers between devices, shards(): lax.psum_scatter(dt_all, ('dp', 'replica'), scatter_dimension=0, tiled=True)  1260 us
    all_gather x1, waiting for transfers between devices, shards(): lax.all_gather(text_halved, ('dp', 'replica'), axis=0, tiled=True)  116 us
    psum x1, blocking collectives, shards(): running_sums = lax.psum(jnp.sum(e_one, axis=0), ('dp', 'replica'))  76.3 us
  transfers between devices with their start and end apart: 2, of which 2 were waited for; matrix products, arithmetic and copies ran while one was open for 1% of the time, Pallas kernels for 0%

commit v1 on v0

v1 whole, which is shorter than its diff:
```python
import jax
import jax.numpy as jnp
from jax import lax
from jax.experimental import pallas as pl
from jax.experimental.pallas import tpu as pltpu
from jax.sharding import Mesh
from jax.sharding import PartitionSpec as P

EPS = 1e-06
VMEM_LIMIT = 56 * 1024 * 1024
SWAP = [(0, 1), (1, 0)]


def normalized_rows(values):
    wide = values.astype(jnp.float32)
    scale = lax.rsqrt(jnp.sum(wide * wide, axis=-1, keepdims=True) + EPS)
    return (wide * scale, scale)


def spread(values, axis):
    count = lax.axis_size(axis)
    return lax.all_to_all(jnp.broadcast_to(values[None], (count, *values.shape)), axis, 0, 0, tiled=True)


def gather_members(near_ref, far_ref, query):
    return jnp.concatenate(
        [near_ref[0, query], near_ref[1, query], far_ref[0, query], far_ref[1, query]], axis=0
    )


def score_kernel(heat_ref, near_ref, far_ref, text_ref, slot_ref, e_ref, row_ref, column_ref):
    step = pl.program_id(0)
    count = near_ref.shape[1]
    images = e_ref.shape[0]
    group = 4
    slots = slot_ref[...].astype(jnp.float32)
    texts = text_ref[...]
    picked = jnp.zeros(e_ref.shape, jnp.float32)
    for first in range(0, count, group):
        queries = jnp.concatenate(
            [gather_members(near_ref, far_ref, first + k) for k in range(group)], axis=0
        )
        dense = lax.dot_general(
            queries, texts, (((1,), (1,)), ((), ())), preferred_element_type=jnp.float32
        )
        for k in range(group):
            picked = jnp.where(slots == float(first + k), dense[k * images : (k + 1) * images], picked)
    e = jnp.exp(picked * (1.0 / heat_ref[0]))
    e_ref[...] = e
    column_ref[...] = jnp.sum(e, axis=0, keepdims=True)

    @pl.when(step == 0)
    def _():
        row_ref[...] = jnp.zeros_like(row_ref)

    row_ref[...] += jnp.sum(e, axis=1, keepdims=True)


def grad_kernel(
    total,
    heat_ref,
    first_ref,
    near_ref,
    far_ref,
    text_ref,
    slot_ref,
    e_ref,
    row_ref,
    column_ref,
    dq_near_ref,
    dq_far_ref,
    dt_ref,
    queries,
    mix,
    mix_turned,
):
    step = pl.program_id(0)
    count = near_ref.shape[1]
    rows = near_ref.shape[2]
    images, tile = e_ref.shape

    @pl.when(step == 0)
    def _():
        for q in range(count):
            queries[q * images : (q + 1) * images] = gather_members(near_ref, far_ref, q)
        dq_near_ref[...] = jnp.zeros_like(dq_near_ref)
        dq_far_ref[...] = jnp.zeros_like(dq_far_ref)

    half = 0.5 * (1.0 / heat_ref[0])
    e = e_ref[...]
    image = lax.broadcasted_iota(jnp.int32, (images, tile), 0)
    text = lax.broadcasted_iota(jnp.int32, (images, tile), 1) + step * tile - first_ref[0]
    target = jnp.where((image == text) & (image < rows), 0.9, 0.0) + 0.1 / total
    g = (e / row_ref[...] - target) * half + (e / column_ref[...] - target) * half
    slots = slot_ref[...].astype(jnp.float32)
    g_turned = g.T
    slots_turned = slots.T
    for q in range(count):
        mix[q * images : (q + 1) * images] = jnp.where(slots == float(q), g, 0.0).astype(jnp.bfloat16)
        mix_turned[:, q * images : (q + 1) * images] = jnp.where(
            slots_turned == float(q), g_turned, 0.0
        ).astype(jnp.bfloat16)
    dt_ref[...] = jnp.dot(mix_turned[...], queries[...], preferred_element_type=jnp.float32)
    texts = text_ref[...]
    group = 8
    for first in range(0, count, group):
        part = jnp.dot(
            mix[first * images : (first + group) * images], texts, preferred_element_type=jnp.float32
        )
        for k in range(group):
            for member in range(4):
                out = dq_near_ref if member < 2 else dq_far_ref
                start = k * images + member * rows
                out[member % 2, first + k] += part[start : start + rows]


def scores(heat, near, far, texts, slots):
    _, count, rows, width = near.shape
    images, held = slots.shape
    tile = min(256, held)
    whole = pl.BlockSpec((2, count, rows, width), lambda s: (0, 0, 0, 0))
    return pl.pallas_call(
        score_kernel,
        grid=(held // tile,),
        in_specs=[
            pl.BlockSpec(memory_space=pltpu.SMEM),
            whole,
            whole,
            pl.BlockSpec((tile, width), lambda s: (s, 0)),
            pl.BlockSpec((images, tile), lambda s: (0, s)),
        ],
        out_specs=[
            pl.BlockSpec((images, tile), lambda s: (0, s)),
            pl.BlockSpec((images, 1), lambda s: (0, 0)),
            pl.BlockSpec((1, tile), lambda s: (0, s)),
        ],
        out_shape=[
            jax.ShapeDtypeStruct((images, held), jnp.float32),
            jax.ShapeDtypeStruct((images, 1), jnp.float32),
            jax.ShapeDtypeStruct((1, held), jnp.float32),
        ],
        compiler_params=pltpu.CompilerParams(
            dimension_semantics=("arbitrary",), vmem_limit_bytes=VMEM_LIMIT
        ),
        name="scores",
    )(heat, near, far, texts, slots)


def gradients(total, heat, first, near, far, texts, slots, e, row, column):
    _, count, rows, width = near.shape
    images, held = slots.shape
    tile = min(512, held)
    whole = pl.BlockSpec((2, count, rows, width), lambda s: (0, 0, 0, 0))

    def body(*refs):
        grad_kernel(total, *refs)

    return pl.pallas_call(
        body,
        grid=(held // tile,),
        in_specs=[
            pl.BlockSpec(memory_space=pltpu.SMEM),
            pl.BlockSpec(memory_space=pltpu.SMEM),
            whole,
            whole,
            pl.BlockSpec((tile, width), lambda s: (s, 0)),
            pl.BlockSpec((images, tile), lambda s: (0, s)),
            pl.BlockSpec((images, tile), lambda s: (0, s)),
            pl.BlockSpec((images, 1), lambda s: (0, 0)),
            pl.BlockSpec((1, tile), lambda s: (0, s)),
        ],
        out_specs=[whole, whole, pl.BlockSpec((tile, width), lambda s: (s, 0))],
        out_shape=[
            jax.ShapeDtypeStruct(near.shape, jnp.float32),
            jax.ShapeDtypeStruct(near.shape, jnp.float32),
            jax.ShapeDtypeStruct((held, width), jnp.float32),
        ],
        scratch_shapes=[
            pltpu.VMEM((count * images, width), jnp.bfloat16),
            pltpu.VMEM((count * images, tile), jnp.bfloat16),
            pltpu.VMEM((tile, count * images), jnp.bfloat16),
        ],
        compiler_params=pltpu.CompilerParams(
            dimension_semantics=("arbitrary",), vmem_limit_bytes=VMEM_LIMIT
        ),
        name="gradients",
    )(heat, first, near, far, texts, slots, e, row, column)


def shards(picture_probes, caption_vectors, chosen_slot_per_match, softmax_heat):
    rows, count, width = picture_probes.shape
    total = chosen_slot_per_match.shape[1]
    fours = total // (4 * rows)
    held = fours * rows
    z_bit = lax.axis_index("zp")
    c_bit = lax.axis_index("c")

    q_unit, q_scale = normalized_rows(picture_probes)
    t_unit, t_scale = normalized_rows(caption_vectors)
    t_half = t_unit.astype(jnp.bfloat16)
    q_half = q_unit.astype(jnp.bfloat16).transpose(1, 0, 2)

    parts = chosen_slot_per_match.astype(jnp.bfloat16).reshape(rows, fours, 2, 2, rows)
    parts = parts.transpose(2, 3, 0, 1, 4).reshape(2, 2, rows, held)

    def part(z_flip, c_flip):
        by_z = jnp.where(z_bit == z_flip, parts[0], parts[1])
        return jnp.where(c_bit == c_flip, by_z[0], by_z[1])

    def swap_z(values):
        return lax.ppermute(values, "zp", SWAP)

    def swap_c(values):
        return lax.ppermute(values, "c", SWAP)

    q_other = swap_z(q_half)
    slots_other = swap_z(jnp.stack([part(1, 0), part(1, 1)]))
    texts = spread(spread(t_half, "zo"), "dp").reshape(held, width)
    near = jnp.stack([q_half, q_other])
    far = swap_c(near)
    slots_far = swap_c(jnp.stack([part(0, 1), slots_other[1]]))
    slots = jnp.concatenate([part(0, 0), slots_other[0], slots_far[0], slots_far[1]], axis=0)

    e, row, column = scores(softmax_heat, near, far, texts, slots)

    row = row.reshape(2, 2, rows)
    row = row + swap_c(row[::-1])
    row = row + swap_z(row[:, ::-1])
    column = jnp.sum(spread(column, "dp"), axis=0)
    column = jnp.sum(spread(column, "zo"), axis=0)

    place = lax.axis_index("dp") * lax.axis_size("zo") + lax.axis_index("zo")
    first = (place * rows).astype(jnp.int32).reshape(1)
    dq_near, dq_far, dt = gradients(
        total, softmax_heat, first, near, far, texts, slots, e, row.reshape(4 * rows, 1), column
    )

    dq_near = dq_near + swap_c(dq_far)
    dq_other = swap_z(dq_near[1])
    dt = dt.reshape(lax.axis_size("dp"), held // lax.axis_size("dp"), width)
    dt = jnp.sum(lax.all_to_all(dt, "dp", 0, 0, tiled=True), axis=0)
    dt = dt.reshape(lax.axis_size("zo"), rows, width)
    dt = jnp.sum(lax.all_to_all(dt, "zo", 0, 0, tiled=True), axis=0)
    text_grads = (dt - t_unit * jnp.sum(t_unit * dt, axis=-1, keepdims=True)) * t_scale
    dq = (dq_near[0] + dq_other).transpose(1, 0, 2)
    query_grads = (dq - q_unit * jnp.sum(q_unit * dq, axis=-1, keepdims=True)) * q_scale
    return (query_grads, text_grads)


def solution(mesh):
    groups, replicas = mesh.devices.shape
    axes = ("dp", "zo", "zp", "c")
    split = Mesh(mesh.devices.reshape(groups, replicas // 4, 2, 2), axes)
    return jax.shard_map(
        shards,
        mesh=split,
        in_specs=(P(axes, None, None), P(axes, None), P(axes, None), P()),
        out_specs=(P(axes, None, None), P(axes, None)),
        check_vma=False,
    )
```

time: 1560 us -> 177 us (0.11)
  waiting for transfers between devices: 1380 us -> 39 us
  blocking collectives: 76.3 us -> 26.2 us
  matrix products: 46.6 us -> 0 us
  starting transfers between devices: 0.08 us -> 31.1 us
  Pallas kernels: 0 us -> 24.5 us
  other arithmetic: 14.1 us -> 36.8 us
    reduce_scatter x1 -> x0, waiting for transfers between devices: 1260 us -> none  [shards(): lax.psum_scatter(dt_all, ('dp', 'replica'), scatter_dimension=0, tiled=True)]
    all_gather x1 -> x0, waiting for transfers between devices: 116 us -> none  [shards(): lax.all_gather(text_halved, ('dp', 'replica'), axis=0, tiled=True)]
    psum x1 -> x0, blocking collectives: 76.3 us -> none  [shards(): running_sums = lax.psum(jnp.sum(e_one, axis=0), ('dp', 'replica'))]
    dot_general x24 -> x0, matrix products: 46.6 us -> none  [the longest x8 17.1 us: grad_step(): jnp.einsum('iqj,jd->iqd', mix, piece, preferred_element_type=jnp.float32)]
    all_to_all x0 -> x4, waiting for transfers between devices: none -> 28.6 us  [the longest x1 24.7 us: shards(): dt = jnp.sum(lax.all_to_all(dt, 'dp', 0, 0, tiled=True), axis=0)]
    all_to_all x0 -> x2, blocking collectives: none -> 26.2 us  [the longest x1 14.2 us: shards(): dt = jnp.sum(lax.all_to_all(dt, 'zo', 0, 0, tiled=True), axis=0)]
    all_to_all x0 -> x4, starting transfers between devices: none -> 26 us  [the longest x3 21.5 us: spread(): lax.all_to_all(jnp.broadcast_to(values[None], (count, *values.shape)), ax...]
    pallas_call x0 -> x2, Pallas kernels: none -> 24.5 us  [the longest x1 14.9 us: gradients(): pl.pallas_call(body, grid=(held // tile,), in_specs=[pl.BlockSpec(memory_...]
  transfers between devices with their start and end apart: 2 -> 12, of which waited for: 2 -> 6; matrix products, arithmetic and copies ran while one was open for 1% -> 21% of each run, Pallas kernels for 0% -> 0%
where the time goes in v1:
time: 177 us; the launch traced here: 175 us
  waiting for transfers between devices  39 us (22%)
  other arithmetic  36.8 us (21%)
  starting transfers between devices  31.1 us (18%)
  blocking collectives  26.2 us (15%)
  Pallas kernels  24.5 us (14%)
  local copies, waits for them, and re-layouts  15.6 us (9%)
    all_to_all x1, waiting for transfers between devices, shards(): dt = jnp.sum(lax.all_to_all(dt, 'dp', 0, 0, tiled=True), axis=0)  24.7 us
    all_to_all x3, starting transfers between devices, spread(): lax.all_to_all(jnp.broadcast_to(values[None], (count, *values.shape)), ax...  21.5 us
    select_n x1, other arithmetic, part(): return jnp.where(c_bit == c_flip, by_z[0], by_z[1])  14.9 us
    pallas_call x1, Pallas kernels, gradients(): pl.pallas_call(body, grid=(held // tile,), in_specs=[pl.BlockSpec(memory_...  14.9 us
    all_to_all x1, blocking collectives, shards(): dt = jnp.sum(lax.all_to_all(dt, 'zo', 0, 0, tiled=True), axis=0)  14.2 us
    all_to_all x1, blocking collectives, spread(): lax.all_to_all(jnp.broadcast_to(values[None], (count, *values.shape)), ax...  12 us
    pallas_call x1, Pallas kernels, scores(): pl.pallas_call(score_kernel, grid=(held // tile,), in_specs=[pl.BlockSpec...  9.63 us
    ppermute x4, waiting for transfers between devices, swap_z(): return lax.ppermute(values, 'zp', SWAP)  9.3 us
  transfers between devices with their start and end apart: 12, of which 6 were waited for; matrix products, arithmetic and copies ran while one was open for 21% of the time, Pallas kernels for 0%

profile of v1, /device:TPU:32, one launch (start us, length us, event | category | flops | bytes accessed | tf_op | source)
XLA Modules:
  0.0 174.6 jit_solution(17218446267868382426)
XLA Ops:
  2.9 7.6 %all-to-all-start = ((bf16[4,32,256]{2,1,0:T(8,128)(2,1)}), bf16[4,32,256]{2,1,0:T(8,128)(2,1)S(1)}, u32[]{:S(2)}, u32[]{:S(2)}) async-start(bf16[4,32,256]{2,1,0:T(8,128)(2,1)} %broadcast_in_dim.10), calls=%async_computation | async-start | bytes 131072 | tf_op jit(solution)/shard_map/all_to_all | solution.py:22
  10.5 1.3 convert_element_type.19
  11.7 1.6 reshape.76
  13.4 1.8 %broadcast_select_fusion.3 = (bf16[1,2,32,64,32]{4,1,0,3,2:T(2,128)(2,1)S(1)}, bf16[1,2,32,64,32]{4,1,0,3,2:T(2,128)(2,1)S(1)}) fusion(pred[]{:T(512)S(6)} %eq.17, bf16[2,2,32,64,32]{4,1,0,3,2:T(2,128)(2,1)S(1)} %bitcast.47, pred[]{:T(512)S(6)} %eq.18), kind=kLoop, calls=%fused_computation.4 | loop fusion | flops 262144 | bytes 1048578 | tf_op jit(solution)/shard_map/jit(_where)/select_n | solution.py:207
  15.2 14.9 %fusion.9 = (bf16[32,64,32]{2,1,0:T(8,128)(2,1)}, bf16[32,64,32]{2,1,0:T(8,128)(2,1)S(1)}, bf16[32,64,32]{2,1,0:T(8,128)(2,1)S(1)}, bf16[32,64,32]{2,1,0:T(8,128)(2,1)S(1)}) fusion(pred[]{:T(512)S(6)} %eq.16, bf16[1,2,32,64,32]{4,1,0,3,2:T(2,128)(2,1)S(1)} %get-tuple-element.26, pred[]{:T(512)S(6)} %eq.19, bf16[1,2,32,64,32]{4,1,0,3,2:T(2,128)(2,1)S(1)} %get-tuple-element.27), kind=kLoop, calls=%fused_computation.16 | loop fusion | flops 262144 | bytes 1048578 | tf_op jit(solution)/shard_map/jit(_where)/select_n | solution.py:208
  32.0 1.0 collective-permute-start.2
  33.7 1.1 collective-permute-start
  35.4 1.1 broadcast_in_dim.11
  36.5 7.0 %all-to-all-start.1 = ((bf16[16,4,32,256]{3,2,1,0:T(8,128)(2,1)}), bf16[16,4,32,256]{3,2,1,0:T(8,128)(2,1)S(1)}, u32[]{:S(2)}, u32[]{:S(2)}) async-start(bf16[16,4,32,256]{3,2,1,0:T(8,128)(2,1)} %broadcast_in_dim.11), calls=%async_computation.1 | async-start | bytes 2097152 | tf_op jit(solution)/shard_map/all_to_all | solution.py:22
  43.5 1.0 slice_bitcast_fusion.4
  44.5 6.6 %collective-permute-done = bf16[32,32,256]{2,1,0:T(8,128)(2,1)S(1)} collective-permute-done((bf16[32,32,256]{2,1,0:T(8,128)(2,1)S(1)}, bf16[32,32,256]{2,1,0:T(8,128)(2,1)S(1)}, u32[]{:S(2)}, u32[]{:S(2)}) %collective-permute-start) | collective-permute-done | bytes 524320 | tf_op jit(solution)/shard_map/ppermute | solution.py:211
  52.0 1.1 pad_maximum_fusion.near_ref.refs_2_
  54.7 1.6 select_n.62
  57.2 2.7 %all-to-all-done.1 = bf16[16,4,32,256]{3,2,1,0:T(8,128)(2,1)S(1)} async-done(((bf16[16,4,32,256]{3,2,1,0:T(8,128)(2,1)}), bf16[16,4,32,256]{3,2,1,0:T(8,128)(2,1)S(1)}, u32[]{:S(2)}, u32[]{:S(2)}) %all-to-all-start.1) | async-done | bytes 1048608 | tf_op jit(solution)/shard_map/all_to_all | solution.py:22
  60.8 9.6 %scores.1 = (f32[128,2048]{1,0:T(8,128)}, f32[128,1]{1,0:T(8,128)}, f32[1,2048]{1,0:T(1,128)}) custom-call(f32[1]{0:T(128)S(6)} %copy.31.heat_ref.refs_0_, bf16[2,32,32,256]{3,2,1,0:T(8,128)(2,1)} %copy-done.1, bf16[2,32,32,256]{3,2,1,0:T(8,128)(2,1)} %collective-permute-done.1.far_ref.refs_3_, bf16[2048,256]{1,0:T(8,128)(2,1)} %bitcast.45, ...), custom_call_target="tpu_custom_call" | custom-call | tf_op jit(solution)/shard_map/scores/pallas_call | solution.py:122
  71.2 12.0 %all_to_all.30 = f32[16,1,2048]{2,1,0:T(1,128)S(1)} all-to-all(f32[16,1,2048]{2,1,0:T(1,128)S(1)} %broadcast_in_dim.13), channel_id=1, replica_groups=mesh['dp'=16,'zo'=4,'zp'=2,'c'=2] {'dp'}, dimensions={0} | all-to-all | bytes 262144 | tf_op jit(solution)/shard_map/all_to_all | solution.py:22
  83.9 6.9 %all-to-all-start.3 = ((f32[4,1,2048]{2,1,0:T(1,128)}), f32[4,1,2048]{2,1,0:T(1,128)S(1)}, u32[]{:S(2)}, u32[]{:S(2)}) async-start(f32[4,1,2048]{2,1,0:T(1,128)} %broadcast_in_dim.14), calls=%async_computation.3 | async-start | bytes 65536 | tf_op jit(solution)/shard_map/all_to_all | solution.py:22
  91.9 1.1 collective-permute-done.4
  93.1 1.1 collective-permute-start.5
  94.2 2.7 %collective-permute-done.5 = f32[2,2,32]{2,1,0:T(2,128)S(1)} collective-permute-done((f32[2,2,32]{2,1,0:T(2,128)S(1)}, f32[2,2,32]{2,1,0:T(2,128)S(1)}, u32[]{:S(2)}, u32[]{:S(2)}) %collective-permute-start.5) | collective-permute-done | bytes 544 | tf_op jit(solution)/shard_map/ppermute | solution.py:211
  97.6 1.1 all-to-all-done.3
  99.4 14.9 %gradients.1 = (f32[2,32,32,256]{3,2,1,0:T(8,128)}, f32[2,32,32,256]{3,2,1,0:T(8,128)}, f32[2048,256]{1,0:T(8,128)}) custom-call(f32[1]{0:T(128)S(6)} %copy.31.heat_ref.refs_0_, s32[1]{0:T(128)} %bitcast.refs_1_, bf16[2,32,32,256]{3,2,1,0:T(8,128)(2,1)} %copy-done.1, bf16[2,32,32,256]{3,2,1,0:T(8,128)(2,1)} %collective-permute-done.1.far_ref.refs_3_, ...), custom_call_target="tpu_custom_call" | custom-call | tf_op jit(solution)/shard_map/gradients/pallas_call | solution.py:158
  114.2 4.4 %all-to-all-start.4 = ((f32[16,128,256]{2,1,0:T(8,128)}), f32[16,128,256]{2,1,0:T(8,128)}, u32[]{:S(2)}, u32[]{:S(2)}) async-start(f32[16,128,256]{2,1,0:T(8,128)} %bitcast.48), calls=%async_computation.4 | async-start | bytes 4194304 | tf_op jit(solution)/shard_map/all_to_all | solution.py:241
  118.7 1.3 copy-done.3
  120.0 2.6 %add.44 = f32[2,32,32,256]{3,2,1,0:T(8,128)S(1)} add(f32[2,32,32,256]{3,2,1,0:T(8,128)} %get-tuple-element.11, f32[2,32,32,256]{3,2,1,0:T(8,128)} %copy-done.3) | non-fusion elementwise | flops 524288 | bytes 6291456 | tf_op jit(solution)/shard_map/add | solution.py:238
  122.7 1.0 slice_bitcast_fusion
  123.7 1.0 collective-permute-start.7
  124.7 24.7 %all-to-all-done.4 = f32[16,128,256]{2,1,0:T(8,128)} async-done(((f32[16,128,256]{2,1,0:T(8,128)}), f32[16,128,256]{2,1,0:T(8,128)}, u32[]{:S(2)}, u32[]{:S(2)}) %all-to-all-start.4) | async-done | bytes 2097184 | tf_op jit(solution)/shard_map/all_to_all | solution.py:241
  149.4 1.7 reduce_sum.80
  151.2 14.2 %all_to_all.31 = f32[4,32,256]{2,1,0:T(8,128)S(1)} all-to-all(f32[4,32,256]{2,1,0:T(8,128)S(1)} %bitcast.49), channel_id=1, replica_groups=mesh['dp'=16,'zo'=4,'zp'=2,'c'=2] {'zo'}, dimensions={0} | all-to-all | bytes 262144 | tf_op jit(solution)/shard_map/all_to_all | solution.py:243
  166.3 6.8 %fusion.3 = f32[32,32,256]{2,0,1:T(8,128)S(1)} fusion(f32[32,32]{0,1:T(8,128)S(1)} %add_rsqrt_fusion, f32[32,32,256]{2,1,0:T(8,128)} %collective-permute-done.7, f32[2,32,32,256]{3,2,1,0:T(8,128)S(1)} %add.44, bf16[32,32,256]{2,1,0:T(8,128)(2,1)S(1)} %copy-done.2), kind=kOutput, calls=%fused_computation.9 | output fusion | flops 2622719 | bytes 6324224 | tf_op jit(solution)/shard_map/mul | solution.py:246
  173.1 1.6 copy.20
  (49 shorter events, 13.7 us)
Async XLA Ops:
  2.9 32.5 %all-to-all-start = ((bf16[4,32,256]{2,1,0:T(8,128)(2,1)}), bf16[4,32,256]{2,1,0:T(8,128)(2,1)S(1)}, u32[]{:S(2)}, u32[]{:S(2)}) async-start(bf16[4,32,256]{2,1,0:T(8,128)(2,1)} %broadcast_in_dim.10), calls=%async_computation | async-start | bytes 131072 | tf_op jit(solution)/shard_map/all_to_all | solution.py:22
  30.1 2.8 %copy-start.2 = (bf16[32,32,256]{2,1,0:T(8,128)(2,1)S(1)}, bf16[32,32,256]{2,1,0:T(8,128)(2,1)}, u32[]{:S(2)}) copy-start(bf16[32,32,256]{2,1,0:T(8,128)(2,1)} %param.4) | copy-start | bytes 1572868
  32.0 11.6 %collective-permute-start.2 = (bf16[2,32,2048]{2,1,0:T(8,128)(2,1)}, bf16[2,32,2048]{2,1,0:T(8,128)(2,1)}, u32[]{:S(2)}, u32[]{:S(2)}) collective-permute-start(bf16[2,32,2048]{2,1,0:T(8,128)(2,1)} %pad_maximum_fusion.2), channel_id=1, source_target_pairs={{0,2},{2,0},{1,3},{3,1},{4,6},{6,4},{5,7},{7,5},{8,10},{10,8},{9,1... | collective-permute-start | bytes 786440 | tf_op jit(solution)/shard_map/ppermute | solution.py:211
  33.7 17.5 %collective-permute-start = (bf16[32,32,256]{2,1,0:T(8,128)(2,1)S(1)}, bf16[32,32,256]{2,1,0:T(8,128)(2,1)S(1)}, u32[]{:S(2)}, u32[]{:S(2)}) collective-permute-start(bf16[32,32,256]{2,1,0:T(8,128)(2,1)S(1)} %get-tuple-element.29), channel_id=1, source_target_pairs={{0,2},{2,0},{1,3},{3,1},{4,6},{6,4},{5,7},{7,5},{8,10},{10,8},{9,1... | collective-permute-start | bytes 1572872 | tf_op jit(solution)/shard_map/ppermute | solution.py:211
  36.5 23.4 %all-to-all-start.1 = ((bf16[16,4,32,256]{3,2,1,0:T(8,128)(2,1)}), bf16[16,4,32,256]{3,2,1,0:T(8,128)(2,1)S(1)}, u32[]{:S(2)}, u32[]{:S(2)}) async-start(bf16[16,4,32,256]{3,2,1,0:T(8,128)(2,1)} %broadcast_in_dim.11), calls=%async_computation.1 | async-start | bytes 2097152 | tf_op jit(solution)/shard_map/all_to_all | solution.py:22
  51.2 0.8 copy-start.4
  53.1 6.8 %copy-start.1 = (bf16[2,32,32,256]{3,2,1,0:T(8,128)(2,1)}, bf16[2,32,32,256]{3,2,1,0:T(8,128)(2,1)S(1)}, u32[]{:S(2)}) copy-start(bf16[2,32,32,256]{3,2,1,0:T(8,128)(2,1)S(1)} %pad_maximum_fusion.near_ref.refs_2_) | copy-start | bytes 3145732
  53.1 6.8 %collective-permute-start.1 = (bf16[2,32,32,256]{3,2,1,0:T(8,128)(2,1)S(1)}, bf16[2,32,32,256]{3,2,1,0:T(8,128)(2,1)}, u32[]{:S(2)}, u32[]{:S(2)}) collective-permute-start(bf16[2,32,32,256]{3,2,1,0:T(8,128)(2,1)S(1)} %pad_maximum_fusion.near_ref.refs_2_), channel_id=1, source_target_pairs={{0,1},{1,0},{2,3},{3,2},{4,5},{5,4},{6,7},{7,6},{8,9},{9,8},{10,11... | collective-permute-start | bytes 3145736 | tf_op jit(solution)/shard_map/ppermute | solution.py:214
  53.3 3.0 %collective-permute-start.3 = (bf16[2,32,2048]{2,1,0:T(8,128)(2,1)S(1)}, bf16[2,32,2048]{2,1,0:T(8,128)(2,1)S(1)}, u32[]{:S(2)}, u32[]{:S(2)}) collective-permute-start(bf16[2,32,2048]{2,1,0:T(8,128)(2,1)S(1)} %pad_maximum_fusion.3), channel_id=1, source_target_pairs={{0,1},{1,0},{2,3},{3,2},{4,5},{5,4},{6,7},{7,6},{8,9},{9,8},{10,11... | collective-permute-start | bytes 786440 | tf_op jit(solution)/shard_map/ppermute | solution.py:214
  59.9 1.0 copy-start
  83.9 14.8 %all-to-all-start.3 = ((f32[4,1,2048]{2,1,0:T(1,128)}), f32[4,1,2048]{2,1,0:T(1,128)S(1)}, u32[]{:S(2)}, u32[]{:S(2)}) async-start(f32[4,1,2048]{2,1,0:T(1,128)} %broadcast_in_dim.14), calls=%async_computation.3 | async-start | bytes 65536 | tf_op jit(solution)/shard_map/all_to_all | solution.py:22
  91.9 1.2 collective-permute-start.4
  93.1 3.7 %collective-permute-start.5 = (f32[2,2,32]{2,1,0:T(2,128)S(1)}, f32[2,2,32]{2,1,0:T(2,128)S(1)}, u32[]{:S(2)}, u32[]{:S(2)}) collective-permute-start(f32[2,2,32]{2,1,0:T(2,128)S(1)} %rev.7), channel_id=1, source_target_pairs={{0,2},{2,0},{1,3},{3,1},{4,6},{6,4},{5,7},{7,5},{8,10},{10,8},{9,1... | collective-permute-start | bytes 1544 | tf_op jit(solution)/shard_map/ppermute | solution.py:211
  114.2 4.5 %collective-permute-start.6 = (f32[2,32,32,256]{3,2,1,0:T(8,128)}, f32[2,32,32,256]{3,2,1,0:T(8,128)S(1)}, u32[]{:S(2)}, u32[]{:S(2)}) collective-permute-start(f32[2,32,32,256]{3,2,1,0:T(8,128)} %get-tuple-element.12), channel_id=1, source_target_pairs={{0,1},{1,0},{2,3},{3,2},{4,5},{5,4},{6,7},{7,6},{8,9},{9,8},{10,11... | collective-permute-start | bytes 6291464 | tf_op jit(solution)/shard_map/ppermute | solution.py:214
  114.2 35.2 %all-to-all-start.4 = ((f32[16,128,256]{2,1,0:T(8,128)}), f32[16,128,256]{2,1,0:T(8,128)}, u32[]{:S(2)}, u32[]{:S(2)}) async-start(f32[16,128,256]{2,1,0:T(8,128)} %bitcast.48), calls=%async_computation.4 | async-start | bytes 4194304 | tf_op jit(solution)/shard_map/all_to_all | solution.py:241
  118.7 1.3 copy-start.3
  122.6 42.7 %copy-start.5 = (bf16[32,256]{1,0:T(8,128)(2,1)S(1)}, bf16[32,256]{1,0:T(8,128)(2,1)}, u32[]{:S(2)}) copy-start(bf16[32,256]{1,0:T(8,128)(2,1)} %param.5) | copy-start | bytes 49156
  123.7 42.6 %collective-permute-start.7 = (f32[32,32,256]{2,1,0:T(8,128)}, f32[32,32,256]{2,1,0:T(8,128)}, u32[]{:S(2)}, u32[]{:S(2)}) collective-permute-start(f32[32,32,256]{2,1,0:T(8,128)} %slice_bitcast_fusion), channel_id=1, source_target_pairs={{0,2},{2,0},{1,3},{3,1},{4,6},{6,4},{5,7},{7,5},{8,10},{10,8},{9,1... | collective-permute-start | bytes 3145736 | tf_op jit(solution)/shard_map/ppermute | solution.py:211

commit v2 on v0

v2 whole, which is shorter than its diff:
```python
import jax
import jax.numpy as jnp
from jax import lax
from jax.experimental import pallas as pl
from jax.experimental.pallas import tpu as pltpu
from jax.sharding import Mesh
from jax.sharding import PartitionSpec as P

EPS = 1e-06
LANES = 128
VMEM_LIMIT = 56 * 1024 * 1024
SWAP = [(0, 1), (1, 0)]
PARAMS = pltpu.CompilerParams(dimension_semantics=("arbitrary",), vmem_limit_bytes=VMEM_LIMIT)
SMEM = pl.BlockSpec(memory_space=pltpu.SMEM)


def normalized_rows(values):
    wide = values.astype(jnp.float32)
    scale = lax.rsqrt(jnp.sum(wide * wide, axis=-1, keepdims=True) + EPS)
    return (wide * scale, scale)


def spread(values, axis):
    count = lax.axis_size(axis)
    return lax.all_to_all(jnp.broadcast_to(values[None], (count, *values.shape)), axis, 0, 0, tiled=True)


def whole_of(shape):
    return pl.BlockSpec(shape, lambda s: (0,) * len(shape))


def text_kernel(caption_ref, copies_ref):
    unit, _ = normalized_rows(caption_ref[...])
    half = unit.astype(jnp.bfloat16)
    for k in range(copies_ref.shape[0]):
        copies_ref[k] = half


def half_texts(captions, copies):
    return pl.pallas_call(
        text_kernel,
        out_shape=jax.ShapeDtypeStruct((copies, *captions.shape), jnp.bfloat16),
        name="half_texts",
    )(captions)


def query_kernel(probe_ref, half_ref, units):
    rows, count, width = probe_ref.shape
    unit, _ = normalized_rows(probe_ref[...])
    unit = unit.reshape(rows * count, width)
    for k in range(width // LANES):
        at = slice(k * LANES, (k + 1) * LANES)
        units[k] = unit[:, at]
        for q in range(count):
            half_ref[q, :, at] = units[k, pl.ds(q, rows, stride=count), :].astype(jnp.bfloat16)


def half_queries(probes):
    rows, count, width = probes.shape
    block = min(16, rows)
    return pl.pallas_call(
        query_kernel,
        grid=(rows // block,),
        in_specs=[pl.BlockSpec((block, count, width), lambda s: (s, 0, 0))],
        out_specs=pl.BlockSpec((count, block, width), lambda s: (0, s, 0)),
        out_shape=jax.ShapeDtypeStruct((count, rows, width), jnp.bfloat16),
        scratch_shapes=[pltpu.VMEM((width // LANES, block * count, LANES), jnp.float32)],
        compiler_params=PARAMS,
        name="half_queries",
    )(probes)


def slot_kernel(bits_ref, slot_ref, own_ref, core_ref, chip_ref, order):
    rows, wide = slot_ref.shape
    lanes = 4 * rows
    block = 4 * lanes

    @pl.when(pl.program_id(0) == 0)
    def _():
        source = lax.broadcasted_iota(jnp.int32, (block, block), 0)
        goal = lax.broadcasted_iota(jnp.int32, (block, block), 1)
        member = (goal // lanes) ^ bits_ref[0]
        wanted = (goal % lanes) // rows * lanes + member * rows + goal % rows
        order[...] = jnp.where(source == wanted, 1.0, 0.0).astype(jnp.bfloat16)

    for k in range(wide // block):
        piece = slot_ref[:, k * block : (k + 1) * block].astype(jnp.float32).astype(jnp.bfloat16)
        moved = jnp.dot(piece, order[...], preferred_element_type=jnp.float32).astype(jnp.bfloat16)
        at = slice(k * lanes, (k + 1) * lanes)
        own_ref[:, at] = moved[:, :lanes]
        core_ref[:, at] = moved[:, lanes : 2 * lanes]
        chip_ref[0, :, at] = moved[:, 2 * lanes : 3 * lanes]
        chip_ref[1, :, at] = moved[:, 3 * lanes :]


def slot_parts(bits, slots):
    rows, total = slots.shape
    held = total // 4
    steps = max(1, total // (64 * rows))
    out = jax.ShapeDtypeStruct((rows, held), jnp.bfloat16)
    pair = jax.ShapeDtypeStruct((2, rows, held), jnp.bfloat16)
    spec = pl.BlockSpec((rows, held // steps), lambda s: (0, s))
    return pl.pallas_call(
        slot_kernel,
        grid=(steps,),
        in_specs=[SMEM, pl.BlockSpec((rows, total // steps), lambda s: (0, s))],
        out_specs=[spec, spec, pl.BlockSpec((2, rows, held // steps), lambda s: (0, 0, s))],
        out_shape=[out, out, pair],
        scratch_shapes=[pltpu.VMEM((16 * rows, 16 * rows), jnp.bfloat16)],
        compiler_params=PARAMS,
        name="slot_parts",
    )(bits, slots)


def slots_of(refs):
    return jnp.concatenate([ref[...].reshape(ref.shape[-2:]) for ref in refs], axis=0).astype(jnp.float32)


def score_kernel(heat_ref, *refs):
    query_refs, slot_refs, (text_ref, e_ref, row_ref, column_ref) = refs[:4], refs[4:8], refs[8:]
    count = query_refs[0].shape[0]
    images = e_ref.shape[0]
    group = 4
    slots = slots_of(slot_refs)
    texts = text_ref[...]
    picked = jnp.zeros(e_ref.shape, jnp.float32)
    for first in range(0, count, group):
        queries = jnp.concatenate(
            [ref[first + k] for k in range(group) for ref in query_refs], axis=0
        )
        dense = lax.dot_general(
            queries, texts, (((1,), (1,)), ((), ())), preferred_element_type=jnp.float32
        )
        for k in range(group):
            picked = jnp.where(slots == float(first + k), dense[k * images : (k + 1) * images], picked)
    e = jnp.exp(picked * (1.0 / heat_ref[0]))
    e_ref[...] = e
    column_ref[...] = jnp.sum(e, axis=0, keepdims=True)

    @pl.when(pl.program_id(0) == 0)
    def _():
        row_ref[...] = jnp.zeros_like(row_ref)

    row_ref[...] += jnp.sum(e, axis=1, keepdims=True)


def slot_specs(rows, tile):
    return [
        pl.BlockSpec((rows, tile), lambda s: (0, s)),
        pl.BlockSpec((1, rows, tile), lambda s: (0, 0, s)),
        pl.BlockSpec((rows, tile), lambda s: (0, s)),
        pl.BlockSpec((1, rows, tile), lambda s: (1, 0, s)),
    ]


def scores(heat, queries, slots, texts):
    count, rows, width = queries[0].shape
    held = texts.shape[0]
    images = 4 * rows
    tile = min(256, held)
    return pl.pallas_call(
        score_kernel,
        grid=(held // tile,),
        in_specs=[SMEM]
        + [whole_of((count, rows, width))] * 4
        + slot_specs(rows, tile)
        + [pl.BlockSpec((tile, width), lambda s: (s, 0))],
        out_specs=[
            pl.BlockSpec((images, tile), lambda s: (0, s)),
            pl.BlockSpec((images, 1), lambda s: (0, 0)),
            pl.BlockSpec((1, tile), lambda s: (0, s)),
        ],
        out_shape=[
            jax.ShapeDtypeStruct((images, held), jnp.float32),
            jax.ShapeDtypeStruct((images, 1), jnp.float32),
            jax.ShapeDtypeStruct((1, held), jnp.float32),
        ],
        compiler_params=PARAMS,
        name="scores",
    )(heat, *queries, *slots, texts)


def score_gradient(total, rows, heat_ref, first_ref, e_ref, row_ref, column_ref):
    images, tile = e_ref.shape
    half = 0.5 * (1.0 / heat_ref[0])
    e = e_ref[...]
    image = lax.broadcasted_iota(jnp.int32, (images, tile), 0)
    text = lax.broadcasted_iota(jnp.int32, (images, tile), 1) + pl.program_id(0) * tile - first_ref[0]
    target = jnp.where((image == text) & (image < rows), 0.9, 0.0) + 0.1 / total
    return (e / row_ref[...] - target) * half + (e / column_ref[...] - target) * half


def text_grad_kernel(total, heat_ref, first_ref, *refs):
    query_refs, slot_refs, (e_ref, row_ref, column_ref, dt_ref, queries, mix) = refs[:4], refs[4:8], refs[8:]
    count, rows, _ = query_refs[0].shape
    images = 4 * rows

    @pl.when(pl.program_id(0) == 0)
    def _():
        for q in range(count):
            for member, ref in enumerate(query_refs):
                start = q * images + member * rows
                queries[start : start + rows] = ref[q]

    g = score_gradient(total, rows, heat_ref, first_ref, e_ref, row_ref, column_ref).T
    slots = slots_of(slot_refs).T
    for q in range(count):
        mix[:, q * images : (q + 1) * images] = jnp.where(slots == float(q), g, 0.0).astype(jnp.bfloat16)
    dt_ref[...] = jnp.dot(mix[...], queries[...], preferred_element_type=jnp.float32)


def query_grad_kernel(total, heat_ref, first_ref, *refs):
    slot_refs, (text_ref, e_ref, row_ref, column_ref), outs, mix = refs[:4], refs[4:8], refs[8:11], refs[11]
    rows = slot_refs[0].shape[-2]
    images = 4 * rows
    count = outs[0].shape[0]
    g = score_gradient(total, rows, heat_ref, first_ref, e_ref, row_ref, column_ref)
    slots = slots_of(slot_refs)

    @pl.when(pl.program_id(0) == 0)
    def _():
        for out in outs:
            out[...] = jnp.zeros_like(out)

    for q in range(count):
        mix[q * images : (q + 1) * images] = jnp.where(slots == float(q), g, 0.0).astype(jnp.bfloat16)
    texts = text_ref[...]
    group = 8
    for first in range(0, count, group):
        part = jnp.dot(
            mix[first * images : (first + group) * images], texts, preferred_element_type=jnp.float32
        )
        for k in range(group):
            at = k * images
            outs[0][first + k] += part[at : at + rows]
            outs[1][first + k] += part[at + rows : at + 2 * rows]
            outs[2][0, first + k] += part[at + 2 * rows : at + 3 * rows]
            outs[2][1, first + k] += part[at + 3 * rows : at + 4 * rows]


def text_gradients(total, heat, first, queries, slots, e, row, column):
    count, rows, width = queries[0].shape
    images, held = e.shape
    tile = min(512, held)

    def body(*refs):
        text_grad_kernel(total, *refs)

    return pl.pallas_call(
        body,
        grid=(held // tile,),
        in_specs=[SMEM, SMEM]
        + [whole_of((count, rows, width))] * 4
        + slot_specs(rows, tile)
        + [
            pl.BlockSpec((images, tile), lambda s: (0, s)),
            whole_of((images, 1)),
            pl.BlockSpec((1, tile), lambda s: (0, s)),
        ],
        out_specs=pl.BlockSpec((tile, width), lambda s: (s, 0)),
        out_shape=jax.ShapeDtypeStruct((held, width), jnp.float32),
        scratch_shapes=[
            pltpu.VMEM((count * images, width), jnp.bfloat16),
            pltpu.VMEM((tile, count * images), jnp.bfloat16),
        ],
        compiler_params=PARAMS,
        name="text_gradients",
    )(heat, first, *queries, *slots, e, row, column)


def query_gradients(total, count, heat, first, slots, texts, e, row, column):
    images, held = e.shape
    rows = images // 4
    width = texts.shape[1]
    tile = min(512, held)
    one = (count, rows, width)

    def body(*refs):
        query_grad_kernel(total, *refs)

    return pl.pallas_call(
        body,
        grid=(held // tile,),
        in_specs=[SMEM, SMEM]
        + slot_specs(rows, tile)
        + [
            pl.BlockSpec((tile, width), lambda s: (s, 0)),
            pl.BlockSpec((images, tile), lambda s: (0, s)),
            whole_of((images, 1)),
            pl.BlockSpec((1, tile), lambda s: (0, s)),
        ],
        out_specs=[whole_of(one), whole_of(one), whole_of((2, *one))],
        out_shape=[
            jax.ShapeDtypeStruct(one, jnp.float32),
            jax.ShapeDtypeStruct(one, jnp.float32),
            jax.ShapeDtypeStruct((2, *one), jnp.float32),
        ],
        scratch_shapes=[pltpu.VMEM((count * images, tile), jnp.bfloat16)],
        compiler_params=PARAMS,
        name="query_gradients",
    )(heat, first, *slots, texts, e, row, column)


def finish_kernel(probe_ref, own_ref, core_ref, chip_ref, out_ref, total):
    block, count, width = probe_ref.shape
    added = (own_ref[...] + core_ref[0] + chip_ref[...]).reshape(count * block, width)
    halves = range(width // LANES)
    for k in halves:
        total[k] = added[:, k * LANES : (k + 1) * LANES]
    for i in range(block):
        unit, scale = normalized_rows(probe_ref[i])
        dq = jnp.concatenate([total[k, pl.ds(i, count, stride=block), :] for k in halves], axis=1)
        out_ref[i] = (dq - unit * jnp.sum(unit * dq, axis=-1, keepdims=True)) * scale


def finish_queries(probes, own, core, chip):
    rows, count, width = probes.shape
    block = min(8, rows)
    moved = pl.BlockSpec((count, block, width), lambda s: (0, s, 0))
    kept = pl.BlockSpec((block, count, width), lambda s: (s, 0, 0))
    return pl.pallas_call(
        finish_kernel,
        grid=(rows // block,),
        in_specs=[kept, moved, pl.BlockSpec((1, count, block, width), lambda s: (0, 0, s, 0)), moved],
        out_specs=kept,
        out_shape=jax.ShapeDtypeStruct(probes.shape, jnp.float32),
        scratch_shapes=[pltpu.VMEM((width // LANES, count * block, LANES), jnp.float32)],
        compiler_params=PARAMS,
        name="finish_queries",
    )(probes, own, core, chip)


def swap_z(values):
    return lax.ppermute(values, "zp", SWAP)


def swap_c(values):
    return lax.ppermute(values, "c", SWAP)


def shards(picture_probes, caption_vectors, chosen_slot_per_match, softmax_heat):
    rows, count, width = picture_probes.shape
    total = chosen_slot_per_match.shape[1]
    held = total // 4
    groups, outer = lax.axis_size("dp"), lax.axis_size("zo")

    text_copies = half_texts(caption_vectors, outer)
    texts = lax.all_to_all(text_copies, "zo", 0, 0, tiled=True)
    texts = spread(texts.reshape(outer * rows, width), "dp").reshape(held, width)

    bits = (lax.axis_index("zp") * 2 + lax.axis_index("c")).astype(jnp.int32).reshape(1)
    q_own = half_queries(picture_probes)
    slots_own, slots_core, slots_chip = slot_parts(bits, chosen_slot_per_match)
    q_chip = swap_z(q_own)
    slots_chip = swap_z(slots_chip)
    queries = (q_own, q_chip, swap_c(q_own), swap_c(q_chip))
    slots = (slots_own, slots_chip, swap_c(slots_core), swap_c(slots_chip))

    e, row, column = scores(softmax_heat, queries, slots, texts)

    row = row.reshape(2, 2, rows)
    row = row + swap_c(row[::-1])
    row = row + swap_z(row[:, ::-1])
    row = row.reshape(4 * rows, 1)
    column = jnp.sum(spread(column, "dp"), axis=0)
    column = jnp.sum(spread(column, "zo"), axis=0)

    place = lax.axis_index("dp") * outer + lax.axis_index("zo")
    first = (place * rows).astype(jnp.int32).reshape(1)
    dt = text_gradients(total, softmax_heat, first, queries, slots, e, row, column)
    dt = lax.all_to_all(dt.reshape(groups, outer * rows, width), "dp", 0, 0, tiled=True)
    dq_own, dq_chip, dq_far = query_gradients(
        total, count, softmax_heat, first, slots, texts, e, row, column
    )
    dq_near = swap_c(dq_far)
    dq_chip = swap_z(dq_chip + dq_near[1])
    dt = jnp.sum(dt, axis=0).reshape(outer, rows, width)
    dt = lax.all_to_all(dt, "zo", 0, 0, tiled=True)
    query_grads = finish_queries(picture_probes, dq_own, dq_near, dq_chip)
    dt, query_grads = lax.optimization_barrier((dt, query_grads))
    dt = jnp.sum(dt, axis=0)
    t_unit, t_scale = normalized_rows(caption_vectors)
    text_grads = (dt - t_unit * jnp.sum(t_unit * dt, axis=-1, keepdims=True)) * t_scale
    return (query_grads, text_grads)


def solution(mesh):
    groups, replicas = mesh.devices.shape
    axes = ("dp", "zo", "zp", "c")
    split = Mesh(mesh.devices.reshape(groups, replicas // 4, 2, 2), axes)
    return jax.shard_map(
        shards,
        mesh=split,
        in_specs=(P(axes, None, None), P(axes, None), P(axes, None), P()),
        out_specs=(P(axes, None, None), P(axes, None)),
        check_vma=False,
    )
```

time: 1560 us -> 149 us (0.10)
  waiting for transfers between devices: 1380 us -> 48.1 us
  blocking collectives: 76.3 us -> 12.2 us
  matrix products: 46.6 us -> 0 us
  Pallas kernels: 0 us -> 40.8 us
  starting transfers between devices: 0.08 us -> 33.1 us
    reduce_scatter x1 -> x0, waiting for transfers between devices: 1260 us -> none  [shards(): lax.psum_scatter(dt_all, ('dp', 'replica'), scatter_dimension=0, tiled=True)]
    all_gather x1 -> x0, waiting for transfers between devices: 116 us -> none  [shards(): lax.all_gather(text_halved, ('dp', 'replica'), axis=0, tiled=True)]
    psum x1 -> x0, blocking collectives: 76.3 us -> none  [shards(): running_sums = lax.psum(jnp.sum(e_one, axis=0), ('dp', 'replica'))]
    dot_general x24 -> x0, matrix products: 46.6 us -> none  [the longest x8 17.1 us: grad_step(): jnp.einsum('iqj,jd->iqd', mix, piece, preferred_element_type=jnp.float32)]
    pallas_call x0 -> x7, Pallas kernels: none -> 40.8 us  [the longest x1 9.83 us: scores(): pl.pallas_call(score_kernel, grid=(held // tile,), in_specs=[SMEM] + [who...]
    all_to_all x0 -> x5, waiting for transfers between devices: none -> 38.9 us  [the longest x1 27.1 us: shards(): lax.all_to_all(dt.reshape(groups, outer * rows, width), 'dp', 0, 0, tiled...]
    all_to_all x0 -> x5, starting transfers between devices: none -> 27.7 us  [the longest x2 10.3 us: spread(): lax.all_to_all(jnp.broadcast_to(values[None], (count, *values.shape)), ax...]
  transfers between devices with their start and end apart: 2 -> 15, of which waited for: 2 -> 9; matrix products, arithmetic and copies ran while one was open for 1% -> 4% of each run, Pallas kernels for 0% -> 14%
where the time goes in v2:
time: 149 us; the launch traced here: 147 us
  waiting for transfers between devices  48.1 us (32%)
  Pallas kernels  40.8 us (27%)
  starting transfers between devices  33.1 us (22%)
  blocking collectives  12.2 us (8%)
  other arithmetic  5.8 us (4%)
  local copies, waits for them, and re-layouts  5.27 us (4%)
    all_to_all x1, waiting for transfers between devices, shards(): lax.all_to_all(dt.reshape(groups, outer * rows, width), 'dp', 0, 0, tiled...  27.1 us
    all_to_all x1, blocking collectives, spread(): lax.all_to_all(jnp.broadcast_to(values[None], (count, *values.shape)), ax...  12.2 us
    all_to_all x2, starting transfers between devices, spread(): lax.all_to_all(jnp.broadcast_to(values[None], (count, *values.shape)), ax...  10.3 us
    pallas_call x1, Pallas kernels, scores(): pl.pallas_call(score_kernel, grid=(held // tile,), in_specs=[SMEM] + [who...  9.83 us
    pallas_call x1, Pallas kernels, query_gradients(): pl.pallas_call(body, grid=(held // tile,), in_specs=[SMEM, SMEM] + slot_s...  9.24 us
    pallas_call x1, Pallas kernels, text_gradients(): pl.pallas_call(body, grid=(held // tile,), in_specs=[SMEM, SMEM] + [whole...  8.91 us
    all_to_all x1, starting transfers between devices, shards(): texts = lax.all_to_all(text_copies, 'zo', 0, 0, tiled=True)  7.56 us
    ppermute x4, waiting for transfers between devices, swap_z(): return lax.ppermute(values, 'zp', SWAP)  7.52 us
  transfers between devices with their start and end apart: 15, of which 9 were waited for; matrix products, arithmetic and copies ran while one was open for 4% of the time, Pallas kernels for 14%

profile of v2, /device:TPU:32, one launch (start us, length us, event | category | flops | bytes accessed | tf_op | source)
XLA Modules:
  0.0 146.7 jit_solution(18222518718624469819)
XLA Ops:
  0.6 1.4 half_texts.1
  2.1 7.6 %all-to-all-start = ((bf16[4,32,256]{2,1,0:T(8,128)(2,1)}), bf16[4,32,256]{2,1,0:T(8,128)(2,1)S(1)}, u32[]{:S(2)}, u32[]{:S(2)}) async-start(bf16[4,32,256]{2,1,0:T(8,128)(2,1)} %half_texts.1), calls=%async_computation | async-start | bytes 131072 | tf_op jit(solution)/shard_map/all_to_all | solution.py:348
  9.6 2.8 %half_queries.1.refs_0_.refs_2_ = bf16[32,32,256]{2,1,0:T(8,128)(2,1)} custom-call(bf16[32,32,256]{2,1,0:T(8,128)(2,1)} %probe_ref.3), custom_call_target="tpu_custom_call" | custom-call | tf_op jit(solution)/shard_map/half_queries/pallas_call | solution.py:61
  12.4 1.0 collective-permute-start
  13.5 4.4 %all-to-all-done = bf16[4,32,256]{2,1,0:T(8,128)(2,1)S(1)} async-done(((bf16[4,32,256]{2,1,0:T(8,128)(2,1)}), bf16[4,32,256]{2,1,0:T(8,128)(2,1)S(1)}, u32[]{:S(2)}, u32[]{:S(2)}) %all-to-all-start) | async-done | bytes 65568 | tf_op jit(solution)/shard_map/all_to_all | solution.py:348
  17.9 1.1 broadcast_in_dim.11
  18.9 7.0 %all-to-all-start.1 = ((bf16[16,128,256]{2,1,0:T(8,128)(2,1)}), bf16[16,128,256]{2,1,0:T(8,128)(2,1)S(1)}, u32[]{:S(2)}, u32[]{:S(2)}) async-start(bf16[16,128,256]{2,1,0:T(8,128)(2,1)} %broadcast_in_dim.11), calls=%async_computation.1 | async-start | bytes 2097152 | tf_op jit(solution)/shard_map/all_to_all | solution.py:25
  26.0 4.3 %slot_parts.1 = (bf16[32,2048]{1,0:T(8,128)(2,1)}, bf16[32,2048]{1,0:T(8,128)(2,1)}, bf16[2,32,2048]{2,1,0:T(8,128)(2,1)}) custom-call(s32[1]{0:T(128)} %bitcast.1.bits_ref, s32[32,8192]{1,0:T(8,128)} %slot_ref.1), custom_call_target="tpu_custom_call" | custom-call | tf_op jit(solution)/shard_map/slot_parts/pallas_call | solution.py:103
  30.3 1.1 collective-permute-start.3
  31.9 5.0 %collective-permute-done.3.refs_5_.refs_7_.refs_3_ = bf16[2,32,2048]{2,1,0:T(8,128)(2,1)S(1)} collective-permute-done((bf16[2,32,2048]{2,1,0:T(8,128)(2,1)}, bf16[2,32,2048]{2,1,0:T(8,128)(2,1)S(1)}, u32[]{:S(2)}, u32[]{:S(2)}) %collective-permute-start.3) | collective-permute-done | bytes 262176 | tf_op jit(solution)/shard_map/ppermute | solution.py:334
  38.7 2.9 %all-to-all-done.1 = bf16[16,128,256]{2,1,0:T(8,128)(2,1)S(1)} async-done(((bf16[16,128,256]{2,1,0:T(8,128)(2,1)}), bf16[16,128,256]{2,1,0:T(8,128)(2,1)S(1)}, u32[]{:S(2)}, u32[]{:S(2)}) %all-to-all-start.1) | async-done | bytes 1048608 | tf_op jit(solution)/shard_map/all_to_all | solution.py:25
  41.7 0.9 copy-done
  42.6 9.8 %scores.1 = (f32[128,2048]{1,0:T(8,128)}, f32[128,1]{1,0:T(8,128)}, f32[1,2048]{1,0:T(1,128)}) custom-call(f32[1]{0:T(128)S(6)} %copy.18.heat_ref.refs_0_, bf16[32,32,256]{2,1,0:T(8,128)(2,1)} %half_queries.1.refs_0_.refs_2_, bf16[32,32,256]{2,1,0:T(8,128)(2,1)} %copy-done.4, bf16[32,32,256]{2,1,0:T(8,128)(2,1)} %copy-done.5, ...), custom_call_target="tpu_custom_call" | custom-call | tf_op jit(solution)/shard_map/scores/pallas_call | solution.py:161
  52.4 0.8 broadcast_in_dim.26
  53.2 12.2 %all_to_all.30 = f32[16,1,2048]{2,1,0:T(1,128)S(1)} all-to-all(f32[16,1,2048]{2,1,0:T(1,128)S(1)} %broadcast_in_dim.26), channel_id=1, replica_groups=mesh['dp'=16,'zo'=4,'zp'=2,'c'=2] {'dp'}, dimensions={0} | all-to-all | bytes 262144 | tf_op jit(solution)/shard_map/all_to_all | solution.py:25
  66.1 3.3 %all-to-all-start.3 = ((f32[4,1,2048]{2,1,0:T(1,128)}), f32[4,1,2048]{2,1,0:T(1,128)S(1)}, u32[]{:S(2)}, u32[]{:S(2)}) async-start(f32[4,1,2048]{2,1,0:T(1,128)} %broadcast_in_dim.27), calls=%async_computation.3 | async-start | bytes 65536 | tf_op jit(solution)/shard_map/all_to_all | solution.py:25
  69.4 0.9 reduce.2
  70.4 1.1 collective-permute-done.6
  71.6 1.2 collective-permute-start.7
  72.8 2.5 %collective-permute-done.7 = f32[2,2,32]{2,1,0:T(2,128)S(1)} collective-permute-done((f32[2,2,32]{2,1,0:T(2,128)S(1)}, f32[2,2,32]{2,1,0:T(2,128)S(1)}, u32[]{:S(2)}, u32[]{:S(2)}) %collective-permute-start.7) | collective-permute-done | bytes 544 | tf_op jit(solution)/shard_map/ppermute | solution.py:334
  76.1 1.1 all-to-all-done.3
  77.8 9.2 %query_gradients.1 = (f32[32,32,256]{2,1,0:T(8,128)}, f32[32,32,256]{2,1,0:T(8,128)}, f32[2,32,32,256]{3,2,1,0:T(8,128)}) custom-call(f32[1]{0:T(128)S(6)} %copy.18.heat_ref.refs_0_, s32[1]{0:T(128)} %bitcast.refs_1_, bf16[32,2048]{1,0:T(8,128)(2,1)} %get-tuple-element.13.refs_4_.refs_6_.refs_2_, bf16[2,32,2048]{2,1,0:T(8,128)(2,1)} %copy-done.2, ...), custom_call_target="tpu_custom_call" | custom-call | tf_op jit(solution)/shard_map/query_gradients/pallas_call | solution.py:281
  87.1 8.9 %text_gradients.1 = f32[2048,256]{1,0:T(8,128)} custom-call(f32[1]{0:T(128)S(6)} %copy.18.heat_ref.refs_0_, s32[1]{0:T(128)} %bitcast.refs_1_, bf16[32,32,256]{2,1,0:T(8,128)(2,1)} %half_queries.1.refs_0_.refs_2_, bf16[32,32,256]{2,1,0:T(8,128)(2,1)} %copy-done.4, bf16[32,32,256]{2,1,0:T(8,128)(2,1)} %copy-done.5, ...), custom_call_target="tpu_custom_call" | custom-call | tf_op jit(solution)/shard_map/text_gradients/pallas_call | solution.py:249
  96.0 3.9 %all-to-all-start.4 = ((f32[16,128,256]{2,1,0:T(8,128)}), f32[16,128,256]{2,1,0:T(8,128)S(1)}, u32[]{:S(2)}, u32[]{:S(2)}) async-start(f32[16,128,256]{2,1,0:T(8,128)} %bitcast.14), calls=%async_computation.4 | async-start | bytes 4194304 | tf_op jit(solution)/shard_map/all_to_all | solution.py:371
  99.9 2.3 %fusion = f32[32,32,256]{2,1,0:T(8,128)} fusion(f32[32,32,256]{2,1,0:T(8,128)S(1)} %copy-done.7, f32[2,32,32,256]{3,2,1,0:T(8,128)} %collective-permute-done.8.core_ref), kind=kLoop, calls=%fused_computation.1 | loop fusion | flops 262144 | bytes 3145728 | tf_op jit(solution)/shard_map/add | solution.py:376
  102.2 1.1 collective-permute-start.9
  103.4 27.1 %all-to-all-done.4 = f32[16,128,256]{2,1,0:T(8,128)S(1)} async-done(((f32[16,128,256]{2,1,0:T(8,128)}), f32[16,128,256]{2,1,0:T(8,128)S(1)}, u32[]{:S(2)}, u32[]{:S(2)}) %all-to-all-start.4) | async-done | bytes 2097184 | tf_op jit(solution)/shard_map/all_to_all | solution.py:371
  130.6 0.8 reduce_sum.59
  131.3 6.0 %all-to-all-start.5 = ((f32[4,32,256]{2,1,0:T(8,128)}), f32[4,32,256]{2,1,0:T(8,128)S(1)}, u32[]{:S(2)}, u32[]{:S(2)}) async-start(f32[4,32,256]{2,1,0:T(8,128)} %bitcast.7), calls=%async_computation.5 | async-start | bytes 262144 | tf_op jit(solution)/shard_map/all_to_all | solution.py:378
  137.3 1.0 copy-done.8
  138.3 4.2 %finish_queries.1 = f32[32,32,256]{2,1,0:T(8,128)} custom-call(bf16[32,32,256]{2,1,0:T(8,128)(2,1)} %probe_ref.3, f32[32,32,256]{2,1,0:T(8,128)} %get-tuple-element.19.own_ref, f32[2,32,32,256]{3,2,1,0:T(8,128)} %collective-permute-done.8.core_ref, f32[32,32,256]{2,1,0:T(8,128)} %copy-done.8), custom_call_target="tpu_custom_call" | custom-call | tf_op jit(solution)/shard_map/finish_queries/pallas_call | solution.py:321
  142.5 3.3 %all-to-all-done.5 = f32[4,32,256]{2,1,0:T(8,128)S(1)} async-done(((f32[4,32,256]{2,1,0:T(8,128)}), f32[4,32,256]{2,1,0:T(8,128)S(1)}, u32[]{:S(2)}, u32[]{:S(2)}) %all-to-all-start.5) | async-done | bytes 131104 | tf_op jit(solution)/shard_map/all_to_all | solution.py:378
  (45 shorter events, 4.9 us)
Async XLA Ops:
  2.1 15.8 %all-to-all-start = ((bf16[4,32,256]{2,1,0:T(8,128)(2,1)}), bf16[4,32,256]{2,1,0:T(8,128)(2,1)S(1)}, u32[]{:S(2)}, u32[]{:S(2)}) async-start(bf16[4,32,256]{2,1,0:T(8,128)(2,1)} %half_texts.1), calls=%async_computation | async-start | bytes 131072 | tf_op jit(solution)/shard_map/all_to_all | solution.py:348
  12.4 18.9 %collective-permute-start = (bf16[32,32,256]{2,1,0:T(8,128)(2,1)}, bf16[32,32,256]{2,1,0:T(8,128)(2,1)S(1)}, u32[]{:S(2)}, u32[]{:S(2)}) collective-permute-start(bf16[32,32,256]{2,1,0:T(8,128)(2,1)} %half_queries.1.refs_0_.refs_2_), channel_id=1, source_target_pairs={{0,2},{2,0},{1,3},{3,1},{4,6},{6,4},{5,7},{7,5},{8,10},{10,8},{9,1... | collective-permute-start | bytes 1572872 | tf_op jit(solution)/shard_map/ppermute | solution.py:334
  17.9 13.5 %copy-start.1 = (bf16[32,32,256]{2,1,0:T(8,128)(2,1)S(1)}, bf16[32,32,256]{2,1,0:T(8,128)(2,1)}, u32[]{:S(2)}) copy-start(bf16[32,32,256]{2,1,0:T(8,128)(2,1)} %half_queries.1.refs_0_.refs_2_) | copy-start | bytes 1572868
  18.9 22.7 %all-to-all-start.1 = ((bf16[16,128,256]{2,1,0:T(8,128)(2,1)}), bf16[16,128,256]{2,1,0:T(8,128)(2,1)S(1)}, u32[]{:S(2)}, u32[]{:S(2)}) async-start(bf16[16,128,256]{2,1,0:T(8,128)(2,1)} %broadcast_in_dim.11), calls=%async_computation.1 | async-start | bytes 2097152 | tf_op jit(solution)/shard_map/all_to_all | solution.py:25
  30.3 6.6 %collective-permute-start.3 = (bf16[2,32,2048]{2,1,0:T(8,128)(2,1)}, bf16[2,32,2048]{2,1,0:T(8,128)(2,1)S(1)}, u32[]{:S(2)}, u32[]{:S(2)}) collective-permute-start(bf16[2,32,2048]{2,1,0:T(8,128)(2,1)} %get-tuple-element.14), channel_id=1, source_target_pairs={{0,2},{2,0},{1,3},{3,1},{4,6},{6,4},{5,7},{7,5},{8,10},{10,8},{9,1... | collective-permute-start | bytes 786440 | tf_op jit(solution)/shard_map/ppermute | solution.py:334
  31.4 7.3 %collective-permute-start.1 = (bf16[32,32,256]{2,1,0:T(8,128)(2,1)S(1)}, bf16[32,32,256]{2,1,0:T(8,128)(2,1)S(1)}, u32[]{:S(2)}, u32[]{:S(2)}) collective-permute-start(bf16[32,32,256]{2,1,0:T(8,128)(2,1)S(1)} %copy-done.1), channel_id=1, source_target_pairs={{0,1},{1,0},{2,3},{3,2},{4,5},{5,4},{6,7},{7,6},{8,9},{9,8},{10,11... | collective-permute-start | bytes 1572872 | tf_op jit(solution)/shard_map/ppermute | solution.py:338
  31.4 10.2 %copy-start.4 = (bf16[32,32,256]{2,1,0:T(8,128)(2,1)}, bf16[32,32,256]{2,1,0:T(8,128)(2,1)S(1)}, u32[]{:S(2)}) copy-start(bf16[32,32,256]{2,1,0:T(8,128)(2,1)S(1)} %collective-permute-done.refs_1_.refs_3_) | copy-start | bytes 1572868
  31.4 7.3 %collective-permute-start.2 = (bf16[32,32,256]{2,1,0:T(8,128)(2,1)S(1)}, bf16[32,32,256]{2,1,0:T(8,128)(2,1)}, u32[]{:S(2)}, u32[]{:S(2)}) collective-permute-start(bf16[32,32,256]{2,1,0:T(8,128)(2,1)S(1)} %collective-permute-done.refs_1_.refs_3_), channel_id=1, source_target_pairs={{0,1},{1,0},{2,3},{3,2},{4,5},{5,4},{6,7},{7,6},{8,9},{9,8},{10,11... | collective-permute-start | bytes 1572872 | tf_op jit(solution)/shard_map/ppermute | solution.py:338
  36.9 4.8 %copy-start.2 = (bf16[2,32,2048]{2,1,0:T(8,128)(2,1)}, bf16[2,32,2048]{2,1,0:T(8,128)(2,1)S(1)}, u32[]{:S(2)}) copy-start(bf16[2,32,2048]{2,1,0:T(8,128)(2,1)S(1)} %collective-permute-done.3.refs_5_.refs_7_.refs_3_) | copy-start | bytes 786436
  36.9 1.8 %collective-permute-start.5 = (bf16[2,32,2048]{2,1,0:T(8,128)(2,1)S(1)}, bf16[2,32,2048]{2,1,0:T(8,128)(2,1)S(1)}, u32[]{:S(2)}, u32[]{:S(2)}) collective-permute-start(bf16[2,32,2048]{2,1,0:T(8,128)(2,1)S(1)} %collective-permute-done.3.refs_5_.refs_7_.refs_3_), channel_id=1, source_target_pairs={{0,1},{1,0},{2,3},{3,2},{4,5},{5,4},{6,7},{7,6},{8,9},{9,8},{10,11... | collective-permute-start | bytes 786440 | tf_op jit(solution)/shard_map/ppermute | solution.py:338
  36.9 1.8 %collective-permute-start.4 = (bf16[32,2048]{1,0:T(8,128)(2,1)}, bf16[32,2048]{1,0:T(8,128)(2,1)S(1)}, u32[]{:S(2)}, u32[]{:S(2)}) collective-permute-start(bf16[32,2048]{1,0:T(8,128)(2,1)} %get-tuple-element.15), channel_id=1, source_target_pairs={{0,1},{1,0},{2,3},{3,2},{4,5},{5,4},{6,7},{7,6},{8,9},{9,8},{10,11... | collective-permute-start | bytes 393224 | tf_op jit(solution)/shard_map/ppermute | solution.py:338
  38.7 3.0 %copy-start.6 = (bf16[32,2048]{1,0:T(8,128)(2,1)}, bf16[32,2048]{1,0:T(8,128)(2,1)S(1)}, u32[]{:S(2)}) copy-start(bf16[32,2048]{1,0:T(8,128)(2,1)S(1)} %collective-permute-done.4.refs_6_.refs_8_.refs_4_) | copy-start | bytes 393220
  38.7 3.0 %copy-start.5 = (bf16[32,32,256]{2,1,0:T(8,128)(2,1)}, bf16[32,32,256]{2,1,0:T(8,128)(2,1)S(1)}, u32[]{:S(2)}) copy-start(bf16[32,32,256]{2,1,0:T(8,128)(2,1)S(1)} %collective-permute-done.1.refs_2_.refs_4_) | copy-start | bytes 1572868
  38.7 3.0 %copy-start.3 = (bf16[2,32,2048]{2,1,0:T(8,128)(2,1)}, bf16[2,32,2048]{2,1,0:T(8,128)(2,1)S(1)}, u32[]{:S(2)}) copy-start(bf16[2,32,2048]{2,1,0:T(8,128)(2,1)S(1)} %collective-permute-done.5.refs_7_.refs_9_.refs_5_) | copy-start | bytes 786436
  41.6 1.0 copy-start
  66.1 11.1 %all-to-all-start.3 = ((f32[4,1,2048]{2,1,0:T(1,128)}), f32[4,1,2048]{2,1,0:T(1,128)S(1)}, u32[]{:S(2)}, u32[]{:S(2)}) async-start(f32[4,1,2048]{2,1,0:T(1,128)} %broadcast_in_dim.27), calls=%async_computation.3 | async-start | bytes 65536 | tf_op jit(solution)/shard_map/all_to_all | solution.py:25
  70.4 1.2 collective-permute-start.6
  71.6 3.7 %collective-permute-start.7 = (f32[2,2,32]{2,1,0:T(2,128)S(1)}, f32[2,2,32]{2,1,0:T(2,128)S(1)}, u32[]{:S(2)}, u32[]{:S(2)}) collective-permute-start(f32[2,2,32]{2,1,0:T(2,128)S(1)} %rev.7), channel_id=1, source_target_pairs={{0,2},{2,0},{1,3},{3,1},{4,6},{6,4},{5,7},{7,5},{8,10},{10,8},{9,1... | collective-permute-start | bytes 1544 | tf_op jit(solution)/shard_map/ppermute | solution.py:334
  87.1 12.8 %collective-permute-start.8 = (f32[2,32,32,256]{3,2,1,0:T(8,128)}, f32[2,32,32,256]{3,2,1,0:T(8,128)}, u32[]{:S(2)}, u32[]{:S(2)}) collective-permute-start(f32[2,32,32,256]{3,2,1,0:T(8,128)} %get-tuple-element.20), channel_id=1, source_target_pairs={{0,1},{1,0},{2,3},{3,2},{4,5},{5,4},{6,7},{7,6},{8,9},{9,8},{10,11... | collective-permute-start | bytes 6291464 | tf_op jit(solution)/shard_map/ppermute | solution.py:338
  96.0 3.9 %copy-start.7 = (f32[32,32,256]{2,1,0:T(8,128)S(1)}, f32[32,32,256]{2,1,0:T(8,128)}, u32[]{:S(2)}) copy-start(f32[32,32,256]{2,1,0:T(8,128)} %get-tuple-element.21) | copy-start | bytes 3145732
  96.0 34.6 %all-to-all-start.4 = ((f32[16,128,256]{2,1,0:T(8,128)}), f32[16,128,256]{2,1,0:T(8,128)S(1)}, u32[]{:S(2)}, u32[]{:S(2)}) async-start(f32[16,128,256]{2,1,0:T(8,128)} %bitcast.14), calls=%async_computation.4 | async-start | bytes 4194304 | tf_op jit(solution)/shard_map/all_to_all | solution.py:371
  99.9 3.5 %copy-start.9 = (bf16[32,256]{1,0:T(8,128)(2,1)S(1)}, bf16[32,256]{1,0:T(8,128)(2,1)}, u32[]{:S(2)}) copy-start(bf16[32,256]{1,0:T(8,128)(2,1)} %caption_ref.1) | copy-start | bytes 49156
  102.2 35.1 %collective-permute-start.9 = (f32[32,32,256]{2,1,0:T(8,128)}, f32[32,32,256]{2,1,0:T(8,128)S(1)}, u32[]{:S(2)}, u32[]{:S(2)}) collective-permute-start(f32[32,32,256]{2,1,0:T(8,128)} %fusion), channel_id=1, source_target_pairs={{0,2},{2,0},{1,3},{3,1},{4,6},{6,4},{5,7},{7,5},{8,10},{10,8},{9,1... | collective-permute-start | bytes 3145736 | tf_op jit(solution)/shard_map/ppermute | solution.py:334
  131.3 14.5 %all-to-all-start.5 = ((f32[4,32,256]{2,1,0:T(8,128)}), f32[4,32,256]{2,1,0:T(8,128)S(1)}, u32[]{:S(2)}, u32[]{:S(2)}) async-start(f32[4,32,256]{2,1,0:T(8,128)} %bitcast.7), calls=%async_computation.5 | async-start | bytes 262144 | tf_op jit(solution)/shard_map/all_to_all | solution.py:378
  137.3 1.0 copy-start.8

commit v3 on v0

v3 whole, which is shorter than its diff:
```python
import jax
import jax.numpy as jnp
from jax import lax
from jax.experimental import pallas as pl
from jax.experimental.pallas import tpu as pltpu
from jax.sharding import Mesh
from jax.sharding import PartitionSpec as P

EPS = 1e-06
LANES = 128
HALF = jnp.float16
SENT = 16.0
SWAP = [(0, 1), (1, 0)]
SMEM = pl.BlockSpec(memory_space=pltpu.SMEM)
VMEM = pl.BlockSpec(memory_space=pltpu.VMEM)


def params(mib):
    return pltpu.CompilerParams(vmem_limit_bytes=mib * 1024 * 1024)


def normalized_rows(values):
    wide = values.astype(jnp.float32)
    scale = lax.rsqrt(jnp.sum(wide * wide, axis=-1, keepdims=True) + EPS)
    return (wide * scale, scale)


def text_kernel(caption_ref, copies_ref):
    unit, _ = normalized_rows(caption_ref[...])
    half = unit.astype(jnp.bfloat16)
    for k in range(copies_ref.shape[0]):
        copies_ref[k] = half


def half_texts(captions, copies):
    return pl.pallas_call(
        text_kernel,
        in_specs=[VMEM],
        out_specs=VMEM,
        out_shape=jax.ShapeDtypeStruct((copies, *captions.shape), jnp.bfloat16),
        compiler_params=params(16),
        name="half_texts",
    )(captions)


def query_kernel(probe_ref, half_ref, units):
    rows, count, width = probe_ref.shape
    unit, _ = normalized_rows(probe_ref[...])
    unit = unit.reshape(rows * count, width)
    here = pl.ds(pl.multiple_of(pl.program_id(0) * rows, rows), rows)
    for k in range(width // LANES):
        at = slice(k * LANES, (k + 1) * LANES)
        units[k] = unit[:, at]
        for q in range(count):
            half_ref[q, here, at] = units[k, pl.ds(q, rows, stride=count), :].astype(jnp.bfloat16)


def half_queries(probes):
    rows, count, width = probes.shape
    block = min(16, rows)
    return pl.pallas_call(
        query_kernel,
        grid=(rows // block,),
        in_specs=[pl.BlockSpec((block, count, width), lambda s: (s, 0, 0))],
        out_specs=VMEM,
        out_shape=jax.ShapeDtypeStruct((count, rows, width), jnp.bfloat16),
        scratch_shapes=[pltpu.VMEM((width // LANES, block * count, LANES), jnp.float32)],
        compiler_params=params(16),
        name="half_queries",
    )(probes)


def slot_kernel(bits_ref, slot_ref, own_ref, core_ref, chip_ref, order):
    rows, wide = slot_ref.shape
    lanes = 4 * rows
    block = 4 * lanes

    @pl.when(pl.program_id(0) == 0)
    def _():
        source = lax.broadcasted_iota(jnp.int32, (block, block), 0)
        goal = lax.broadcasted_iota(jnp.int32, (1, block), 1)
        member = (goal // lanes) ^ bits_ref[0]
        wanted = (goal % lanes) // rows * lanes + member * rows + goal % rows
        order[...] = jnp.where(source == wanted, 1.0, 0.0).astype(jnp.bfloat16)

    blocks = wide // block
    pieces = [slot_ref[:, k * block : (k + 1) * block] for k in range(blocks)]
    pieces = jnp.concatenate(pieces, axis=0).astype(jnp.float32).astype(jnp.bfloat16)
    moved = jnp.dot(pieces, order[...], preferred_element_type=jnp.float32).astype(jnp.bfloat16)
    for k in range(blocks):
        at = pl.ds(pl.multiple_of((pl.program_id(0) * blocks + k) * lanes, lanes), lanes)
        piece = moved[k * rows : (k + 1) * rows]
        own_ref[:, at] = piece[:, :lanes]
        core_ref[:, at] = piece[:, lanes : 2 * lanes]
        chip_ref[0, :, at] = piece[:, 2 * lanes : 3 * lanes]
        chip_ref[1, :, at] = piece[:, 3 * lanes :]


def slot_parts(bits, slots):
    rows, total = slots.shape
    held = total // 4
    steps = 4 if total >= 64 * rows else 1
    out = jax.ShapeDtypeStruct((rows, held), jnp.bfloat16)
    pair = jax.ShapeDtypeStruct((2, rows, held), jnp.bfloat16)
    return pl.pallas_call(
        slot_kernel,
        grid=(steps,),
        in_specs=[SMEM, pl.BlockSpec((rows, total // steps), lambda s: (0, s))],
        out_specs=[VMEM, VMEM, VMEM],
        out_shape=[out, out, pair],
        scratch_shapes=[pltpu.VMEM((16 * rows, 16 * rows), jnp.bfloat16)],
        compiler_params=params(16),
        name="slot_parts",
    )(bits, slots)


def slots_at(refs, at):
    own, core, chip, both = refs
    return jnp.concatenate([own[:, at], core[:, at], chip[0, :, at], both[1, :, at]], axis=0).astype(jnp.float32)


def score_kernel(tile, group, heat_ref, *refs):
    query_refs, slot_refs = refs[:4], refs[4:8]
    text_ref, stack_ref, e_ref, row_ref, column_ref = refs[8:]
    count, rows, _ = query_refs[0].shape
    images, held = e_ref.shape
    row_ref[...] = jnp.zeros_like(row_ref)
    for q in range(count):
        for member, ref in enumerate(query_refs):
            start = q * images + member * rows
            stack_ref[start : start + rows] = ref[q]

    @pl.loop(0, held // tile)
    def _(step):
        at = pl.ds(pl.multiple_of(step * tile, tile), tile)
        slots = slots_at(slot_refs, at)
        texts = text_ref[at, :]
        picked = jnp.zeros((images, tile), jnp.float32)
        for first in range(0, count, group):
            queries = stack_ref[first * images : (first + group) * images]
            dense = lax.dot_general(
                queries, texts, (((1,), (1,)), ((), ())), preferred_element_type=jnp.float32
            )
            for k in range(group):
                part = dense[k * images : (k + 1) * images]
                picked = jnp.where(slots == float(first + k), part, picked)
        e = jnp.exp(picked * (1.0 / heat_ref[0]))
        e_ref[:, at] = e
        total = jnp.sum(e, axis=0, keepdims=True)
        for k in range(column_ref.shape[0]):
            column_ref[k, :, at] = total
        row_ref[...] += jnp.sum(e, axis=1, keepdims=True)


def scores(copies, heat, queries, slots, texts):
    count, rows, width = queries[0].shape
    held = texts.shape[0]
    images = 4 * rows
    tile = min(512, held)

    def body(*refs):
        score_kernel(tile, 4, *refs)

    return pl.pallas_call(
        body,
        in_specs=[SMEM] + [VMEM] * 9,
        out_specs=[VMEM] * 4,
        out_shape=[
            jax.ShapeDtypeStruct((count * images, width), jnp.bfloat16),
            jax.ShapeDtypeStruct((images, held), jnp.float32),
            jax.ShapeDtypeStruct((images, 1), jnp.float32),
            jax.ShapeDtypeStruct((copies, 1, held), jnp.float32),
        ],
        compiler_params=params(24),
        name="scores",
    )(heat, *queries, *slots, texts)


def column_kernel(column_ref, copies_ref):
    total = jnp.sum(column_ref[...], axis=0, keepdims=True)
    for k in range(copies_ref.shape[0]):
        copies_ref[k] = total


def column_sums(columns, copies):
    held = columns.shape[-1]
    return pl.pallas_call(
        column_kernel,
        in_specs=[VMEM],
        out_specs=VMEM,
        out_shape=jax.ShapeDtypeStruct((copies, 1, held), jnp.float32),
        compiler_params=params(16),
        name="column_sums",
    )(columns.reshape(-1, held))


def row_totals(row_refs):
    rows = row_refs[0].shape[0] // 4
    members = []
    for member in range(4):
        parts = [ref[(member ^ k) * rows : ((member ^ k) + 1) * rows] for k, ref in enumerate(row_refs)]
        members.append((parts[0] + parts[1]) + (parts[2] + parts[3]))
    return jnp.concatenate(members, axis=0)


def score_gradient(total, heat_ref, e, row, columns, target):
    half = 0.5 * (1.0 / heat_ref[0])
    column = jnp.sum(columns, axis=0)
    return (e / row - target) * half + (e / column - target) * half


def smooth_target(total, rows, shape, start):
    image = lax.broadcasted_iota(jnp.int32, shape, 0)
    text = lax.broadcasted_iota(jnp.int32, shape, 1) + start
    return jnp.where((image == text) & (image < rows), 0.9, 0.0) + 0.1 / total


def text_grad_kernel(total, heat_ref, first_ref, stack_ref, *refs):
    slot_refs, row_refs, (e_ref, column_ref, dt_ref, mark_ref, mix) = refs[:4], refs[4:8], refs[8:]
    images = e_ref.shape[0]
    tile, depth = mix.shape
    start = pl.multiple_of(pl.program_id(0) * tile, tile)
    at = pl.ds(start, tile)
    target = smooth_target(total, images // 4, (images, tile), start - first_ref[0])
    g = score_gradient(total, heat_ref, e_ref[:, at], row_totals(row_refs), column_ref[:, :, at], target).T
    slots = slots_at(slot_refs, at).T
    for q in range(depth // images):
        mix[:, q * images : (q + 1) * images] = jnp.where(slots == float(q), g, 0.0).astype(jnp.bfloat16)
    dt_ref[...] = jnp.dot(mix[...], stack_ref[...], preferred_element_type=jnp.float32) * SENT
    mark_ref[...] = dt_ref[:8, :LANES]


def text_gradients(total, heat, first, stack, slots, rows, e, column):
    depth, width = stack.shape
    held = e.shape[1]
    tile = min(512, held)

    def body(*refs):
        text_grad_kernel(total, *refs)

    return pl.pallas_call(
        body,
        grid=(held // tile,),
        in_specs=[SMEM, SMEM] + [VMEM] * 11,
        out_specs=[pl.BlockSpec((tile, width), lambda s: (s, 0)), VMEM],
        out_shape=[
            jax.ShapeDtypeStruct((held, width), jnp.float32),
            jax.ShapeDtypeStruct((8, LANES), jnp.float32),
        ],
        scratch_shapes=[pltpu.VMEM((tile, depth), jnp.bfloat16)],
        compiler_params=params(28),
        name="text_gradients",
    )(heat, first, stack, *slots, *rows, e, column)


def query_grad_kernel(total, low, heat_ref, mark_ref, *refs):
    slot_refs, row_refs, (text_ref, e_ref, column_ref), outs, mix = refs[:4], refs[4:8], refs[8:11], refs[11:-1], refs[-1]
    count, rows, _ = outs[0].shape
    images = len(outs) * rows
    group = mix.shape[0] // images
    at = slice(low * rows, low * rows + images)
    slots = slots_at(slot_refs, slice(None))[at]
    row = row_totals(row_refs)[at]
    g = score_gradient(total, heat_ref, e_ref[at], row, column_ref[...], 0.1 / total)
    texts = text_ref[...]
    for first in range(0, count, group):
        for k in range(group):
            kept = jnp.where(slots == float(first + k), g, 0.0)
            mix[k * images : (k + 1) * images] = kept.astype(jnp.bfloat16)
        part = jnp.dot(mix[...], texts, preferred_element_type=jnp.float32)
        for k in range(group):
            for member, out in enumerate(outs):
                at = k * images + member * rows
                out[first + k] = part[at : at + rows]


def query_gradients(total, count, low, members, heat, mark, slots, row_parts, texts, e, column):
    images, held = e.shape
    rows = images // 4
    width = texts.shape[1]
    group = 8

    def body(*refs):
        query_grad_kernel(total, low, *refs)

    return pl.pallas_call(
        body,
        in_specs=[SMEM, pl.BlockSpec(memory_space=pl.ANY)] + [VMEM] * 11,
        out_specs=[VMEM] * members,
        out_shape=[jax.ShapeDtypeStruct((count, rows, width), jnp.float32)] * members,
        scratch_shapes=[pltpu.VMEM((group * members * rows, held), jnp.bfloat16)],
        compiler_params=params(28),
        name="query_gradients",
    )(heat, mark, *slots, *row_parts, texts, e, column)


def finish_kernel(total, heat_ref, first_ref, probe_ref, slot_ref, *refs):
    row_refs, (text_ref, e_ref, column_ref, core_ref, chip_ref, out_ref, mix, sums) = refs[:4], refs[4:]
    block, count, width = probe_ref.shape
    held = e_ref.shape[1]
    start = pl.multiple_of(pl.program_id(0) * block, block)
    here = pl.ds(start, block)
    rows = slot_ref.shape[0]
    row = sum(ref[pl.ds(k * rows + start, block), :] for k, ref in enumerate(row_refs))
    image = lax.broadcasted_iota(jnp.int32, (block, held), 0) + start
    text = lax.broadcasted_iota(jnp.int32, (block, held), 1) - first_ref[0]
    target = jnp.where(image == text, 0.9, 0.0) + 0.1 / total
    g = score_gradient(total, heat_ref, e_ref[here, :], row, column_ref[...], target)
    slots = slot_ref[here, :].astype(jnp.float32)
    for q in range(count):
        mix[q * block : (q + 1) * block] = jnp.where(slots == float(q), g, 0.0).astype(jnp.bfloat16)
    added = jnp.dot(mix[...], text_ref[...], preferred_element_type=jnp.float32)
    added += (core_ref[:, here, :] + chip_ref[:, here, :].astype(jnp.float32)).reshape(count * block, width)
    halves = range(width // LANES)
    for k in halves:
        sums[k] = added[:, k * LANES : (k + 1) * LANES]
    for i in range(block):
        unit, scale = normalized_rows(probe_ref[i])
        dq = jnp.concatenate([sums[k, pl.ds(i, count, stride=block), :] for k in halves], axis=1)
        out_ref[i] = (dq - unit * jnp.sum(unit * dq, axis=-1, keepdims=True)) * scale


def finish_queries(total, heat, first, probes, slots, row_parts, texts, e, column, core, chip):
    rows, count, width = probes.shape
    block = min(16, rows)
    kept = pl.BlockSpec((block, count, width), lambda s: (s, 0, 0))

    def body(*refs):
        finish_kernel(total, *refs)

    return pl.pallas_call(
        body,
        grid=(rows // block,),
        in_specs=[SMEM, SMEM, kept] + [VMEM] * 10,
        out_specs=kept,
        out_shape=jax.ShapeDtypeStruct(probes.shape, jnp.float32),
        scratch_shapes=[
            pltpu.VMEM((count * block, e.shape[1]), jnp.bfloat16),
            pltpu.VMEM((width // LANES, count * block, LANES), jnp.float32),
        ],
        compiler_params=params(24),
        name="finish_queries",
    )(heat, first, probes, slots, *row_parts, texts, e, column, core, chip)


def finish_text_kernel(caption_ref, block_ref, out_ref):
    unit, scale = normalized_rows(caption_ref[...])
    dt = jnp.sum(block_ref[...], axis=0) * (1.0 / SENT)
    out_ref[...] = (dt - unit * jnp.sum(unit * dt, axis=-1, keepdims=True)) * scale


def finish_texts(captions, blocks):
    return pl.pallas_call(
        finish_text_kernel,
        in_specs=[VMEM, VMEM],
        out_specs=VMEM,
        out_shape=jax.ShapeDtypeStruct(captions.shape, jnp.float32),
        compiler_params=params(16),
        name="finish_texts",
    )(captions, blocks)


def swap_z(values):
    return lax.ppermute(values, "zp", SWAP)


def swap_c(values):
    return lax.ppermute(values, "c", SWAP)


def shards(picture_probes, caption_vectors, chosen_slot_per_match, softmax_heat):
    rows, count, width = picture_probes.shape
    total = chosen_slot_per_match.shape[1]
    held = total // 4
    groups, outer = lax.axis_size("dp"), lax.axis_size("zo")

    texts = lax.all_to_all(half_texts(caption_vectors, outer), "zo", 0, 0, tiled=True)
    texts = jnp.broadcast_to(texts.reshape(1, outer * rows, width), (groups, outer * rows, width))
    texts = lax.all_to_all(texts, "dp", 0, 0, tiled=True).reshape(held, width)

    bits = (lax.axis_index("zp") * 2 + lax.axis_index("c")).astype(jnp.int32).reshape(1)
    q_own = half_queries(picture_probes)
    slots_own, slots_core, slots_chip = slot_parts(bits, chosen_slot_per_match)
    q_chip = swap_z(q_own)
    slots_chip = swap_z(slots_chip)
    queries = (q_own, swap_c(q_own), q_chip, swap_c(q_chip))
    slots = (slots_own, swap_c(slots_core), slots_chip, swap_c(slots_chip))

    stack, e, row, column = scores(groups, softmax_heat, queries, slots, texts)

    row_chip = swap_z(row)
    row_parts = (row, swap_c(row), row_chip, swap_c(row_chip))
    column = lax.all_to_all(column, "dp", 0, 0, tiled=True)
    column = lax.all_to_all(column_sums(column, outer), "zo", 0, 0, tiled=True)

    place = lax.axis_index("dp") * outer + lax.axis_index("zo")
    first = (place * rows).astype(jnp.int32).reshape(1)
    dt, mark = text_gradients(total, softmax_heat, first, stack, slots, row_parts, e, column)
    dt = lax.all_to_all(dt.astype(HALF).reshape(groups, outer * rows, width), "dp", 0, 0, tiled=True)
    common = (row_parts, texts, e, column)
    dq_chip, dq_both = query_gradients(total, count, 2, 2, softmax_heat, first, slots, *common)
    dq_chip = swap_z((dq_chip + swap_c(dq_both)).astype(HALF)).astype(jnp.float32)
    (dq_core,) = query_gradients(total, count, 1, 1, softmax_heat, mark, slots, *common)
    dq_core = swap_c(dq_core)
    dt = jnp.sum(dt.astype(jnp.float32), axis=0).reshape(outer, rows, width)
    dt = lax.all_to_all(dt, "zo", 0, 0, tiled=True)
    query_grads = finish_queries(
        total, softmax_heat, first, picture_probes, slots[0], *common, dq_core, dq_chip
    )
    dt, query_grads = lax.optimization_barrier((dt, query_grads))
    text_grads = finish_texts(caption_vectors, dt)
    return (query_grads, text_grads)


def solution(mesh):
    groups, replicas = mesh.devices.shape
    axes = ("dp", "zo", "zp", "c")
    split = Mesh(mesh.devices.reshape(groups, replicas // 4, 2, 2), axes)
    return jax.shard_map(
        shards,
        mesh=split,
        in_specs=(P(axes, None, None), P(axes, None), P(axes, None), P()),
        out_specs=(P(axes, None, None), P(axes, None)),
        check_vma=False,
    )
```

time: 1560 us -> 127 us (0.08)
  waiting for transfers between devices: 1380 us -> 37.7 us
  blocking collectives: 76.3 us -> 11.2 us
  matrix products: 46.6 us -> 0 us
  starting transfers between devices: 0.08 us -> 32.8 us
  Pallas kernels: 0 us -> 27.2 us
    reduce_scatter x1 -> x0, waiting for transfers between devices: 1260 us -> none  [shards(): lax.psum_scatter(dt_all, ('dp', 'replica'), scatter_dimension=0, tiled=True)]
    all_gather x1 -> x0, waiting for transfers between devices: 116 us -> none  [shards(): lax.all_gather(text_halved, ('dp', 'replica'), axis=0, tiled=True)]
    psum x1 -> x0, blocking collectives: 76.3 us -> none  [shards(): running_sums = lax.psum(jnp.sum(e_one, axis=0), ('dp', 'replica'))]
    dot_general x24 -> x0, matrix products: 46.6 us -> none  [the longest x8 17.1 us: grad_step(): jnp.einsum('iqj,jd->iqd', mix, piece, preferred_element_type=jnp.float32)]
    all_to_all x0 -> x5, waiting for transfers between devices: none -> 27.8 us  [the longest x1 12.9 us: shards(): lax.all_to_all(dt.astype(HALF).reshape(groups, outer * rows, width), 'dp'...]
    pallas_call x0 -> x10, Pallas kernels: none -> 27.2 us  [the longest x1 6.8 us: scores(): pl.pallas_call(body, in_specs=[SMEM] + [VMEM] * 9, out_specs=[VMEM] * 4,...]
    all_to_all x0 -> x5, starting transfers between devices: none -> 26.9 us  [the longest x1 7.56 us: shards(): lax.all_to_all(half_texts(caption_vectors, outer), 'zo', 0, 0, tiled=True)]
  transfers between devices with their start and end apart: 2 -> 17, of which waited for: 2 -> 9; matrix products, arithmetic and copies ran while one was open for 1% -> 6% of each run, Pallas kernels for 0% -> 12%
where the time goes in v3:
time: 127 us; the launch traced here: 126 us
  waiting for transfers between devices  37.7 us (30%)
  starting transfers between devices  32.8 us (26%)
  Pallas kernels  27.2 us (21%)
  blocking collectives  11.2 us (9%)
  local copies, waits for them, and re-layouts  8.9 us (7%)
  other arithmetic  6.56 us (5%)
  between operations  1.44 us (1%)
    all_to_all x1, waiting for transfers between devices, shards(): lax.all_to_all(dt.astype(HALF).reshape(groups, outer * rows, width), 'dp'...  12.9 us
    all_to_all x1, blocking collectives, shards(): column = lax.all_to_all(column, 'dp', 0, 0, tiled=True)  11.2 us
    ppermute x4, waiting for transfers between devices, swap_z(): return lax.ppermute(values, 'zp', SWAP)  8.06 us
    unnamed x27, local copies, waits for them, and re-layouts  7.83 us
    all_to_all x1, starting transfers between devices, shards(): lax.all_to_all(half_texts(caption_vectors, outer), 'zo', 0, 0, tiled=True)  7.56 us
    all_to_all x1, starting transfers between devices, shards(): texts = lax.all_to_all(texts, 'dp', 0, 0, tiled=True).reshape(held, width)  7.03 us
    pallas_call x1, Pallas kernels, scores(): pl.pallas_call(body, in_specs=[SMEM] + [VMEM] * 9, out_specs=[VMEM] * 4,...  6.8 us
    pallas_call x1, Pallas kernels, text_gradients(): pl.pallas_call(body, grid=(held // tile,), in_specs=[SMEM, SMEM] + [VMEM]...  6.07 us
  transfers between devices with their start and end apart: 17, of which 9 were waited for; matrix products, arithmetic and copies ran while one was open for 6% of the time, Pallas kernels for 12%

profile of v3, /device:TPU:32, one launch (start us, length us, event | category | flops | bytes accessed | tf_op | source)
XLA Modules:
  0.0 125.7 jit_solution(6879460628327124605)
XLA Ops:
  2.1 7.6 %all-to-all-start = ((bf16[4,32,256]{2,1,0:T(8,128)(2,1)}), bf16[4,32,256]{2,1,0:T(8,128)(2,1)S(1)}, u32[]{:S(2)}, u32[]{:S(2)}) async-start(bf16[4,32,256]{2,1,0:T(8,128)(2,1)} %half_texts.1), calls=%async_computation | async-start | bytes 131072 | tf_op jit(solution)/shard_map/all_to_all | solution.py:377
  9.6 1.0 copy-done.2
  10.7 1.1 half_queries.1.refs_1_
  11.8 1.1 collective-permute-start.1
  12.9 4.9 %all-to-all-done = bf16[4,32,256]{2,1,0:T(8,128)(2,1)S(1)} async-done(((bf16[4,32,256]{2,1,0:T(8,128)(2,1)}), bf16[4,32,256]{2,1,0:T(8,128)(2,1)S(1)}, u32[]{:S(2)}, u32[]{:S(2)}) %all-to-all-start) | async-done | bytes 65568 | tf_op jit(solution)/shard_map/all_to_all | solution.py:377
  17.9 1.1 broadcast_in_dim.8
  18.9 7.0 %all-to-all-start.1 = ((bf16[16,128,256]{2,1,0:T(8,128)(2,1)}), bf16[16,128,256]{2,1,0:T(8,128)(2,1)S(1)}, u32[]{:S(2)}, u32[]{:S(2)}) async-start(bf16[16,128,256]{2,1,0:T(8,128)(2,1)} %broadcast_in_dim.8), calls=%async_computation.1 | async-start | bytes 2097152 | tf_op jit(solution)/shard_map/all_to_all | solution.py:379
  26.0 1.2 slot_parts.1
  27.2 1.2 collective-permute-start.4
  28.9 4.8 %collective-permute-done.4.refs_7_.refs_5_.refs_4_ = bf16[2,32,2048]{2,1,0:T(8,128)(2,1)S(1)} collective-permute-done((bf16[2,32,2048]{2,1,0:T(8,128)(2,1)S(1)}, bf16[2,32,2048]{2,1,0:T(8,128)(2,1)S(1)}, u32[]{:S(2)}, u32[]{:S(2)}) %collective-permute-start.4) | collective-permute-done | bytes 262176 | tf_op jit(solution)/shard_map/ppermute | solution.py:364
  37.0 4.7 %all-to-all-done.1 = bf16[16,128,256]{2,1,0:T(8,128)(2,1)S(1)} async-done(((bf16[16,128,256]{2,1,0:T(8,128)(2,1)}), bf16[16,128,256]{2,1,0:T(8,128)(2,1)S(1)}, u32[]{:S(2)}, u32[]{:S(2)}) %all-to-all-start.1) | async-done | bytes 1048608 | tf_op jit(solution)/shard_map/all_to_all | solution.py:379
  41.6 1.0 copy-done.8
  43.7 6.8 %scores.1 = (bf16[4096,256]{1,0:T(8,128)(2,1)S(1)}, f32[128,2048]{1,0:T(8,128)S(1)}, f32[128,1]{1,0:T(8,128)S(1)}, f32[16,1,2048]{2,1,0:T(1,128)S(1)}) custom-call(f32[1]{0:T(128)S(6)} %copy.10.refs_0_, bf16[32,32,256]{2,1,0:T(8,128)(2,1)S(1)} %half_queries.1.refs_1_, bf16[32,32,256]{2,1,0:T(8,128)(2,1)S(1)} %copy-done.8, ...), custom_call_target="tpu_custom_call" | custom-call | tf_op jit(solution)/shard_map/scores/pallas_call | solution.py:164
  50.5 1.3 %copy-done = bf16[4096,256]{1,0:T(8,128)(2,1)} copy-done((bf16[4096,256]{1,0:T(8,128)(2,1)}, bf16[4096,256]{1,0:T(8,128)(2,1)S(1)}, u32[]{:S(2)}) %copy-start) | copy-done | bytes 2097176
  51.9 11.2 %all_to_all.30 = f32[16,1,2048]{2,1,0:T(1,128)S(1)} all-to-all(f32[16,1,2048]{2,1,0:T(1,128)S(1)} %get-tuple-element.21), channel_id=1, replica_groups=mesh['dp'=16,'zo'=4,'zp'=2,'c'=2] {'dp'}, dimensions={0} | all-to-all | bytes 262144 | tf_op jit(solution)/shard_map/all_to_all | solution.py:393
  63.7 3.3 %all-to-all-start.3 = ((f32[4,1,2048]{2,1,0:T(1,128)}), f32[4,1,2048]{2,1,0:T(1,128)S(1)}, u32[]{:S(2)}, u32[]{:S(2)}) async-start(f32[4,1,2048]{2,1,0:T(1,128)} %column_sums.1), calls=%async_computation.3 | async-start | bytes 65536 | tf_op jit(solution)/shard_map/all_to_all | solution.py:394
  67.0 1.1 collective-permute-start.7
  68.1 3.3 %collective-permute-done.7.refs_9_.refs_8_.refs_6_ = f32[128,1]{1,0:T(8,128)S(1)} collective-permute-done((f32[128,1]{1,0:T(8,128)S(1)}, f32[128,1]{1,0:T(8,128)S(1)}, u32[]{:S(2)}, u32[]{:S(2)}) %collective-permute-start.7) | collective-permute-done | bytes 544 | tf_op jit(solution)/shard_map/ppermute | solution.py:364
  71.4 1.2 collective-permute-done.8.refs_10_.refs_9_.refs_7_
  72.7 2.2 %all-to-all-done.3.refs_12_.refs_10_ = f32[4,1,2048]{2,1,0:T(1,128)S(1)} async-done(((f32[4,1,2048]{2,1,0:T(1,128)}), f32[4,1,2048]{2,1,0:T(1,128)S(1)}, u32[]{:S(2)}, u32[]{:S(2)}) %all-to-all-start.3) | async-done | bytes 32800 | tf_op jit(solution)/shard_map/all_to_all | solution.py:394
  74.8 3.4 %query_gradients.3 = (f32[32,32,256]{2,1,0:T(8,128)S(1)}, f32[32,32,256]{2,1,0:T(8,128)}) custom-call(f32[1]{0:T(128)S(6)} %copy.10.refs_0_, s32[1]{0:T(128)} %bitcast.refs_1_, bf16[32,2048]{1,0:T(8,128)(2,1)S(1)} %get-tuple-element.15.refs_5_.refs_3_.refs_2_, bf16[32,2048]{1,0:T(8,128)(2,1)S(1)} %collective-permute-done.3.refs_6_.refs_4_.refs_3_, ...), custom_call_target="tpu_custom_call" | custom-call | tf_op jit(solution)/shard_map/query_gradients/pallas_call | solution.py:286
  79.3 6.1 %text_gradients.1 = (f32[2048,256]{1,0:T(8,128)S(1)}, f32[8,128]{1,0:T(8,128)S(1)}) custom-call(f32[1]{0:T(128)S(6)} %copy.10.refs_0_, s32[1]{0:T(128)} %bitcast.refs_1_, bf16[4096,256]{1,0:T(8,128)(2,1)S(1)} %copy-done.1, bf16[32,2048]{1,0:T(8,128)(2,1)S(1)} %get-tuple-element.15.refs_5_.refs_3_.refs_2_, ...), custom_call_target="tpu_custom_call" | custom-call | tf_op jit(solution)/shard_map/text_gradients/pallas_call | solution.py:241
  85.3 1.2 convert_element_type.12
  86.5 4.3 %all-to-all-start.4 = ((f16[16,128,256]{2,1,0:T(8,128)(2,1)}), f16[16,128,256]{2,1,0:T(8,128)(2,1)}, u32[]{:S(2)}, u32[]{:S(2)}) async-start(f16[16,128,256]{2,1,0:T(8,128)(2,1)} %bitcast.14), calls=%async_computation.4 | async-start | bytes 2097152 | tf_op jit(solution)/shard_map/all_to_all | solution.py:399
  90.9 2.3 %query_gradients.2 = f32[32,32,256]{2,1,0:T(8,128)} custom-call(f32[1]{0:T(128)S(6)} %copy.10.refs_0_, f32[8,128]{1,0:T(8,128)S(1)} %get-tuple-element.23.refs_1_, bf16[32,2048]{1,0:T(8,128)(2,1)S(1)} %get-tuple-element.15.refs_5_.refs_3_.refs_2_, bf16[32,2048]{1,0:T(8,128)(2,1)S(1)} %collective-permute-done.3.refs_6_.refs_4_.refs_3_, ...), custom_call_target="tpu_custom_call" | custom-call | tf_op jit(solution)/shard_map/query_gradients/pallas_call | solution.py:286
  93.7 2.2 %add_convert_fusion = f16[32,32,256]{2,1,0:T(8,128)(2,1)} fusion(f32[32,32,256]{2,1,0:T(8,128)S(1)} %copy-done.6, f32[32,32,256]{2,1,0:T(8,128)} %collective-permute-done.10), kind=kLoop, calls=%fused_computation.1 | loop fusion | flops 524288 | bytes 2621440 | tf_op jit(solution)/shard_map/convert_element_type | solution.py:402
  96.9 12.9 %all-to-all-done.4 = f16[16,128,256]{2,1,0:T(8,128)(2,1)} async-done(((f16[16,128,256]{2,1,0:T(8,128)(2,1)}), f16[16,128,256]{2,1,0:T(8,128)(2,1)}, u32[]{:S(2)}, u32[]{:S(2)}) %all-to-all-start.4) | async-done | bytes 1048608 | tf_op jit(solution)/shard_map/all_to_all | solution.py:399
  109.8 2.0 %convert_reduce_fusion = f32[128,256]{1,0:T(8,128)} fusion(f16[16,128,256]{2,1,0:T(8,128)(2,1)} %all-to-all-done.4), kind=kLoop, calls=%fused_computation | loop fusion | flops 1015808 | bytes 1179648 | tf_op jit(solution)/shard_map/reduce_sum | solution.py:405
  111.9 4.7 %all-to-all-start.5 = ((f32[4,32,256]{2,1,0:T(8,128)}), f32[4,32,256]{2,1,0:T(8,128)S(1)}, u32[]{:S(2)}, u32[]{:S(2)}) async-start(f32[4,32,256]{2,1,0:T(8,128)} %bitcast.5), calls=%async_computation.5 | async-start | bytes 262144 | tf_op jit(solution)/shard_map/all_to_all | solution.py:406
  116.6 1.1 convert_element_type.15.refs_12_
  117.7 4.1 %finish_queries.1 = f32[32,32,256]{2,1,0:T(8,128)} custom-call(f32[1]{0:T(128)S(6)} %copy.10.refs_0_, s32[1]{0:T(128)} %bitcast.refs_1_, bf16[32,32,256]{2,1,0:T(8,128)(2,1)S(1)} %copy-done.3, bf16[32,2048]{1,0:T(8,128)(2,1)S(1)} %get-tuple-element.15.refs_5_.refs_3_.refs_2_, f32[128,1]{1,0:T(8,128)S(1)} %get-tuple-element.19.refs_7_.refs_6_.refs_4_, ...), custom_call_target="tpu_custom_call" | custom-call | tf_op jit(solution)/shard_map/finish_queries/pallas_call | solution.py:331
  121.8 3.1 %all-to-all-done.5.block_ref = f32[4,32,256]{2,1,0:T(8,128)S(1)} async-done(((f32[4,32,256]{2,1,0:T(8,128)}), f32[4,32,256]{2,1,0:T(8,128)S(1)}, u32[]{:S(2)}, u32[]{:S(2)}) %all-to-all-start.5) | async-done | bytes 131104 | tf_op jit(solution)/shard_map/all_to_all | solution.py:406
  (45 shorter events, 9.7 us)
Async XLA Ops:
  0.6 0.7 copy-start.11
  2.1 15.8 %all-to-all-start = ((bf16[4,32,256]{2,1,0:T(8,128)(2,1)}), bf16[4,32,256]{2,1,0:T(8,128)(2,1)S(1)}, u32[]{:S(2)}, u32[]{:S(2)}) async-start(bf16[4,32,256]{2,1,0:T(8,128)(2,1)} %half_texts.1), calls=%async_computation | async-start | bytes 131072 | tf_op jit(solution)/shard_map/all_to_all | solution.py:377
  9.6 1.0 copy-start.2
  10.7 15.3 %copy-start.4 = (s32[32,8192]{1,0:T(8,128)S(1)}, s32[32,8192]{1,0:T(8,128)}, u32[]{:S(2)}) copy-start(s32[32,8192]{1,0:T(8,128)} %slot_ref.1) | copy-start | bytes 3145732
  11.8 16.6 %collective-permute-start.1 = (bf16[32,32,256]{2,1,0:T(8,128)(2,1)S(1)}, bf16[32,32,256]{2,1,0:T(8,128)(2,1)}, u32[]{:S(2)}, u32[]{:S(2)}) collective-permute-start(bf16[32,32,256]{2,1,0:T(8,128)(2,1)S(1)} %half_queries.1.refs_1_), channel_id=1, source_target_pairs={{0,2},{2,0},{1,3},{3,1},{4,6},{6,4},{5,7},{7,5},{8,10},{10,8},{9,1... | collective-permute-start | bytes 1572872 | tf_op jit(solution)/shard_map/ppermute | solution.py:364
  18.9 22.7 %all-to-all-start.1 = ((bf16[16,128,256]{2,1,0:T(8,128)(2,1)}), bf16[16,128,256]{2,1,0:T(8,128)(2,1)S(1)}, u32[]{:S(2)}, u32[]{:S(2)}) async-start(bf16[16,128,256]{2,1,0:T(8,128)(2,1)} %broadcast_in_dim.8), calls=%async_computation.1 | async-start | bytes 2097152 | tf_op jit(solution)/shard_map/all_to_all | solution.py:379
  27.2 6.5 %collective-permute-start.4 = (bf16[2,32,2048]{2,1,0:T(8,128)(2,1)S(1)}, bf16[2,32,2048]{2,1,0:T(8,128)(2,1)S(1)}, u32[]{:S(2)}, u32[]{:S(2)}) collective-permute-start(bf16[2,32,2048]{2,1,0:T(8,128)(2,1)S(1)} %get-tuple-element.17), channel_id=1, source_target_pairs={{0,2},{2,0},{1,3},{3,1},{4,6},{6,4},{5,7},{7,5},{8,10},{10,8},{9,1... | collective-permute-start | bytes 786440 | tf_op jit(solution)/shard_map/ppermute | solution.py:364
  28.4 7.0 %collective-permute-start = (bf16[32,32,256]{2,1,0:T(8,128)(2,1)S(1)}, bf16[32,32,256]{2,1,0:T(8,128)(2,1)S(1)}, u32[]{:S(2)}, u32[]{:S(2)}) collective-permute-start(bf16[32,32,256]{2,1,0:T(8,128)(2,1)S(1)} %half_queries.1.refs_1_), channel_id=1, source_target_pairs={{0,1},{1,0},{2,3},{3,2},{4,5},{5,4},{6,7},{7,6},{8,9},{9,8},{10,11... | collective-permute-start | bytes 1572872 | tf_op jit(solution)/shard_map/ppermute | solution.py:368
  28.4 7.8 %collective-permute-start.2 = (bf16[32,32,256]{2,1,0:T(8,128)(2,1)}, bf16[32,32,256]{2,1,0:T(8,128)(2,1)S(1)}, u32[]{:S(2)}, u32[]{:S(2)}) collective-permute-start(bf16[32,32,256]{2,1,0:T(8,128)(2,1)} %collective-permute-done.1.refs_3_), channel_id=1, source_target_pairs={{0,1},{1,0},{2,3},{3,2},{4,5},{5,4},{6,7},{7,6},{8,9},{9,8},{10,11... | collective-permute-start | bytes 1572872 | tf_op jit(solution)/shard_map/ppermute | solution.py:368
  33.6 1.7 %collective-permute-start.5 = (bf16[2,32,2048]{2,1,0:T(8,128)(2,1)S(1)}, bf16[2,32,2048]{2,1,0:T(8,128)(2,1)S(1)}, u32[]{:S(2)}, u32[]{:S(2)}) collective-permute-start(bf16[2,32,2048]{2,1,0:T(8,128)(2,1)S(1)} %collective-permute-done.4.refs_7_.refs_5_.refs_4_), channel_id=1, source_target_pairs={{0,1},{1,0},{2,3},{3,2},{4,5},{5,4},{6,7},{7,6},{8,9},{9,8},{10,11... | collective-permute-start | bytes 786440 | tf_op jit(solution)/shard_map/ppermute | solution.py:368
  33.7 1.7 %collective-permute-start.3 = (bf16[32,2048]{1,0:T(8,128)(2,1)S(1)}, bf16[32,2048]{1,0:T(8,128)(2,1)S(1)}, u32[]{:S(2)}, u32[]{:S(2)}) collective-permute-start(bf16[32,2048]{1,0:T(8,128)(2,1)S(1)} %get-tuple-element.16), channel_id=1, source_target_pairs={{0,1},{1,0},{2,3},{3,2},{4,5},{5,4},{6,7},{7,6},{8,9},{9,8},{10,11... | collective-permute-start | bytes 393224 | tf_op jit(solution)/shard_map/ppermute | solution.py:368
  35.4 0.8 copy-start.7
  36.2 0.8 copy-start.9
  41.6 1.0 copy-start.8
  42.7 1.0 copy-start.10
  50.5 1.3 %copy-start = (bf16[4096,256]{1,0:T(8,128)(2,1)}, bf16[4096,256]{1,0:T(8,128)(2,1)S(1)}, u32[]{:S(2)}) copy-start(bf16[4096,256]{1,0:T(8,128)(2,1)S(1)} %get-tuple-element.18.refs_2_) | copy-start | bytes 6291460
  63.7 11.1 %all-to-all-start.3 = ((f32[4,1,2048]{2,1,0:T(1,128)}), f32[4,1,2048]{2,1,0:T(1,128)S(1)}, u32[]{:S(2)}, u32[]{:S(2)}) async-start(f32[4,1,2048]{2,1,0:T(1,128)} %column_sums.1), calls=%async_computation.3 | async-start | bytes 65536 | tf_op jit(solution)/shard_map/all_to_all | solution.py:394
  67.0 4.4 %collective-permute-start.7 = (f32[128,1]{1,0:T(8,128)S(1)}, f32[128,1]{1,0:T(8,128)S(1)}, u32[]{:S(2)}, u32[]{:S(2)}) collective-permute-start(f32[128,1]{1,0:T(8,128)S(1)} %get-tuple-element.19.refs_7_.refs_6_.refs_4_), channel_id=1, source_target_pairs={{0,2},{2,0},{1,3},{3,1},{4,6},{6,4},{5,7},{7,5},{8,10},{10,8},{9,1... | collective-permute-start | bytes 1544 | tf_op jit(solution)/shard_map/ppermute | solution.py:364
  68.1 3.3 %collective-permute-start.6 = (f32[128,1]{1,0:T(8,128)S(1)}, f32[128,1]{1,0:T(8,128)S(1)}, u32[]{:S(2)}, u32[]{:S(2)}) collective-permute-start(f32[128,1]{1,0:T(8,128)S(1)} %get-tuple-element.19.refs_7_.refs_6_.refs_4_), channel_id=1, source_target_pairs={{0,1},{1,0},{2,3},{3,2},{4,5},{5,4},{6,7},{7,6},{8,9},{9,8},{10,11... | collective-permute-start | bytes 1544 | tf_op jit(solution)/shard_map/ppermute | solution.py:368
  71.4 1.3 collective-permute-start.8
  74.8 4.4 %copy-start.1 = (bf16[4096,256]{1,0:T(8,128)(2,1)S(1)}, bf16[4096,256]{1,0:T(8,128)(2,1)}, u32[]{:S(2)}) copy-start(bf16[4096,256]{1,0:T(8,128)(2,1)} %copy-done) | copy-start | bytes 6291460
  78.3 1.0 copy-start.5
  79.3 14.4 %collective-permute-start.10 = (f32[32,32,256]{2,1,0:T(8,128)}, f32[32,32,256]{2,1,0:T(8,128)}, u32[]{:S(2)}, u32[]{:S(2)}) collective-permute-start(f32[32,32,256]{2,1,0:T(8,128)} %get-tuple-element.25), channel_id=1, source_target_pairs={{0,1},{1,0},{2,3},{3,2},{4,5},{5,4},{6,7},{7,6},{8,9},{9,8},{10,11... | collective-permute-start | bytes 3145736 | tf_op jit(solution)/shard_map/ppermute | solution.py:368
  86.5 23.3 %all-to-all-start.4 = ((f16[16,128,256]{2,1,0:T(8,128)(2,1)}), f16[16,128,256]{2,1,0:T(8,128)(2,1)}, u32[]{:S(2)}, u32[]{:S(2)}) async-start(f16[16,128,256]{2,1,0:T(8,128)(2,1)} %bitcast.14), calls=%async_computation.4 | async-start | bytes 2097152 | tf_op jit(solution)/shard_map/all_to_all | solution.py:399
  90.9 2.8 %copy-start.6 = (f32[32,32,256]{2,1,0:T(8,128)S(1)}, f32[32,32,256]{2,1,0:T(8,128)}, u32[]{:S(2)}) copy-start(f32[32,32,256]{2,1,0:T(8,128)} %copy-done.5) | copy-start | bytes 3145732
  93.1 24.6 %collective-permute-start.9 = (f32[32,32,256]{2,1,0:T(8,128)}, f32[32,32,256]{2,1,0:T(8,128)}, u32[]{:S(2)}, u32[]{:S(2)}) collective-permute-start(f32[32,32,256]{2,1,0:T(8,128)} %query_gradients.2), channel_id=1, source_target_pairs={{0,1},{1,0},{2,3},{3,2},{4,5},{5,4},{6,7},{7,6},{8,9},{9,8},{10,11... | collective-permute-start | bytes 3145736 | tf_op jit(solution)/shard_map/ppermute | solution.py:368
  95.9 21.8 %copy-start.3 = (bf16[32,32,256]{2,1,0:T(8,128)(2,1)S(1)}, bf16[32,32,256]{2,1,0:T(8,128)(2,1)}, u32[]{:S(2)}) copy-start(bf16[32,32,256]{2,1,0:T(8,128)(2,1)} %refs_2_.1) | copy-start | bytes 1572868
  95.9 20.7 %collective-permute-start.11 = (f16[32,32,256]{2,1,0:T(8,128)(2,1)}, f16[32,32,256]{2,1,0:T(8,128)(2,1)}, u32[]{:S(2)}, u32[]{:S(2)}) collective-permute-start(f16[32,32,256]{2,1,0:T(8,128)(2,1)} %add_convert_fusion), channel_id=1, source_target_pairs={{0,2},{2,0},{1,3},{3,1},{4,6},{6,4},{5,7},{7,5},{8,10},{10,8},{9,1... | collective-permute-start | bytes 1572872 | tf_op jit(solution)/shard_map/ppermute | solution.py:364
  111.9 13.1 %all-to-all-start.5 = ((f32[4,32,256]{2,1,0:T(8,128)}), f32[4,32,256]{2,1,0:T(8,128)S(1)}, u32[]{:S(2)}, u32[]{:S(2)}) async-start(f32[4,32,256]{2,1,0:T(8,128)} %bitcast.5), calls=%async_computation.5 | async-start | bytes 262144 | tf_op jit(solution)/shard_map/all_to_all | solution.py:406
  117.7 7.3 %copy-start.12 = (bf16[32,256]{1,0:T(8,128)(2,1)S(1)}, bf16[32,256]{1,0:T(8,128)(2,1)}, u32[]{:S(2)}) copy-start(bf16[32,256]{1,0:T(8,128)(2,1)} %caption_ref.3) | copy-start | bytes 49156

commit v4 on v3

--- a/solution.py
+++ b/solution.py
@@ -209,20 +209,16 @@
     return (e / row - target) * half + (e / column - target) * half
 
 
-def smooth_target(total, rows, shape, start):
-    image = lax.broadcasted_iota(jnp.int32, shape, 0)
-    text = lax.broadcasted_iota(jnp.int32, shape, 1) + start
-    return jnp.where((image == text) & (image < rows), 0.9, 0.0) + 0.1 / total
-
-
 def text_grad_kernel(total, heat_ref, first_ref, stack_ref, *refs):
     slot_refs, row_refs, (e_ref, column_ref, dt_ref, mark_ref, mix) = refs[:4], refs[4:8], refs[8:]
     images = e_ref.shape[0]
     tile, depth = mix.shape
     start = pl.multiple_of(pl.program_id(0) * tile, tile)
     at = pl.ds(start, tile)
-    target = smooth_target(total, images // 4, (images, tile), start - first_ref[0])
-    g = score_gradient(total, heat_ref, e_ref[:, at], row_totals(row_refs), column_ref[:, :, at], target).T
+    image = lax.broadcasted_iota(jnp.int32, (images, tile), 0)
+    text = lax.broadcasted_iota(jnp.int32, (images, tile), 1) + (start - first_ref[0])
+    g = score_gradient(total, heat_ref, e_ref[:, at], row_totals(row_refs), column_ref[:, :, at], 0.1 / total)
+    g = jnp.where((image == text) & (image < images // 4), 0.0, g).T
     slots = slots_at(slot_refs, at).T
     for q in range(depth // images):
         mix[:, q * images : (q + 1) * images] = jnp.where(slots == float(q), g, 0.0).astype(jnp.bfloat16)
@@ -253,15 +249,14 @@
     )(heat, first, stack, *slots, *rows, e, column)
 
 
-def query_grad_kernel(total, low, heat_ref, mark_ref, *refs):
-    slot_refs, row_refs, (text_ref, e_ref, column_ref), outs, mix = refs[:4], refs[4:8], refs[8:11], refs[11:-1], refs[-1]
+def query_grad_kernel(total, heat_ref, mark_ref, *refs):
+    slot_refs, row_refs, (text_ref, e_ref, column_ref), outs, mix = refs[:4], refs[4:8], refs[8:11], refs[11:14], refs[14]
     count, rows, _ = outs[0].shape
-    images = len(outs) * rows
+    images = 3 * rows
     group = mix.shape[0] // images
-    at = slice(low * rows, low * rows + images)
-    slots = slots_at(slot_refs, slice(None))[at]
-    row = row_totals(row_refs)[at]
-    g = score_gradient(total, heat_ref, e_ref[at], row, column_ref[...], 0.1 / total)
+    slots = slots_at(slot_refs, slice(None))[rows:]
+    row = row_totals(row_refs)[rows:]
+    g = score_gradient(total, heat_ref, e_ref[rows:], row, column_ref[...], 0.1 / total)
     texts = text_ref[...]
     for first in range(0, count, group):
         for k in range(group):
@@ -274,28 +269,28 @@
                 out[first + k] = part[at : at + rows]
 
 
-def query_gradients(total, count, low, members, heat, mark, slots, row_parts, texts, e, column):
+def query_gradients(total, count, heat, mark, slots, row_parts, texts, e, column):
     images, held = e.shape
     rows = images // 4
     width = texts.shape[1]
     group = 8
 
     def body(*refs):
-        query_grad_kernel(total, low, *refs)
+        query_grad_kernel(total, *refs)
 
     return pl.pallas_call(
         body,
         in_specs=[SMEM, pl.BlockSpec(memory_space=pl.ANY)] + [VMEM] * 11,
-        out_specs=[VMEM] * members,
-        out_shape=[jax.ShapeDtypeStruct((count, rows, width), jnp.float32)] * members,
-        scratch_shapes=[pltpu.VMEM((group * members * rows, held), jnp.bfloat16)],
+        out_specs=[VMEM] * 3,
+        out_shape=[jax.ShapeDtypeStruct((count, rows, width), jnp.float32)] * 3,
+        scratch_shapes=[pltpu.VMEM((group * 3 * rows, held), jnp.bfloat16)],
         compiler_params=params(28),
         name="query_gradients",
     )(heat, mark, *slots, *row_parts, texts, e, column)
 
 
 def finish_kernel(total, heat_ref, first_ref, probe_ref, slot_ref, *refs):
-    row_refs, (text_ref, e_ref, column_ref, core_ref, chip_ref, out_ref, mix, sums) = refs[:4], refs[4:]
+    row_refs, (text_ref, e_ref, column_ref, core_ref, chip_ref, out_ref, pair_ref, mix, sums, pair_mix, half) = refs[:4], refs[4:]
     block, count, width = probe_ref.shape
     held = e_ref.shape[1]
     start = pl.multiple_of(pl.program_id(0) * block, block)
@@ -304,9 +299,15 @@
     row = sum(ref[pl.ds(k * rows + start, block), :] for k, ref in enumerate(row_refs))
     image = lax.broadcasted_iota(jnp.int32, (block, held), 0) + start
     text = lax.broadcasted_iota(jnp.int32, (block, held), 1) - first_ref[0]
-    target = jnp.where(image == text, 0.9, 0.0) + 0.1 / total
+    matched = image == text
+    target = jnp.where(matched, 0.9, 0.0) + 0.1 / total
     g = score_gradient(total, heat_ref, e_ref[here, :], row, column_ref[...], target)
     slots = slot_ref[here, :].astype(jnp.float32)
+    pair_g = jnp.sum(jnp.where(matched, g, 0.0), axis=1, keepdims=True)
+    pair_slot = jnp.sum(jnp.where(matched, slots, 0.0), axis=1, keepdims=True)
+    query = lax.broadcasted_iota(jnp.int32, (count, 1), 0).astype(jnp.float32)
+    pair_mix[...] = jnp.broadcast_to(pair_g, pair_mix.shape).astype(jnp.bfloat16)
+    pair_g = pair_mix[...].astype(jnp.float32)[:, :1]
     for q in range(count):
         mix[q * block : (q + 1) * block] = jnp.where(slots == float(q), g, 0.0).astype(jnp.bfloat16)
     added = jnp.dot(mix[...], text_ref[...], preferred_element_type=jnp.float32)
@@ -316,6 +317,9 @@
         sums[k] = added[:, k * LANES : (k + 1) * LANES]
     for i in range(block):
         unit, scale = normalized_rows(probe_ref[i])
+        half[i] = unit.astype(jnp.bfloat16)
+        pair = jnp.where(query == pair_slot[i : i + 1], pair_g[i : i + 1], 0.0)
+        pair_ref[i : i + 1, :] = jnp.sum(pair * half[i].astype(jnp.float32), axis=0, keepdims=True)
         dq = jnp.concatenate([sums[k, pl.ds(i, count, stride=block), :] for k in halves], axis=1)
         out_ref[i] = (dq - unit * jnp.sum(unit * dq, axis=-1, keepdims=True)) * scale
 
@@ -332,32 +336,37 @@
         body,
         grid=(rows // block,),
         in_specs=[SMEM, SMEM, kept] + [VMEM] * 10,
-        out_specs=kept,
-        out_shape=jax.ShapeDtypeStruct(probes.shape, jnp.float32),
+        out_specs=[kept, pl.BlockSpec((block, width), lambda s: (s, 0))],
+        out_shape=[
+            jax.ShapeDtypeStruct(probes.shape, jnp.float32),
+            jax.ShapeDtypeStruct((rows, width), jnp.float32),
+        ],
         scratch_shapes=[
             pltpu.VMEM((count * block, e.shape[1]), jnp.bfloat16),
             pltpu.VMEM((width // LANES, count * block, LANES), jnp.float32),
+            pltpu.VMEM((block, LANES), jnp.bfloat16),
+            pltpu.VMEM((block, count, width), jnp.bfloat16),
         ],
         compiler_params=params(24),
         name="finish_queries",
     )(heat, first, probes, slots, *row_parts, texts, e, column, core, chip)
 
 
-def finish_text_kernel(caption_ref, block_ref, out_ref):
+def finish_text_kernel(caption_ref, block_ref, pair_ref, out_ref):
     unit, scale = normalized_rows(caption_ref[...])
-    dt = jnp.sum(block_ref[...], axis=0) * (1.0 / SENT)
+    dt = jnp.sum(block_ref[...], axis=0) * (1.0 / SENT) + pair_ref[...]
     out_ref[...] = (dt - unit * jnp.sum(unit * dt, axis=-1, keepdims=True)) * scale
 
 
-def finish_texts(captions, blocks):
+def finish_texts(captions, blocks, pairs):
     return pl.pallas_call(
         finish_text_kernel,
-        in_specs=[VMEM, VMEM],
+        in_specs=[VMEM] * 3,
         out_specs=VMEM,
         out_shape=jax.ShapeDtypeStruct(captions.shape, jnp.float32),
         compiler_params=params(16),
         name="finish_texts",
-    )(captions, blocks)
+    )(captions, blocks, pairs)
 
 
 def swap_z(values):
@@ -398,17 +407,16 @@
     dt, mark = text_gradients(total, softmax_heat, first, stack, slots, row_parts, e, column)
     dt = lax.all_to_all(dt.astype(HALF).reshape(groups, outer * rows, width), "dp", 0, 0, tiled=True)
     common = (row_parts, texts, e, column)
-    dq_chip, dq_both = query_gradients(total, count, 2, 2, softmax_heat, first, slots, *common)
-    dq_chip = swap_z((dq_chip + swap_c(dq_both)).astype(HALF)).astype(jnp.float32)
-    (dq_core,) = query_gradients(total, count, 1, 1, softmax_heat, mark, slots, *common)
+    dq_core, dq_chip, dq_both = query_gradients(total, count, softmax_heat, mark, slots, *common)
+    dq_chip = dq_chip + swap_c(dq_both.astype(HALF)).astype(jnp.float32)
+    dq_chip = swap_z(dq_chip.astype(HALF)).astype(jnp.float32)
     dq_core = swap_c(dq_core)
     dt = jnp.sum(dt.astype(jnp.float32), axis=0).reshape(outer, rows, width)
     dt = lax.all_to_all(dt, "zo", 0, 0, tiled=True)
-    query_grads = finish_queries(
+    query_grads, pairs = finish_queries(
         total, softmax_heat, first, picture_probes, slots[0], *common, dq_core, dq_chip
     )
-    dt, query_grads = lax.optimization_barrier((dt, query_grads))
-    text_grads = finish_texts(caption_vectors, dt)
+    text_grads = finish_texts(caption_vectors, dt, pairs)
     return (query_grads, text_grads)
 
 

time: 127 us -> 123 us (0.969)
  waiting for transfers between devices: 37.7 us -> 32.9 us
  starting transfers between devices: 32.8 us -> 36.1 us
    all_to_all x1, waiting for transfers between devices: 12.9 us -> 6.86 us  [shards(): lax.all_to_all(dt.astype(HALF).reshape(groups, outer * rows, width), 'dp'...]
    all_to_all x1, starting transfers between devices: 4.68 us -> 7.72 us  [shards(): dt = lax.all_to_all(dt, 'zo', 0, 0, tiled=True)]
    ppermute x8, waiting for transfers between devices: 1.82 us -> 3.22 us  [swap_c(): return lax.ppermute(values, 'c', SWAP)]
    pallas_call x2 -> x1, Pallas kernels: 5.68 us -> 4.41 us  [query_gradients(): pl.pallas_call(body, in_specs=[SMEM, pl.BlockSpec(memory_space=pl.ANY)] +...]
    convert_element_type x2 -> x3, other arithmetic: 3.36 us -> 2.19 us  [the longest x2 2.09 us: shards(): dq_chip = swap_z(dq_chip.astype(HALF)).astype(jnp.float32)]
    unnamed x27 -> x23, local copies, waits for them, and re-layouts: 7.83 us -> 8.42 us
  transfers between devices with their start and end apart: 17 -> 17, of which waited for: 9 -> 10; matrix products, arithmetic and copies ran while one was open for 6% -> 4% of each run, Pallas kernels for 12% -> 9%
where the time goes in v4:
time: 123 us; the launch traced here: 122 us
  starting transfers between devices  36.1 us (29%)
  waiting for transfers between devices  32.9 us (27%)
  Pallas kernels  26 us (21%)
  blocking collectives  11.2 us (9%)
  local copies, waits for them, and re-layouts  9.49 us (8%)
  other arithmetic  5.37 us (4%)
  between operations  1.44 us (1%)
    all_to_all x1, blocking collectives, shards(): column = lax.all_to_all(column, 'dp', 0, 0, tiled=True)  11.2 us
    unnamed x23, local copies, waits for them, and re-layouts  8.42 us
    ppermute x4, waiting for transfers between devices, swap_z(): return lax.ppermute(values, 'zp', SWAP)  8.06 us
    all_to_all x1, starting transfers between devices, shards(): dt = lax.all_to_all(dt, 'zo', 0, 0, tiled=True)  7.72 us
    all_to_all x1, starting transfers between devices, shards(): lax.all_to_all(half_texts(caption_vectors, outer), 'zo', 0, 0, tiled=True)  7.56 us
    all_to_all x1, starting transfers between devices, shards(): texts = lax.all_to_all(texts, 'dp', 0, 0, tiled=True).reshape(held, width)  7.03 us
    all_to_all x1, waiting for transfers between devices, shards(): lax.all_to_all(dt.astype(HALF).reshape(groups, outer * rows, width), 'dp'...  6.86 us
    pallas_call x1, Pallas kernels, scores(): pl.pallas_call(body, in_specs=[SMEM] + [VMEM] * 9, out_specs=[VMEM] * 4,...  6.8 us
  transfers between devices with their start and end apart: 17, of which 10 were waited for; matrix products, arithmetic and copies ran while one was open for 4% of the time, Pallas kernels for 9%

profile of v4, /device:TPU:32, one launch (start us, length us, event | category | flops | bytes accessed | tf_op | source)
XLA Modules:
  0.0 122.5 jit_solution(2571414851405637799)
XLA Ops:
  2.1 7.6 %all-to-all-start = ((bf16[4,32,256]{2,1,0:T(8,128)(2,1)}), bf16[4,32,256]{2,1,0:T(8,128)(2,1)S(1)}, u32[]{:S(2)}, u32[]{:S(2)}) async-start(bf16[4,32,256]{2,1,0:T(8,128)(2,1)} %half_texts.1), calls=%async_computation | async-start | bytes 131072 | tf_op jit(solution)/shard_map/all_to_all | solution.py:386
  9.6 1.0 copy-done.2
  10.7 1.1 half_queries.1.refs_1_
  11.8 1.1 collective-permute-start.1
  12.9 4.9 %all-to-all-done = bf16[4,32,256]{2,1,0:T(8,128)(2,1)S(1)} async-done(((bf16[4,32,256]{2,1,0:T(8,128)(2,1)}), bf16[4,32,256]{2,1,0:T(8,128)(2,1)S(1)}, u32[]{:S(2)}, u32[]{:S(2)}) %all-to-all-start) | async-done | bytes 65568 | tf_op jit(solution)/shard_map/all_to_all | solution.py:386
  17.9 1.1 broadcast_in_dim.8
  18.9 7.0 %all-to-all-start.1 = ((bf16[16,128,256]{2,1,0:T(8,128)(2,1)}), bf16[16,128,256]{2,1,0:T(8,128)(2,1)S(1)}, u32[]{:S(2)}, u32[]{:S(2)}) async-start(bf16[16,128,256]{2,1,0:T(8,128)(2,1)} %broadcast_in_dim.8), calls=%async_computation.1 | async-start | bytes 2097152 | tf_op jit(solution)/shard_map/all_to_all | solution.py:388
  26.0 1.2 slot_parts.1
  27.2 1.2 collective-permute-start.4
  28.9 4.8 %collective-permute-done.4.refs_7_.refs_5_.refs_4_ = bf16[2,32,2048]{2,1,0:T(8,128)(2,1)S(1)} collective-permute-done((bf16[2,32,2048]{2,1,0:T(8,128)(2,1)S(1)}, bf16[2,32,2048]{2,1,0:T(8,128)(2,1)S(1)}, u32[]{:S(2)}, u32[]{:S(2)}) %collective-permute-start.4) | collective-permute-done | bytes 262176 | tf_op jit(solution)/shard_map/ppermute | solution.py:373
  37.0 4.7 %all-to-all-done.1 = bf16[16,128,256]{2,1,0:T(8,128)(2,1)S(1)} async-done(((bf16[16,128,256]{2,1,0:T(8,128)(2,1)}), bf16[16,128,256]{2,1,0:T(8,128)(2,1)S(1)}, u32[]{:S(2)}, u32[]{:S(2)}) %all-to-all-start.1) | async-done | bytes 1048608 | tf_op jit(solution)/shard_map/all_to_all | solution.py:388
  41.6 1.0 copy-done.6
  43.7 6.8 %scores.1 = (bf16[4096,256]{1,0:T(8,128)(2,1)S(1)}, f32[128,2048]{1,0:T(8,128)S(1)}, f32[128,1]{1,0:T(8,128)S(1)}, f32[16,1,2048]{2,1,0:T(1,128)S(1)}) custom-call(f32[1]{0:T(128)S(6)} %copy.10.refs_0_, bf16[32,32,256]{2,1,0:T(8,128)(2,1)S(1)} %half_queries.1.refs_1_, bf16[32,32,256]{2,1,0:T(8,128)(2,1)S(1)} %copy-done.6, ...), custom_call_target="tpu_custom_call" | custom-call | tf_op jit(solution)/shard_map/scores/pallas_call | solution.py:164
  50.5 1.3 %copy-done = bf16[4096,256]{1,0:T(8,128)(2,1)} copy-done((bf16[4096,256]{1,0:T(8,128)(2,1)}, bf16[4096,256]{1,0:T(8,128)(2,1)S(1)}, u32[]{:S(2)}) %copy-start) | copy-done | bytes 2097176
  51.9 11.2 %all_to_all.30 = f32[16,1,2048]{2,1,0:T(1,128)S(1)} all-to-all(f32[16,1,2048]{2,1,0:T(1,128)S(1)} %get-tuple-element.21), channel_id=1, replica_groups=mesh['dp'=16,'zo'=4,'zp'=2,'c'=2] {'dp'}, dimensions={0} | all-to-all | bytes 262144 | tf_op jit(solution)/shard_map/all_to_all | solution.py:402
  63.8 3.3 %all-to-all-start.3 = ((f32[4,1,2048]{2,1,0:T(1,128)}), f32[4,1,2048]{2,1,0:T(1,128)S(1)}, u32[]{:S(2)}, u32[]{:S(2)}) async-start(f32[4,1,2048]{2,1,0:T(1,128)} %column_sums.1), calls=%async_computation.3 | async-start | bytes 65536 | tf_op jit(solution)/shard_map/all_to_all | solution.py:403
  67.0 1.1 collective-permute-start.7
  68.1 3.3 %collective-permute-done.7.refs_9_.refs_8_.refs_6_ = f32[128,1]{1,0:T(8,128)S(1)} collective-permute-done((f32[128,1]{1,0:T(8,128)S(1)}, f32[128,1]{1,0:T(8,128)S(1)}, u32[]{:S(2)}, u32[]{:S(2)}) %collective-permute-start.7) | collective-permute-done | bytes 544 | tf_op jit(solution)/shard_map/ppermute | solution.py:373
  71.4 1.2 %collective-permute-done.8.refs_10_.refs_9_.refs_7_ = f32[128,1]{1,0:T(8,128)S(1)} collective-permute-done((f32[128,1]{1,0:T(8,128)S(1)}, f32[128,1]{1,0:T(8,128)S(1)}, u32[]{:S(2)}, u32[]{:S(2)}) %collective-permute-start.8) | collective-permute-done | bytes 544 | tf_op jit(solution)/shard_map/ppermute | solution.py:377
  72.7 2.2 %all-to-all-done.3.refs_12_.refs_10_ = f32[4,1,2048]{2,1,0:T(1,128)S(1)} async-done(((f32[4,1,2048]{2,1,0:T(1,128)}), f32[4,1,2048]{2,1,0:T(1,128)S(1)}, u32[]{:S(2)}, u32[]{:S(2)}) %all-to-all-start.3) | async-done | bytes 32800 | tf_op jit(solution)/shard_map/all_to_all | solution.py:403
  74.9 1.6 %copy-done.1 = bf16[4096,256]{1,0:T(8,128)(2,1)S(1)} copy-done((bf16[4096,256]{1,0:T(8,128)(2,1)S(1)}, bf16[4096,256]{1,0:T(8,128)(2,1)}, u32[]{:S(2)}) %copy-start.1) | copy-done | bytes 2097176
  76.4 6.1 %text_gradients.1 = (f32[2048,256]{1,0:T(8,128)S(1)}, f32[8,128]{1,0:T(8,128)S(1)}) custom-call(f32[1]{0:T(128)S(6)} %copy.10.refs_0_, s32[1]{0:T(128)} %bitcast.refs_1_, bf16[4096,256]{1,0:T(8,128)(2,1)S(1)} %copy-done.1, bf16[32,2048]{1,0:T(8,128)(2,1)S(1)} %get-tuple-element.16.refs_5_.refs_3_.refs_2_, ...), custom_call_target="tpu_custom_call" | custom-call | tf_op jit(solution)/shard_map/text_gradients/pallas_call | solution.py:237
  82.5 1.2 convert_element_type.22
  83.7 4.5 %all-to-all-start.4 = ((f16[16,128,256]{2,1,0:T(8,128)(2,1)}), f16[16,128,256]{2,1,0:T(8,128)(2,1)}, u32[]{:S(2)}, u32[]{:S(2)}) async-start(f16[16,128,256]{2,1,0:T(8,128)(2,1)} %bitcast.13), calls=%async_computation.4 | async-start | bytes 2097152 | tf_op jit(solution)/shard_map/all_to_all | solution.py:408
  88.2 4.4 %query_gradients.1 = (f32[32,32,256]{2,1,0:T(8,128)}, f32[32,32,256]{2,1,0:T(8,128)S(1)}, f32[32,32,256]{2,1,0:T(8,128)S(1)}) custom-call(f32[1]{0:T(128)S(6)} %copy.10.refs_0_, f32[8,128]{1,0:T(8,128)S(1)} %get-tuple-element.23.refs_1_, bf16[32,2048]{1,0:T(8,128)(2,1)S(1)} %get-tuple-element.16.refs_5_.refs_3_.refs_2_, ...), custom_call_target="tpu_custom_call" | custom-call | tf_op jit(solution)/shard_map/query_gradients/pallas_call | solution.py:281
  93.3 1.4 %collective-permute-done.10 = f16[32,32,256]{2,1,0:T(8,128)(2,1)S(1)} collective-permute-done((f16[32,32,256]{2,1,0:T(8,128)(2,1)S(1)}, f16[32,32,256]{2,1,0:T(8,128)(2,1)S(1)}, u32[]{:S(2)}, u32[]{:S(2)}) %collective-permute-start.10) | collective-permute-done | bytes 524320 | tf_op jit(solution)/shard_map/ppermute | solution.py:377
  96.7 6.9 %all-to-all-done.4 = f16[16,128,256]{2,1,0:T(8,128)(2,1)} async-done(((f16[16,128,256]{2,1,0:T(8,128)(2,1)}), f16[16,128,256]{2,1,0:T(8,128)(2,1)}, u32[]{:S(2)}, u32[]{:S(2)}) %all-to-all-start.4) | async-done | bytes 1048608 | tf_op jit(solution)/shard_map/all_to_all | solution.py:408
  103.6 2.0 %convert_reduce_fusion = f32[128,256]{1,0:T(8,128)} fusion(f16[16,128,256]{2,1,0:T(8,128)(2,1)} %all-to-all-done.4), kind=kLoop, calls=%fused_computation | loop fusion | flops 1015808 | bytes 1179648 | tf_op jit(solution)/shard_map/reduce_sum | solution.py:414
  105.6 7.7 %all-to-all-start.5 = ((f32[4,32,256]{2,1,0:T(8,128)}), f32[4,32,256]{2,1,0:T(8,128)S(1)}, u32[]{:S(2)}, u32[]{:S(2)}) async-start(f32[4,32,256]{2,1,0:T(8,128)} %bitcast.5), calls=%async_computation.5 | async-start | bytes 262144 | tf_op jit(solution)/shard_map/all_to_all | solution.py:415
  113.3 1.1 convert_element_type.21.refs_12_
  114.5 4.3 %finish_queries.1 = (f32[32,32,256]{2,1,0:T(8,128)}, f32[32,256]{1,0:T(8,128)S(1)}) custom-call(f32[1]{0:T(128)S(6)} %copy.10.refs_0_, s32[1]{0:T(128)} %bitcast.refs_1_, bf16[32,32,256]{2,1,0:T(8,128)(2,1)S(1)} %copy-done.3, bf16[32,2048]{1,0:T(8,128)(2,1)S(1)} %get-tuple-element.16.refs_5_.refs_3_.refs_2_, ...), custom_call_target="tpu_custom_call" | custom-call | tf_op jit(solution)/shard_map/finish_queries/pallas_call | solution.py:335
  118.7 3.0 %all-to-all-done.5.block_ref = f32[4,32,256]{2,1,0:T(8,128)S(1)} async-done(((f32[4,32,256]{2,1,0:T(8,128)}), f32[4,32,256]{2,1,0:T(8,128)S(1)}, u32[]{:S(2)}, u32[]{:S(2)}) %all-to-all-start.5) | async-done | bytes 131104 | tf_op jit(solution)/shard_map/all_to_all | solution.py:415
  (41 shorter events, 9.8 us)
Async XLA Ops:
  0.6 0.7 copy-start.9
  2.1 15.8 %all-to-all-start = ((bf16[4,32,256]{2,1,0:T(8,128)(2,1)}), bf16[4,32,256]{2,1,0:T(8,128)(2,1)S(1)}, u32[]{:S(2)}, u32[]{:S(2)}) async-start(bf16[4,32,256]{2,1,0:T(8,128)(2,1)} %half_texts.1), calls=%async_computation | async-start | bytes 131072 | tf_op jit(solution)/shard_map/all_to_all | solution.py:386
  9.6 1.0 copy-start.2
  10.7 15.3 %copy-start.4 = (s32[32,8192]{1,0:T(8,128)S(1)}, s32[32,8192]{1,0:T(8,128)}, u32[]{:S(2)}) copy-start(s32[32,8192]{1,0:T(8,128)} %slot_ref.1) | copy-start | bytes 3145732
  11.8 16.6 %collective-permute-start.1 = (bf16[32,32,256]{2,1,0:T(8,128)(2,1)S(1)}, bf16[32,32,256]{2,1,0:T(8,128)(2,1)}, u32[]{:S(2)}, u32[]{:S(2)}) collective-permute-start(bf16[32,32,256]{2,1,0:T(8,128)(2,1)S(1)} %half_queries.1.refs_1_), channel_id=1, source_target_pairs={{0,2},{2,0},{1,3},{3,1},{4,6},{6,4},{5,7},{7,5},{8,10},{10,8},{9,1... | collective-permute-start | bytes 1572872 | tf_op jit(solution)/shard_map/ppermute | solution.py:373
  18.9 22.7 %all-to-all-start.1 = ((bf16[16,128,256]{2,1,0:T(8,128)(2,1)}), bf16[16,128,256]{2,1,0:T(8,128)(2,1)S(1)}, u32[]{:S(2)}, u32[]{:S(2)}) async-start(bf16[16,128,256]{2,1,0:T(8,128)(2,1)} %broadcast_in_dim.8), calls=%async_computation.1 | async-start | bytes 2097152 | tf_op jit(solution)/shard_map/all_to_all | solution.py:388
  27.2 6.5 %collective-permute-start.4 = (bf16[2,32,2048]{2,1,0:T(8,128)(2,1)S(1)}, bf16[2,32,2048]{2,1,0:T(8,128)(2,1)S(1)}, u32[]{:S(2)}, u32[]{:S(2)}) collective-permute-start(bf16[2,32,2048]{2,1,0:T(8,128)(2,1)S(1)} %get-tuple-element.18), channel_id=1, source_target_pairs={{0,2},{2,0},{1,3},{3,1},{4,6},{6,4},{5,7},{7,5},{8,10},{10,8},{9,1... | collective-permute-start | bytes 786440 | tf_op jit(solution)/shard_map/ppermute | solution.py:373
  28.4 7.0 %collective-permute-start = (bf16[32,32,256]{2,1,0:T(8,128)(2,1)S(1)}, bf16[32,32,256]{2,1,0:T(8,128)(2,1)S(1)}, u32[]{:S(2)}, u32[]{:S(2)}) collective-permute-start(bf16[32,32,256]{2,1,0:T(8,128)(2,1)S(1)} %half_queries.1.refs_1_), channel_id=1, source_target_pairs={{0,1},{1,0},{2,3},{3,2},{4,5},{5,4},{6,7},{7,6},{8,9},{9,8},{10,11... | collective-permute-start | bytes 1572872 | tf_op jit(solution)/shard_map/ppermute | solution.py:377
  28.4 7.8 %collective-permute-start.2 = (bf16[32,32,256]{2,1,0:T(8,128)(2,1)}, bf16[32,32,256]{2,1,0:T(8,128)(2,1)S(1)}, u32[]{:S(2)}, u32[]{:S(2)}) collective-permute-start(bf16[32,32,256]{2,1,0:T(8,128)(2,1)} %collective-permute-done.1.refs_3_), channel_id=1, source_target_pairs={{0,1},{1,0},{2,3},{3,2},{4,5},{5,4},{6,7},{7,6},{8,9},{9,8},{10,11... | collective-permute-start | bytes 1572872 | tf_op jit(solution)/shard_map/ppermute | solution.py:377
  33.6 1.7 %collective-permute-start.5 = (bf16[2,32,2048]{2,1,0:T(8,128)(2,1)S(1)}, bf16[2,32,2048]{2,1,0:T(8,128)(2,1)S(1)}, u32[]{:S(2)}, u32[]{:S(2)}) collective-permute-start(bf16[2,32,2048]{2,1,0:T(8,128)(2,1)S(1)} %collective-permute-done.4.refs_7_.refs_5_.refs_4_), channel_id=1, source_target_pairs={{0,1},{1,0},{2,3},{3,2},{4,5},{5,4},{6,7},{7,6},{8,9},{9,8},{10,11... | collective-permute-start | bytes 786440 | tf_op jit(solution)/shard_map/ppermute | solution.py:377
  33.7 1.7 %collective-permute-start.3 = (bf16[32,2048]{1,0:T(8,128)(2,1)S(1)}, bf16[32,2048]{1,0:T(8,128)(2,1)S(1)}, u32[]{:S(2)}, u32[]{:S(2)}) collective-permute-start(bf16[32,2048]{1,0:T(8,128)(2,1)S(1)} %get-tuple-element.17), channel_id=1, source_target_pairs={{0,1},{1,0},{2,3},{3,2},{4,5},{5,4},{6,7},{7,6},{8,9},{9,8},{10,11... | collective-permute-start | bytes 393224 | tf_op jit(solution)/shard_map/ppermute | solution.py:377
  35.4 0.8 copy-start.5
  36.2 0.8 copy-start.7
  41.6 1.0 copy-start.6
  42.7 1.0 copy-start.8
  50.5 1.3 %copy-start = (bf16[4096,256]{1,0:T(8,128)(2,1)}, bf16[4096,256]{1,0:T(8,128)(2,1)S(1)}, u32[]{:S(2)}) copy-start(bf16[4096,256]{1,0:T(8,128)(2,1)S(1)} %get-tuple-element.22.refs_2_) | copy-start | bytes 6291460
  63.8 11.1 %all-to-all-start.3 = ((f32[4,1,2048]{2,1,0:T(1,128)}), f32[4,1,2048]{2,1,0:T(1,128)S(1)}, u32[]{:S(2)}, u32[]{:S(2)}) async-start(f32[4,1,2048]{2,1,0:T(1,128)} %column_sums.1), calls=%async_computation.3 | async-start | bytes 65536 | tf_op jit(solution)/shard_map/all_to_all | solution.py:403
  67.0 4.4 %collective-permute-start.7 = (f32[128,1]{1,0:T(8,128)S(1)}, f32[128,1]{1,0:T(8,128)S(1)}, u32[]{:S(2)}, u32[]{:S(2)}) collective-permute-start(f32[128,1]{1,0:T(8,128)S(1)} %get-tuple-element.19.refs_7_.refs_6_.refs_4_), channel_id=1, source_target_pairs={{0,2},{2,0},{1,3},{3,1},{4,6},{6,4},{5,7},{7,5},{8,10},{10,8},{9,1... | collective-permute-start | bytes 1544 | tf_op jit(solution)/shard_map/ppermute | solution.py:373
  68.1 3.3 %collective-permute-start.6 = (f32[128,1]{1,0:T(8,128)S(1)}, f32[128,1]{1,0:T(8,128)S(1)}, u32[]{:S(2)}, u32[]{:S(2)}) collective-permute-start(f32[128,1]{1,0:T(8,128)S(1)} %get-tuple-element.19.refs_7_.refs_6_.refs_4_), channel_id=1, source_target_pairs={{0,1},{1,0},{2,3},{3,2},{4,5},{5,4},{6,7},{7,6},{8,9},{9,8},{10,11... | collective-permute-start | bytes 1544 | tf_op jit(solution)/shard_map/ppermute | solution.py:377
  71.4 1.3 %collective-permute-start.8 = (f32[128,1]{1,0:T(8,128)S(1)}, f32[128,1]{1,0:T(8,128)S(1)}, u32[]{:S(2)}, u32[]{:S(2)}) collective-permute-start(f32[128,1]{1,0:T(8,128)S(1)} %collective-permute-done.7.refs_9_.refs_8_.refs_6_), channel_id=1, source_target_pairs={{0,1},{1,0},{2,3},{3,2},{4,5},{5,4},{6,7},{7,6},{8,9},{9,8},{10,11... | collective-permute-start | bytes 1544 | tf_op jit(solution)/shard_map/ppermute | solution.py:377
  74.9 1.6 %copy-start.1 = (bf16[4096,256]{1,0:T(8,128)(2,1)S(1)}, bf16[4096,256]{1,0:T(8,128)(2,1)}, u32[]{:S(2)}) copy-start(bf16[4096,256]{1,0:T(8,128)(2,1)} %copy-done) | copy-start | bytes 6291460
  83.7 19.9 %all-to-all-start.4 = ((f16[16,128,256]{2,1,0:T(8,128)(2,1)}), f16[16,128,256]{2,1,0:T(8,128)(2,1)}, u32[]{:S(2)}, u32[]{:S(2)}) async-start(f16[16,128,256]{2,1,0:T(8,128)(2,1)} %bitcast.13), calls=%async_computation.4 | async-start | bytes 2097152 | tf_op jit(solution)/shard_map/all_to_all | solution.py:408
  92.7 2.0 %collective-permute-start.10 = (f16[32,32,256]{2,1,0:T(8,128)(2,1)S(1)}, f16[32,32,256]{2,1,0:T(8,128)(2,1)S(1)}, u32[]{:S(2)}, u32[]{:S(2)}) collective-permute-start(f16[32,32,256]{2,1,0:T(8,128)(2,1)S(1)} %convert_element_type.18), channel_id=1, source_target_pairs={{0,1},{1,0},{2,3},{3,2},{4,5},{5,4},{6,7},{7,6},{8,9},{9,8},{10,11... | collective-permute-start | bytes 1572872 | tf_op jit(solution)/shard_map/ppermute | solution.py:377
  92.8 21.6 %collective-permute-start.9 = (f32[32,32,256]{2,1,0:T(8,128)}, f32[32,32,256]{2,1,0:T(8,128)}, u32[]{:S(2)}, u32[]{:S(2)}) collective-permute-start(f32[32,32,256]{2,1,0:T(8,128)} %get-tuple-element.24), channel_id=1, source_target_pairs={{0,1},{1,0},{2,3},{3,2},{4,5},{5,4},{6,7},{7,6},{8,9},{9,8},{10,11... | collective-permute-start | bytes 3145736 | tf_op jit(solution)/shard_map/ppermute | solution.py:377
  94.7 19.7 %copy-start.3 = (bf16[32,32,256]{2,1,0:T(8,128)(2,1)S(1)}, bf16[32,32,256]{2,1,0:T(8,128)(2,1)}, u32[]{:S(2)}) copy-start(bf16[32,32,256]{2,1,0:T(8,128)(2,1)} %refs_2_.1) | copy-start | bytes 1572868
  95.7 17.6 %collective-permute-start.11 = (f16[32,32,256]{2,1,0:T(8,128)(2,1)}, f16[32,32,256]{2,1,0:T(8,128)(2,1)}, u32[]{:S(2)}, u32[]{:S(2)}) collective-permute-start(f16[32,32,256]{2,1,0:T(8,128)(2,1)} %add_convert_fusion), channel_id=1, source_target_pairs={{0,2},{2,0},{1,3},{3,1},{4,6},{6,4},{5,7},{7,5},{8,10},{10,8},{9,1... | collective-permute-start | bytes 1572872 | tf_op jit(solution)/shard_map/ppermute | solution.py:373
  105.6 16.1 %all-to-all-start.5 = ((f32[4,32,256]{2,1,0:T(8,128)}), f32[4,32,256]{2,1,0:T(8,128)S(1)}, u32[]{:S(2)}, u32[]{:S(2)}) async-start(f32[4,32,256]{2,1,0:T(8,128)} %bitcast.5), calls=%async_computation.5 | async-start | bytes 262144 | tf_op jit(solution)/shard_map/all_to_all | solution.py:415
  114.4 7.2 %copy-start.10 = (bf16[32,256]{1,0:T(8,128)(2,1)S(1)}, bf16[32,256]{1,0:T(8,128)(2,1)}, u32[]{:S(2)}) copy-start(bf16[32,256]{1,0:T(8,128)(2,1)} %caption_ref.3) | copy-start | bytes 49156

commit v5 on v4

--- a/solution.py
+++ b/solution.py
@@ -50,7 +50,7 @@
     here = pl.ds(pl.multiple_of(pl.program_id(0) * rows, rows), rows)
     for k in range(width // LANES):
         at = slice(k * LANES, (k + 1) * LANES)
-        units[k] = unit[:, at]
+        units[k, : rows * count] = unit[:, at]
         for q in range(count):
             half_ref[q, here, at] = units[k, pl.ds(q, rows, stride=count), :].astype(jnp.bfloat16)
 
@@ -64,7 +64,7 @@
         in_specs=[pl.BlockSpec((block, count, width), lambda s: (s, 0, 0))],
         out_specs=VMEM,
         out_shape=jax.ShapeDtypeStruct((count, rows, width), jnp.bfloat16),
-        scratch_shapes=[pltpu.VMEM((width // LANES, block * count, LANES), jnp.float32)],
+        scratch_shapes=[pltpu.VMEM((width // LANES, (block + 1) * count, LANES), jnp.float32)],
         compiler_params=params(16),
         name="half_queries",
     )(probes)
@@ -314,7 +314,7 @@
     added += (core_ref[:, here, :] + chip_ref[:, here, :].astype(jnp.float32)).reshape(count * block, width)
     halves = range(width // LANES)
     for k in halves:
-        sums[k] = added[:, k * LANES : (k + 1) * LANES]
+        sums[k, : count * block] = added[:, k * LANES : (k + 1) * LANES]
     for i in range(block):
         unit, scale = normalized_rows(probe_ref[i])
         half[i] = unit.astype(jnp.bfloat16)
@@ -343,7 +343,7 @@
         ],
         scratch_shapes=[
             pltpu.VMEM((count * block, e.shape[1]), jnp.bfloat16),
-            pltpu.VMEM((width // LANES, count * block, LANES), jnp.float32),
+            pltpu.VMEM((width // LANES, (count + 1) * block, LANES), jnp.float32),
             pltpu.VMEM((block, LANES), jnp.bfloat16),
             pltpu.VMEM((block, count, width), jnp.bfloat16),
         ],

time: 123 us -> 123 us (level)
  no operation moved by 1% of the time
where the time goes in v5:
time: 123 us; the launch traced here: 122 us
  starting transfers between devices  36.1 us (29%)
  waiting for transfers between devices  32.9 us (27%)
  Pallas kernels  26 us (21%)
  blocking collectives  11.2 us (9%)
  local copies, waits for them, and re-layouts  9.49 us (8%)
  other arithmetic  5.37 us (4%)
  between operations  1.44 us (1%)
    all_to_all x1, blocking collectives, shards(): column = lax.all_to_all(column, 'dp', 0, 0, tiled=True)  11.2 us
    unnamed x23, local copies, waits for them, and re-layouts  8.42 us
    ppermute x4, waiting for transfers between devices, swap_z(): return lax.ppermute(values, 'zp', SWAP)  8.06 us
    all_to_all x1, starting transfers between devices, shards(): dt = lax.all_to_all(dt, 'zo', 0, 0, tiled=True)  7.72 us
    all_to_all x1, starting transfers between devices, shards(): lax.all_to_all(half_texts(caption_vectors, outer), 'zo', 0, 0, tiled=True)  7.56 us
    all_to_all x1, starting transfers between devices, shards(): texts = lax.all_to_all(texts, 'dp', 0, 0, tiled=True).reshape(held, width)  7.03 us
    all_to_all x1, waiting for transfers between devices, shards(): lax.all_to_all(dt.astype(HALF).reshape(groups, outer * rows, width), 'dp'...  6.86 us
    pallas_call x1, Pallas kernels, scores(): pl.pallas_call(body, in_specs=[SMEM] + [VMEM] * 9, out_specs=[VMEM] * 4,...  6.8 us
  transfers between devices with their start and end apart: 17, of which 10 were waited for; matrix products, arithmetic and copies ran while one was open for 4% of the time, Pallas kernels for 9%

profile of v5, /device:TPU:32, one launch (start us, length us, event | category | flops | bytes accessed | tf_op | source)
XLA Modules:
  0.0 122.5 jit_solution(5554251996674597948)
XLA Ops:
  2.1 7.6 %all-to-all-start = ((bf16[4,32,256]{2,1,0:T(8,128)(2,1)}), bf16[4,32,256]{2,1,0:T(8,128)(2,1)S(1)}, u32[]{:S(2)}, u32[]{:S(2)}) async-start(bf16[4,32,256]{2,1,0:T(8,128)(2,1)} %half_texts.1), calls=%async_computation | async-start | bytes 131072 | tf_op jit(solution)/shard_map/all_to_all | solution.py:386
  10.7 1.1 half_queries.1.refs_1_
  11.8 1.1 collective-permute-start.1
  12.9 4.9 %all-to-all-done = bf16[4,32,256]{2,1,0:T(8,128)(2,1)S(1)} async-done(((bf16[4,32,256]{2,1,0:T(8,128)(2,1)}), bf16[4,32,256]{2,1,0:T(8,128)(2,1)S(1)}, u32[]{:S(2)}, u32[]{:S(2)}) %all-to-all-start) | async-done | bytes 65568 | tf_op jit(solution)/shard_map/all_to_all | solution.py:386
  17.9 1.1 broadcast_in_dim.8
  18.9 7.0 %all-to-all-start.1 = ((bf16[16,128,256]{2,1,0:T(8,128)(2,1)}), bf16[16,128,256]{2,1,0:T(8,128)(2,1)S(1)}, u32[]{:S(2)}, u32[]{:S(2)}) async-start(bf16[16,128,256]{2,1,0:T(8,128)(2,1)} %broadcast_in_dim.8), calls=%async_computation.1 | async-start | bytes 2097152 | tf_op jit(solution)/shard_map/all_to_all | solution.py:388
  26.0 1.2 slot_parts.1
  27.2 1.2 collective-permute-start.4
  28.9 4.8 %collective-permute-done.4.refs_7_.refs_5_.refs_4_ = bf16[2,32,2048]{2,1,0:T(8,128)(2,1)S(1)} collective-permute-done((bf16[2,32,2048]{2,1,0:T(8,128)(2,1)S(1)}, bf16[2,32,2048]{2,1,0:T(8,128)(2,1)S(1)}, u32[]{:S(2)}, u32[]{:S(2)}) %collective-permute-start.4) | collective-permute-done | bytes 262176 | tf_op jit(solution)/shard_map/ppermute | solution.py:373
  37.0 4.7 %all-to-all-done.1 = bf16[16,128,256]{2,1,0:T(8,128)(2,1)S(1)} async-done(((bf16[16,128,256]{2,1,0:T(8,128)(2,1)}), bf16[16,128,256]{2,1,0:T(8,128)(2,1)S(1)}, u32[]{:S(2)}, u32[]{:S(2)}) %all-to-all-start.1) | async-done | bytes 1048608 | tf_op jit(solution)/shard_map/all_to_all | solution.py:388
  41.6 1.0 copy-done.6
  42.7 1.0 copy-done.8
  43.7 6.8 %scores.1 = (bf16[4096,256]{1,0:T(8,128)(2,1)S(1)}, f32[128,2048]{1,0:T(8,128)S(1)}, f32[128,1]{1,0:T(8,128)S(1)}, f32[16,1,2048]{2,1,0:T(1,128)S(1)}) custom-call(f32[1]{0:T(128)S(6)} %copy.10.refs_0_, bf16[32,32,256]{2,1,0:T(8,128)(2,1)S(1)} %half_queries.1.refs_1_, bf16[32,32,256]{2,1,0:T(8,128)(2,1)S(1)} %copy-done.6, ...), custom_call_target="tpu_custom_call" | custom-call | tf_op jit(solution)/shard_map/scores/pallas_call | solution.py:164
  50.5 1.3 %copy-done = bf16[4096,256]{1,0:T(8,128)(2,1)} copy-done((bf16[4096,256]{1,0:T(8,128)(2,1)}, bf16[4096,256]{1,0:T(8,128)(2,1)S(1)}, u32[]{:S(2)}) %copy-start) | copy-done | bytes 2097176
  51.9 11.2 %all_to_all.30 = f32[16,1,2048]{2,1,0:T(1,128)S(1)} all-to-all(f32[16,1,2048]{2,1,0:T(1,128)S(1)} %get-tuple-element.21), channel_id=1, replica_groups=mesh['dp'=16,'zo'=4,'zp'=2,'c'=2] {'dp'}, dimensions={0} | all-to-all | bytes 262144 | tf_op jit(solution)/shard_map/all_to_all | solution.py:402
  63.8 3.3 %all-to-all-start.3 = ((f32[4,1,2048]{2,1,0:T(1,128)}), f32[4,1,2048]{2,1,0:T(1,128)S(1)}, u32[]{:S(2)}, u32[]{:S(2)}) async-start(f32[4,1,2048]{2,1,0:T(1,128)} %column_sums.1), calls=%async_computation.3 | async-start | bytes 65536 | tf_op jit(solution)/shard_map/all_to_all | solution.py:403
  67.0 1.1 collective-permute-start.7
  68.1 3.3 %collective-permute-done.7.refs_9_.refs_8_.refs_6_ = f32[128,1]{1,0:T(8,128)S(1)} collective-permute-done((f32[128,1]{1,0:T(8,128)S(1)}, f32[128,1]{1,0:T(8,128)S(1)}, u32[]{:S(2)}, u32[]{:S(2)}) %collective-permute-start.7) | collective-permute-done | bytes 544 | tf_op jit(solution)/shard_map/ppermute | solution.py:373
  71.4 1.2 %collective-permute-done.8.refs_10_.refs_9_.refs_7_ = f32[128,1]{1,0:T(8,128)S(1)} collective-permute-done((f32[128,1]{1,0:T(8,128)S(1)}, f32[128,1]{1,0:T(8,128)S(1)}, u32[]{:S(2)}, u32[]{:S(2)}) %collective-permute-start.8) | collective-permute-done | bytes 544 | tf_op jit(solution)/shard_map/ppermute | solution.py:377
  72.7 2.2 %all-to-all-done.3.refs_12_.refs_10_ = f32[4,1,2048]{2,1,0:T(1,128)S(1)} async-done(((f32[4,1,2048]{2,1,0:T(1,128)}), f32[4,1,2048]{2,1,0:T(1,128)S(1)}, u32[]{:S(2)}, u32[]{:S(2)}) %all-to-all-start.3) | async-done | bytes 32800 | tf_op jit(solution)/shard_map/all_to_all | solution.py:403
  74.9 1.6 %copy-done.1 = bf16[4096,256]{1,0:T(8,128)(2,1)S(1)} copy-done((bf16[4096,256]{1,0:T(8,128)(2,1)S(1)}, bf16[4096,256]{1,0:T(8,128)(2,1)}, u32[]{:S(2)}) %copy-start.1) | copy-done | bytes 2097176
  76.4 6.1 %text_gradients.1 = (f32[2048,256]{1,0:T(8,128)S(1)}, f32[8,128]{1,0:T(8,128)S(1)}) custom-call(f32[1]{0:T(128)S(6)} %copy.10.refs_0_, s32[1]{0:T(128)} %bitcast.refs_1_, bf16[4096,256]{1,0:T(8,128)(2,1)S(1)} %copy-done.1, bf16[32,2048]{1,0:T(8,128)(2,1)S(1)} %get-tuple-element.16.refs_5_.refs_3_.refs_2_, ...), custom_call_target="tpu_custom_call" | custom-call | tf_op jit(solution)/shard_map/text_gradients/pallas_call | solution.py:237
  82.5 1.2 convert_element_type.22
  83.7 4.5 %all-to-all-start.4 = ((f16[16,128,256]{2,1,0:T(8,128)(2,1)}), f16[16,128,256]{2,1,0:T(8,128)(2,1)}, u32[]{:S(2)}, u32[]{:S(2)}) async-start(f16[16,128,256]{2,1,0:T(8,128)(2,1)} %bitcast.13), calls=%async_computation.4 | async-start | bytes 2097152 | tf_op jit(solution)/shard_map/all_to_all | solution.py:408
  88.2 4.4 %query_gradients.1 = (f32[32,32,256]{2,1,0:T(8,128)}, f32[32,32,256]{2,1,0:T(8,128)S(1)}, f32[32,32,256]{2,1,0:T(8,128)S(1)}) custom-call(f32[1]{0:T(128)S(6)} %copy.10.refs_0_, f32[8,128]{1,0:T(8,128)S(1)} %get-tuple-element.23.refs_1_, bf16[32,2048]{1,0:T(8,128)(2,1)S(1)} %get-tuple-element.16.refs_5_.refs_3_.refs_2_, ...), custom_call_target="tpu_custom_call" | custom-call | tf_op jit(solution)/shard_map/query_gradients/pallas_call | solution.py:281
  93.3 1.4 %collective-permute-done.10 = f16[32,32,256]{2,1,0:T(8,128)(2,1)S(1)} collective-permute-done((f16[32,32,256]{2,1,0:T(8,128)(2,1)S(1)}, f16[32,32,256]{2,1,0:T(8,128)(2,1)S(1)}, u32[]{:S(2)}, u32[]{:S(2)}) %collective-permute-start.10) | collective-permute-done | bytes 524320 | tf_op jit(solution)/shard_map/ppermute | solution.py:377
  96.7 6.9 %all-to-all-done.4 = f16[16,128,256]{2,1,0:T(8,128)(2,1)} async-done(((f16[16,128,256]{2,1,0:T(8,128)(2,1)}), f16[16,128,256]{2,1,0:T(8,128)(2,1)}, u32[]{:S(2)}, u32[]{:S(2)}) %all-to-all-start.4) | async-done | bytes 1048608 | tf_op jit(solution)/shard_map/all_to_all | solution.py:408
  103.6 2.0 %convert_reduce_fusion = f32[128,256]{1,0:T(8,128)} fusion(f16[16,128,256]{2,1,0:T(8,128)(2,1)} %all-to-all-done.4), kind=kLoop, calls=%fused_computation | loop fusion | flops 1015808 | bytes 1179648 | tf_op jit(solution)/shard_map/reduce_sum | solution.py:414
  105.6 7.7 %all-to-all-start.5 = ((f32[4,32,256]{2,1,0:T(8,128)}), f32[4,32,256]{2,1,0:T(8,128)S(1)}, u32[]{:S(2)}, u32[]{:S(2)}) async-start(f32[4,32,256]{2,1,0:T(8,128)} %bitcast.5), calls=%async_computation.5 | async-start | bytes 262144 | tf_op jit(solution)/shard_map/all_to_all | solution.py:415
  113.3 1.1 convert_element_type.21.refs_12_
  114.5 4.3 %finish_queries.1 = (f32[32,32,256]{2,1,0:T(8,128)}, f32[32,256]{1,0:T(8,128)S(1)}) custom-call(f32[1]{0:T(128)S(6)} %copy.10.refs_0_, s32[1]{0:T(128)} %bitcast.refs_1_, bf16[32,32,256]{2,1,0:T(8,128)(2,1)S(1)} %copy-done.3, bf16[32,2048]{1,0:T(8,128)(2,1)S(1)} %get-tuple-element.16.refs_5_.refs_3_.refs_2_, ...), custom_call_target="tpu_custom_call" | custom-call | tf_op jit(solution)/shard_map/finish_queries/pallas_call | solution.py:335
  118.7 3.0 %all-to-all-done.5.block_ref = f32[4,32,256]{2,1,0:T(8,128)S(1)} async-done(((f32[4,32,256]{2,1,0:T(8,128)}), f32[4,32,256]{2,1,0:T(8,128)S(1)}, u32[]{:S(2)}, u32[]{:S(2)}) %all-to-all-start.5) | async-done | bytes 131104 | tf_op jit(solution)/shard_map/all_to_all | solution.py:415
  (41 shorter events, 9.8 us)
Async XLA Ops:
  0.6 0.7 copy-start.9
  2.1 15.8 %all-to-all-start = ((bf16[4,32,256]{2,1,0:T(8,128)(2,1)}), bf16[4,32,256]{2,1,0:T(8,128)(2,1)S(1)}, u32[]{:S(2)}, u32[]{:S(2)}) async-start(bf16[4,32,256]{2,1,0:T(8,128)(2,1)} %half_texts.1), calls=%async_computation | async-start | bytes 131072 | tf_op jit(solution)/shard_map/all_to_all | solution.py:386
  9.6 1.0 copy-start.2
  10.7 15.3 %copy-start.4 = (s32[32,8192]{1,0:T(8,128)S(1)}, s32[32,8192]{1,0:T(8,128)}, u32[]{:S(2)}) copy-start(s32[32,8192]{1,0:T(8,128)} %slot_ref.1) | copy-start | bytes 3145732
  11.8 16.6 %collective-permute-start.1 = (bf16[32,32,256]{2,1,0:T(8,128)(2,1)S(1)}, bf16[32,32,256]{2,1,0:T(8,128)(2,1)}, u32[]{:S(2)}, u32[]{:S(2)}) collective-permute-start(bf16[32,32,256]{2,1,0:T(8,128)(2,1)S(1)} %half_queries.1.refs_1_), channel_id=1, source_target_pairs={{0,2},{2,0},{1,3},{3,1},{4,6},{6,4},{5,7},{7,5},{8,10},{10,8},{9,1... | collective-permute-start | bytes 1572872 | tf_op jit(solution)/shard_map/ppermute | solution.py:373
  18.9 22.7 %all-to-all-start.1 = ((bf16[16,128,256]{2,1,0:T(8,128)(2,1)}), bf16[16,128,256]{2,1,0:T(8,128)(2,1)S(1)}, u32[]{:S(2)}, u32[]{:S(2)}) async-start(bf16[16,128,256]{2,1,0:T(8,128)(2,1)} %broadcast_in_dim.8), calls=%async_computation.1 | async-start | bytes 2097152 | tf_op jit(solution)/shard_map/all_to_all | solution.py:388
  27.2 6.5 %collective-permute-start.4 = (bf16[2,32,2048]{2,1,0:T(8,128)(2,1)S(1)}, bf16[2,32,2048]{2,1,0:T(8,128)(2,1)S(1)}, u32[]{:S(2)}, u32[]{:S(2)}) collective-permute-start(bf16[2,32,2048]{2,1,0:T(8,128)(2,1)S(1)} %get-tuple-element.18), channel_id=1, source_target_pairs={{0,2},{2,0},{1,3},{3,1},{4,6},{6,4},{5,7},{7,5},{8,10},{10,8},{9,1... | collective-permute-start | bytes 786440 | tf_op jit(solution)/shard_map/ppermute | solution.py:373
  28.4 7.0 %collective-permute-start = (bf16[32,32,256]{2,1,0:T(8,128)(2,1)S(1)}, bf16[32,32,256]{2,1,0:T(8,128)(2,1)S(1)}, u32[]{:S(2)}, u32[]{:S(2)}) collective-permute-start(bf16[32,32,256]{2,1,0:T(8,128)(2,1)S(1)} %half_queries.1.refs_1_), channel_id=1, source_target_pairs={{0,1},{1,0},{2,3},{3,2},{4,5},{5,4},{6,7},{7,6},{8,9},{9,8},{10,11... | collective-permute-start | bytes 1572872 | tf_op jit(solution)/shard_map/ppermute | solution.py:377
  28.4 7.8 %collective-permute-start.2 = (bf16[32,32,256]{2,1,0:T(8,128)(2,1)}, bf16[32,32,256]{2,1,0:T(8,128)(2,1)S(1)}, u32[]{:S(2)}, u32[]{:S(2)}) collective-permute-start(bf16[32,32,256]{2,1,0:T(8,128)(2,1)} %collective-permute-done.1.refs_3_), channel_id=1, source_target_pairs={{0,1},{1,0},{2,3},{3,2},{4,5},{5,4},{6,7},{7,6},{8,9},{9,8},{10,11... | collective-permute-start | bytes 1572872 | tf_op jit(solution)/shard_map/ppermute | solution.py:377
  33.6 1.7 %collective-permute-start.5 = (bf16[2,32,2048]{2,1,0:T(8,128)(2,1)S(1)}, bf16[2,32,2048]{2,1,0:T(8,128)(2,1)S(1)}, u32[]{:S(2)}, u32[]{:S(2)}) collective-permute-start(bf16[2,32,2048]{2,1,0:T(8,128)(2,1)S(1)} %collective-permute-done.4.refs_7_.refs_5_.refs_4_), channel_id=1, source_target_pairs={{0,1},{1,0},{2,3},{3,2},{4,5},{5,4},{6,7},{7,6},{8,9},{9,8},{10,11... | collective-permute-start | bytes 786440 | tf_op jit(solution)/shard_map/ppermute | solution.py:377
  33.7 1.7 %collective-permute-start.3 = (bf16[32,2048]{1,0:T(8,128)(2,1)S(1)}, bf16[32,2048]{1,0:T(8,128)(2,1)S(1)}, u32[]{:S(2)}, u32[]{:S(2)}) collective-permute-start(bf16[32,2048]{1,0:T(8,128)(2,1)S(1)} %get-tuple-element.17), channel_id=1, source_target_pairs={{0,1},{1,0},{2,3},{3,2},{4,5},{5,4},{6,7},{7,6},{8,9},{9,8},{10,11... | collective-permute-start | bytes 393224 | tf_op jit(solution)/shard_map/ppermute | solution.py:377
  35.4 0.8 copy-start.5
  36.2 0.8 copy-start.7
  41.6 1.0 copy-start.6
  42.7 1.0 copy-start.8
  50.5 1.3 %copy-start = (bf16[4096,256]{1,0:T(8,128)(2,1)}, bf16[4096,256]{1,0:T(8,128)(2,1)S(1)}, u32[]{:S(2)}) copy-start(bf16[4096,256]{1,0:T(8,128)(2,1)S(1)} %get-tuple-element.22.refs_2_) | copy-start | bytes 6291460
  63.8 11.1 %all-to-all-start.3 = ((f32[4,1,2048]{2,1,0:T(1,128)}), f32[4,1,2048]{2,1,0:T(1,128)S(1)}, u32[]{:S(2)}, u32[]{:S(2)}) async-start(f32[4,1,2048]{2,1,0:T(1,128)} %column_sums.1), calls=%async_computation.3 | async-start | bytes 65536 | tf_op jit(solution)/shard_map/all_to_all | solution.py:403
  67.0 4.4 %collective-permute-start.7 = (f32[128,1]{1,0:T(8,128)S(1)}, f32[128,1]{1,0:T(8,128)S(1)}, u32[]{:S(2)}, u32[]{:S(2)}) collective-permute-start(f32[128,1]{1,0:T(8,128)S(1)} %get-tuple-element.19.refs_7_.refs_6_.refs_4_), channel_id=1, source_target_pairs={{0,2},{2,0},{1,3},{3,1},{4,6},{6,4},{5,7},{7,5},{8,10},{10,8},{9,1... | collective-permute-start | bytes 1544 | tf_op jit(solution)/shard_map/ppermute | solution.py:373
  68.1 3.3 %collective-permute-start.6 = (f32[128,1]{1,0:T(8,128)S(1)}, f32[128,1]{1,0:T(8,128)S(1)}, u32[]{:S(2)}, u32[]{:S(2)}) collective-permute-start(f32[128,1]{1,0:T(8,128)S(1)} %get-tuple-element.19.refs_7_.refs_6_.refs_4_), channel_id=1, source_target_pairs={{0,1},{1,0},{2,3},{3,2},{4,5},{5,4},{6,7},{7,6},{8,9},{9,8},{10,11... | collective-permute-start | bytes 1544 | tf_op jit(solution)/shard_map/ppermute | solution.py:377
  71.4 1.3 %collective-permute-start.8 = (f32[128,1]{1,0:T(8,128)S(1)}, f32[128,1]{1,0:T(8,128)S(1)}, u32[]{:S(2)}, u32[]{:S(2)}) collective-permute-start(f32[128,1]{1,0:T(8,128)S(1)} %collective-permute-done.7.refs_9_.refs_8_.refs_6_), channel_id=1, source_target_pairs={{0,1},{1,0},{2,3},{3,2},{4,5},{5,4},{6,7},{7,6},{8,9},{9,8},{10,11... | collective-permute-start | bytes 1544 | tf_op jit(solution)/shard_map/ppermute | solution.py:377
  74.9 1.6 %copy-start.1 = (bf16[4096,256]{1,0:T(8,128)(2,1)S(1)}, bf16[4096,256]{1,0:T(8,128)(2,1)}, u32[]{:S(2)}) copy-start(bf16[4096,256]{1,0:T(8,128)(2,1)} %copy-done) | copy-start | bytes 6291460
  83.7 19.9 %all-to-all-start.4 = ((f16[16,128,256]{2,1,0:T(8,128)(2,1)}), f16[16,128,256]{2,1,0:T(8,128)(2,1)}, u32[]{:S(2)}, u32[]{:S(2)}) async-start(f16[16,128,256]{2,1,0:T(8,128)(2,1)} %bitcast.13), calls=%async_computation.4 | async-start | bytes 2097152 | tf_op jit(solution)/shard_map/all_to_all | solution.py:408
  92.7 2.0 %collective-permute-start.10 = (f16[32,32,256]{2,1,0:T(8,128)(2,1)S(1)}, f16[32,32,256]{2,1,0:T(8,128)(2,1)S(1)}, u32[]{:S(2)}, u32[]{:S(2)}) collective-permute-start(f16[32,32,256]{2,1,0:T(8,128)(2,1)S(1)} %convert_element_type.18), channel_id=1, source_target_pairs={{0,1},{1,0},{2,3},{3,2},{4,5},{5,4},{6,7},{7,6},{8,9},{9,8},{10,11... | collective-permute-start | bytes 1572872 | tf_op jit(solution)/shard_map/ppermute | solution.py:377
  92.8 21.6 %collective-permute-start.9 = (f32[32,32,256]{2,1,0:T(8,128)}, f32[32,32,256]{2,1,0:T(8,128)}, u32[]{:S(2)}, u32[]{:S(2)}) collective-permute-start(f32[32,32,256]{2,1,0:T(8,128)} %get-tuple-element.24), channel_id=1, source_target_pairs={{0,1},{1,0},{2,3},{3,2},{4,5},{5,4},{6,7},{7,6},{8,9},{9,8},{10,11... | collective-permute-start | bytes 3145736 | tf_op jit(solution)/shard_map/ppermute | solution.py:377
  94.7 19.7 %copy-start.3 = (bf16[32,32,256]{2,1,0:T(8,128)(2,1)S(1)}, bf16[32,32,256]{2,1,0:T(8,128)(2,1)}, u32[]{:S(2)}) copy-start(bf16[32,32,256]{2,1,0:T(8,128)(2,1)} %refs_2_.1) | copy-start | bytes 1572868
  95.7 17.6 %collective-permute-start.11 = (f16[32,32,256]{2,1,0:T(8,128)(2,1)}, f16[32,32,256]{2,1,0:T(8,128)(2,1)}, u32[]{:S(2)}, u32[]{:S(2)}) collective-permute-start(f16[32,32,256]{2,1,0:T(8,128)(2,1)} %add_convert_fusion), channel_id=1, source_target_pairs={{0,2},{2,0},{1,3},{3,1},{4,6},{6,4},{5,7},{7,5},{8,10},{10,8},{9,1... | collective-permute-start | bytes 1572872 | tf_op jit(solution)/shard_map/ppermute | solution.py:373
  105.6 16.1 %all-to-all-start.5 = ((f32[4,32,256]{2,1,0:T(8,128)}), f32[4,32,256]{2,1,0:T(8,128)S(1)}, u32[]{:S(2)}, u32[]{:S(2)}) async-start(f32[4,32,256]{2,1,0:T(8,128)} %bitcast.5), calls=%async_computation.5 | async-start | bytes 262144 | tf_op jit(solution)/shard_map/all_to_all | solution.py:415
  114.4 7.2 %copy-start.10 = (bf16[32,256]{1,0:T(8,128)(2,1)S(1)}, bf16[32,256]{1,0:T(8,128)(2,1)}, u32[]{:S(2)}) copy-start(bf16[32,256]{1,0:T(8,128)(2,1)} %caption_ref.3) | copy-start | bytes 49156

commit v6 on v5

--- a/solution.py
+++ b/solution.py
@@ -156,7 +156,7 @@
     count, rows, width = queries[0].shape
     held = texts.shape[0]
     images = 4 * rows
-    tile = min(512, held)
+    tile = min(1024, held)
 
     def body(*refs):
         score_kernel(tile, 4, *refs)
@@ -229,7 +229,7 @@
 def text_gradients(total, heat, first, stack, slots, rows, e, column):
     depth, width = stack.shape
     held = e.shape[1]
-    tile = min(512, held)
+    tile = min(1024, held)
 
     def body(*refs):
         text_grad_kernel(total, *refs)

time: 123 us -> 122 us (level)
  no operation moved by 1% of the time
where the time goes in v6:
time: 122 us; the launch traced here: 121 us
  starting transfers between devices  35.9 us (29%)
  waiting for transfers between devices  33 us (27%)
  Pallas kernels  25 us (20%)
  blocking collectives  11.2 us (9%)
  local copies, waits for them, and re-layouts  9.49 us (8%)
  other arithmetic  5.37 us (4%)
  between operations  1.44 us (1%)
    all_to_all x1, blocking collectives, shards(): column = lax.all_to_all(column, 'dp', 0, 0, tiled=True)  11.2 us
    unnamed x23, local copies, waits for them, and re-layouts  8.42 us
    ppermute x4, waiting for transfers between devices, swap_z(): return lax.ppermute(values, 'zp', SWAP)  8.06 us
    all_to_all x1, starting transfers between devices, shards(): dt = lax.all_to_all(dt, 'zo', 0, 0, tiled=True)  7.73 us
    all_to_all x1, starting transfers between devices, shards(): lax.all_to_all(half_texts(caption_vectors, outer), 'zo', 0, 0, tiled=True)  7.56 us
    all_to_all x1, starting transfers between devices, shards(): texts = lax.all_to_all(texts, 'dp', 0, 0, tiled=True).reshape(held, width)  7.03 us
    all_to_all x1, waiting for transfers between devices, shards(): lax.all_to_all(dt.astype(HALF).reshape(groups, outer * rows, width), 'dp'...  7.03 us
    pallas_call x1, Pallas kernels, scores(): pl.pallas_call(body, in_specs=[SMEM] + [VMEM] * 9, out_specs=[VMEM] * 4,...  6.24 us
  transfers between devices with their start and end apart: 17, of which 10 were waited for; matrix products, arithmetic and copies ran while one was open for 4% of the time, Pallas kernels for 9%

profile of v6, /device:TPU:32, one launch (start us, length us, event | category | flops | bytes accessed | tf_op | source)
XLA Modules:
  0.0 121.4 jit_solution(16120832522967814228)
XLA Ops:
  2.1 7.6 %all-to-all-start = ((bf16[4,32,256]{2,1,0:T(8,128)(2,1)}), bf16[4,32,256]{2,1,0:T(8,128)(2,1)S(1)}, u32[]{:S(2)}, u32[]{:S(2)}) async-start(bf16[4,32,256]{2,1,0:T(8,128)(2,1)} %half_texts.1), calls=%async_computation | async-start | bytes 131072 | tf_op jit(solution)/shard_map/all_to_all | solution.py:386
  9.6 1.0 copy-done.2
  10.7 1.1 half_queries.1.refs_1_
  11.8 1.1 collective-permute-start.1
  12.9 4.9 %all-to-all-done = bf16[4,32,256]{2,1,0:T(8,128)(2,1)S(1)} async-done(((bf16[4,32,256]{2,1,0:T(8,128)(2,1)}), bf16[4,32,256]{2,1,0:T(8,128)(2,1)S(1)}, u32[]{:S(2)}, u32[]{:S(2)}) %all-to-all-start) | async-done | bytes 65568 | tf_op jit(solution)/shard_map/all_to_all | solution.py:386
  17.9 1.1 broadcast_in_dim.8
  18.9 7.0 %all-to-all-start.1 = ((bf16[16,128,256]{2,1,0:T(8,128)(2,1)}), bf16[16,128,256]{2,1,0:T(8,128)(2,1)S(1)}, u32[]{:S(2)}, u32[]{:S(2)}) async-start(bf16[16,128,256]{2,1,0:T(8,128)(2,1)} %broadcast_in_dim.8), calls=%async_computation.1 | async-start | bytes 2097152 | tf_op jit(solution)/shard_map/all_to_all | solution.py:388
  26.0 1.2 slot_parts.1
  27.2 1.2 collective-permute-start.4
  28.9 4.8 %collective-permute-done.4.refs_7_.refs_5_.refs_4_ = bf16[2,32,2048]{2,1,0:T(8,128)(2,1)S(1)} collective-permute-done((bf16[2,32,2048]{2,1,0:T(8,128)(2,1)S(1)}, bf16[2,32,2048]{2,1,0:T(8,128)(2,1)S(1)}, u32[]{:S(2)}, u32[]{:S(2)}) %collective-permute-start.4) | collective-permute-done | bytes 262176 | tf_op jit(solution)/shard_map/ppermute | solution.py:373
  37.0 4.7 %all-to-all-done.1 = bf16[16,128,256]{2,1,0:T(8,128)(2,1)S(1)} async-done(((bf16[16,128,256]{2,1,0:T(8,128)(2,1)}), bf16[16,128,256]{2,1,0:T(8,128)(2,1)S(1)}, u32[]{:S(2)}, u32[]{:S(2)}) %all-to-all-start.1) | async-done | bytes 1048608 | tf_op jit(solution)/shard_map/all_to_all | solution.py:388
  41.6 1.0 copy-done.6
  43.7 6.2 %scores.1 = (bf16[4096,256]{1,0:T(8,128)(2,1)S(1)}, f32[128,2048]{1,0:T(8,128)S(1)}, f32[128,1]{1,0:T(8,128)S(1)}, f32[16,1,2048]{2,1,0:T(1,128)S(1)}) custom-call(f32[1]{0:T(128)S(6)} %copy.10.refs_0_, bf16[32,32,256]{2,1,0:T(8,128)(2,1)S(1)} %half_queries.1.refs_1_, bf16[32,32,256]{2,1,0:T(8,128)(2,1)S(1)} %copy-done.6, ...), custom_call_target="tpu_custom_call" | custom-call | tf_op jit(solution)/shard_map/scores/pallas_call | solution.py:164
  50.0 1.3 %copy-done = bf16[4096,256]{1,0:T(8,128)(2,1)} copy-done((bf16[4096,256]{1,0:T(8,128)(2,1)}, bf16[4096,256]{1,0:T(8,128)(2,1)S(1)}, u32[]{:S(2)}) %copy-start) | copy-done | bytes 2097176
  51.3 11.2 %all_to_all.30 = f32[16,1,2048]{2,1,0:T(1,128)S(1)} all-to-all(f32[16,1,2048]{2,1,0:T(1,128)S(1)} %get-tuple-element.21), channel_id=1, replica_groups=mesh['dp'=16,'zo'=4,'zp'=2,'c'=2] {'dp'}, dimensions={0} | all-to-all | bytes 262144 | tf_op jit(solution)/shard_map/all_to_all | solution.py:402
  63.2 3.3 %all-to-all-start.3 = ((f32[4,1,2048]{2,1,0:T(1,128)}), f32[4,1,2048]{2,1,0:T(1,128)S(1)}, u32[]{:S(2)}, u32[]{:S(2)}) async-start(f32[4,1,2048]{2,1,0:T(1,128)} %column_sums.1), calls=%async_computation.3 | async-start | bytes 65536 | tf_op jit(solution)/shard_map/all_to_all | solution.py:403
  66.5 1.1 collective-permute-start.7
  67.6 3.3 %collective-permute-done.7.refs_9_.refs_8_.refs_6_ = f32[128,1]{1,0:T(8,128)S(1)} collective-permute-done((f32[128,1]{1,0:T(8,128)S(1)}, f32[128,1]{1,0:T(8,128)S(1)}, u32[]{:S(2)}, u32[]{:S(2)}) %collective-permute-start.7) | collective-permute-done | bytes 544 | tf_op jit(solution)/shard_map/ppermute | solution.py:373
  70.9 1.2 %collective-permute-done.8.refs_10_.refs_9_.refs_7_ = f32[128,1]{1,0:T(8,128)S(1)} collective-permute-done((f32[128,1]{1,0:T(8,128)S(1)}, f32[128,1]{1,0:T(8,128)S(1)}, u32[]{:S(2)}, u32[]{:S(2)}) %collective-permute-start.8) | collective-permute-done | bytes 544 | tf_op jit(solution)/shard_map/ppermute | solution.py:377
  72.1 2.2 %all-to-all-done.3.refs_12_.refs_10_ = f32[4,1,2048]{2,1,0:T(1,128)S(1)} async-done(((f32[4,1,2048]{2,1,0:T(1,128)}), f32[4,1,2048]{2,1,0:T(1,128)S(1)}, u32[]{:S(2)}, u32[]{:S(2)}) %all-to-all-start.3) | async-done | bytes 32800 | tf_op jit(solution)/shard_map/all_to_all | solution.py:403
  74.3 1.6 %copy-done.1 = bf16[4096,256]{1,0:T(8,128)(2,1)S(1)} copy-done((bf16[4096,256]{1,0:T(8,128)(2,1)S(1)}, bf16[4096,256]{1,0:T(8,128)(2,1)}, u32[]{:S(2)}) %copy-start.1) | copy-done | bytes 2097176
  75.9 5.6 %text_gradients.1 = (f32[2048,256]{1,0:T(8,128)S(1)}, f32[8,128]{1,0:T(8,128)S(1)}) custom-call(f32[1]{0:T(128)S(6)} %copy.10.refs_0_, s32[1]{0:T(128)} %bitcast.refs_1_, bf16[4096,256]{1,0:T(8,128)(2,1)S(1)} %copy-done.1, bf16[32,2048]{1,0:T(8,128)(2,1)S(1)} %get-tuple-element.16.refs_5_.refs_3_.refs_2_, ...), custom_call_target="tpu_custom_call" | custom-call | tf_op jit(solution)/shard_map/text_gradients/pallas_call | solution.py:237
  81.5 1.2 convert_element_type.22
  82.6 4.3 %all-to-all-start.4 = ((f16[16,128,256]{2,1,0:T(8,128)(2,1)}), f16[16,128,256]{2,1,0:T(8,128)(2,1)}, u32[]{:S(2)}, u32[]{:S(2)}) async-start(f16[16,128,256]{2,1,0:T(8,128)(2,1)} %bitcast.13), calls=%async_computation.4 | async-start | bytes 2097152 | tf_op jit(solution)/shard_map/all_to_all | solution.py:408
  87.0 4.4 %query_gradients.1 = (f32[32,32,256]{2,1,0:T(8,128)}, f32[32,32,256]{2,1,0:T(8,128)S(1)}, f32[32,32,256]{2,1,0:T(8,128)S(1)}) custom-call(f32[1]{0:T(128)S(6)} %copy.10.refs_0_, f32[8,128]{1,0:T(8,128)S(1)} %get-tuple-element.23.refs_1_, bf16[32,2048]{1,0:T(8,128)(2,1)S(1)} %get-tuple-element.16.refs_5_.refs_3_.refs_2_, ...), custom_call_target="tpu_custom_call" | custom-call | tf_op jit(solution)/shard_map/query_gradients/pallas_call | solution.py:281
  92.1 1.4 %collective-permute-done.10 = f16[32,32,256]{2,1,0:T(8,128)(2,1)S(1)} collective-permute-done((f16[32,32,256]{2,1,0:T(8,128)(2,1)S(1)}, f16[32,32,256]{2,1,0:T(8,128)(2,1)S(1)}, u32[]{:S(2)}, u32[]{:S(2)}) %collective-permute-start.10) | collective-permute-done | bytes 524320 | tf_op jit(solution)/shard_map/ppermute | solution.py:377
  95.5 7.0 %all-to-all-done.4 = f16[16,128,256]{2,1,0:T(8,128)(2,1)} async-done(((f16[16,128,256]{2,1,0:T(8,128)(2,1)}), f16[16,128,256]{2,1,0:T(8,128)(2,1)}, u32[]{:S(2)}, u32[]{:S(2)}) %all-to-all-start.4) | async-done | bytes 1048608 | tf_op jit(solution)/shard_map/all_to_all | solution.py:408
  102.5 2.0 %convert_reduce_fusion = f32[128,256]{1,0:T(8,128)} fusion(f16[16,128,256]{2,1,0:T(8,128)(2,1)} %all-to-all-done.4), kind=kLoop, calls=%fused_computation | loop fusion | flops 1015808 | bytes 1179648 | tf_op jit(solution)/shard_map/reduce_sum | solution.py:414
  104.5 7.7 %all-to-all-start.5 = ((f32[4,32,256]{2,1,0:T(8,128)}), f32[4,32,256]{2,1,0:T(8,128)S(1)}, u32[]{:S(2)}, u32[]{:S(2)}) async-start(f32[4,32,256]{2,1,0:T(8,128)} %bitcast.5), calls=%async_computation.5 | async-start | bytes 262144 | tf_op jit(solution)/shard_map/all_to_all | solution.py:415
  112.2 1.1 convert_element_type.21.refs_12_
  113.4 4.3 %finish_queries.1 = (f32[32,32,256]{2,1,0:T(8,128)}, f32[32,256]{1,0:T(8,128)S(1)}) custom-call(f32[1]{0:T(128)S(6)} %copy.10.refs_0_, s32[1]{0:T(128)} %bitcast.refs_1_, bf16[32,32,256]{2,1,0:T(8,128)(2,1)S(1)} %copy-done.3, bf16[32,2048]{1,0:T(8,128)(2,1)S(1)} %get-tuple-element.16.refs_5_.refs_3_.refs_2_, ...), custom_call_target="tpu_custom_call" | custom-call | tf_op jit(solution)/shard_map/finish_queries/pallas_call | solution.py:335
  117.7 3.0 %all-to-all-done.5.block_ref = f32[4,32,256]{2,1,0:T(8,128)S(1)} async-done(((f32[4,32,256]{2,1,0:T(8,128)}), f32[4,32,256]{2,1,0:T(8,128)S(1)}, u32[]{:S(2)}, u32[]{:S(2)}) %all-to-all-start.5) | async-done | bytes 131104 | tf_op jit(solution)/shard_map/all_to_all | solution.py:415
  (41 shorter events, 9.8 us)
Async XLA Ops:
  0.6 0.7 copy-start.9
  2.1 15.8 %all-to-all-start = ((bf16[4,32,256]{2,1,0:T(8,128)(2,1)}), bf16[4,32,256]{2,1,0:T(8,128)(2,1)S(1)}, u32[]{:S(2)}, u32[]{:S(2)}) async-start(bf16[4,32,256]{2,1,0:T(8,128)(2,1)} %half_texts.1), calls=%async_computation | async-start | bytes 131072 | tf_op jit(solution)/shard_map/all_to_all | solution.py:386
  9.6 1.0 copy-start.2
  10.7 15.3 %copy-start.4 = (s32[32,8192]{1,0:T(8,128)S(1)}, s32[32,8192]{1,0:T(8,128)}, u32[]{:S(2)}) copy-start(s32[32,8192]{1,0:T(8,128)} %slot_ref.1) | copy-start | bytes 3145732
  11.8 16.6 %collective-permute-start.1 = (bf16[32,32,256]{2,1,0:T(8,128)(2,1)S(1)}, bf16[32,32,256]{2,1,0:T(8,128)(2,1)}, u32[]{:S(2)}, u32[]{:S(2)}) collective-permute-start(bf16[32,32,256]{2,1,0:T(8,128)(2,1)S(1)} %half_queries.1.refs_1_), channel_id=1, source_target_pairs={{0,2},{2,0},{1,3},{3,1},{4,6},{6,4},{5,7},{7,5},{8,10},{10,8},{9,1... | collective-permute-start | bytes 1572872 | tf_op jit(solution)/shard_map/ppermute | solution.py:373
  18.9 22.7 %all-to-all-start.1 = ((bf16[16,128,256]{2,1,0:T(8,128)(2,1)}), bf16[16,128,256]{2,1,0:T(8,128)(2,1)S(1)}, u32[]{:S(2)}, u32[]{:S(2)}) async-start(bf16[16,128,256]{2,1,0:T(8,128)(2,1)} %broadcast_in_dim.8), calls=%async_computation.1 | async-start | bytes 2097152 | tf_op jit(solution)/shard_map/all_to_all | solution.py:388
  27.2 6.5 %collective-permute-start.4 = (bf16[2,32,2048]{2,1,0:T(8,128)(2,1)S(1)}, bf16[2,32,2048]{2,1,0:T(8,128)(2,1)S(1)}, u32[]{:S(2)}, u32[]{:S(2)}) collective-permute-start(bf16[2,32,2048]{2,1,0:T(8,128)(2,1)S(1)} %get-tuple-element.18), channel_id=1, source_target_pairs={{0,2},{2,0},{1,3},{3,1},{4,6},{6,4},{5,7},{7,5},{8,10},{10,8},{9,1... | collective-permute-start | bytes 786440 | tf_op jit(solution)/shard_map/ppermute | solution.py:373
  28.4 7.0 %collective-permute-start = (bf16[32,32,256]{2,1,0:T(8,128)(2,1)S(1)}, bf16[32,32,256]{2,1,0:T(8,128)(2,1)S(1)}, u32[]{:S(2)}, u32[]{:S(2)}) collective-permute-start(bf16[32,32,256]{2,1,0:T(8,128)(2,1)S(1)} %half_queries.1.refs_1_), channel_id=1, source_target_pairs={{0,1},{1,0},{2,3},{3,2},{4,5},{5,4},{6,7},{7,6},{8,9},{9,8},{10,11... | collective-permute-start | bytes 1572872 | tf_op jit(solution)/shard_map/ppermute | solution.py:377
  28.4 7.8 %collective-permute-start.2 = (bf16[32,32,256]{2,1,0:T(8,128)(2,1)}, bf16[32,32,256]{2,1,0:T(8,128)(2,1)S(1)}, u32[]{:S(2)}, u32[]{:S(2)}) collective-permute-start(bf16[32,32,256]{2,1,0:T(8,128)(2,1)} %collective-permute-done.1.refs_3_), channel_id=1, source_target_pairs={{0,1},{1,0},{2,3},{3,2},{4,5},{5,4},{6,7},{7,6},{8,9},{9,8},{10,11... | collective-permute-start | bytes 1572872 | tf_op jit(solution)/shard_map/ppermute | solution.py:377
  33.6 1.7 %collective-permute-start.5 = (bf16[2,32,2048]{2,1,0:T(8,128)(2,1)S(1)}, bf16[2,32,2048]{2,1,0:T(8,128)(2,1)S(1)}, u32[]{:S(2)}, u32[]{:S(2)}) collective-permute-start(bf16[2,32,2048]{2,1,0:T(8,128)(2,1)S(1)} %collective-permute-done.4.refs_7_.refs_5_.refs_4_), channel_id=1, source_target_pairs={{0,1},{1,0},{2,3},{3,2},{4,5},{5,4},{6,7},{7,6},{8,9},{9,8},{10,11... | collective-permute-start | bytes 786440 | tf_op jit(solution)/shard_map/ppermute | solution.py:377
  33.7 1.7 %collective-permute-start.3 = (bf16[32,2048]{1,0:T(8,128)(2,1)S(1)}, bf16[32,2048]{1,0:T(8,128)(2,1)S(1)}, u32[]{:S(2)}, u32[]{:S(2)}) collective-permute-start(bf16[32,2048]{1,0:T(8,128)(2,1)S(1)} %get-tuple-element.17), channel_id=1, source_target_pairs={{0,1},{1,0},{2,3},{3,2},{4,5},{5,4},{6,7},{7,6},{8,9},{9,8},{10,11... | collective-permute-start | bytes 393224 | tf_op jit(solution)/shard_map/ppermute | solution.py:377
  35.4 0.8 copy-start.5
  36.2 0.8 copy-start.7
  41.6 1.0 copy-start.6
  42.7 1.0 copy-start.8
  50.0 1.3 %copy-start = (bf16[4096,256]{1,0:T(8,128)(2,1)}, bf16[4096,256]{1,0:T(8,128)(2,1)S(1)}, u32[]{:S(2)}) copy-start(bf16[4096,256]{1,0:T(8,128)(2,1)S(1)} %get-tuple-element.22.refs_2_) | copy-start | bytes 6291460
  63.2 11.1 %all-to-all-start.3 = ((f32[4,1,2048]{2,1,0:T(1,128)}), f32[4,1,2048]{2,1,0:T(1,128)S(1)}, u32[]{:S(2)}, u32[]{:S(2)}) async-start(f32[4,1,2048]{2,1,0:T(1,128)} %column_sums.1), calls=%async_computation.3 | async-start | bytes 65536 | tf_op jit(solution)/shard_map/all_to_all | solution.py:403
  66.5 4.4 %collective-permute-start.7 = (f32[128,1]{1,0:T(8,128)S(1)}, f32[128,1]{1,0:T(8,128)S(1)}, u32[]{:S(2)}, u32[]{:S(2)}) collective-permute-start(f32[128,1]{1,0:T(8,128)S(1)} %get-tuple-element.19.refs_7_.refs_6_.refs_4_), channel_id=1, source_target_pairs={{0,2},{2,0},{1,3},{3,1},{4,6},{6,4},{5,7},{7,5},{8,10},{10,8},{9,1... | collective-permute-start | bytes 1544 | tf_op jit(solution)/shard_map/ppermute | solution.py:373
  67.6 3.3 %collective-permute-start.6 = (f32[128,1]{1,0:T(8,128)S(1)}, f32[128,1]{1,0:T(8,128)S(1)}, u32[]{:S(2)}, u32[]{:S(2)}) collective-permute-start(f32[128,1]{1,0:T(8,128)S(1)} %get-tuple-element.19.refs_7_.refs_6_.refs_4_), channel_id=1, source_target_pairs={{0,1},{1,0},{2,3},{3,2},{4,5},{5,4},{6,7},{7,6},{8,9},{9,8},{10,11... | collective-permute-start | bytes 1544 | tf_op jit(solution)/shard_map/ppermute | solution.py:377
  70.9 1.3 %collective-permute-start.8 = (f32[128,1]{1,0:T(8,128)S(1)}, f32[128,1]{1,0:T(8,128)S(1)}, u32[]{:S(2)}, u32[]{:S(2)}) collective-permute-start(f32[128,1]{1,0:T(8,128)S(1)} %collective-permute-done.7.refs_9_.refs_8_.refs_6_), channel_id=1, source_target_pairs={{0,1},{1,0},{2,3},{3,2},{4,5},{5,4},{6,7},{7,6},{8,9},{9,8},{10,11... | collective-permute-start | bytes 1544 | tf_op jit(solution)/shard_map/ppermute | solution.py:377
  74.3 1.6 %copy-start.1 = (bf16[4096,256]{1,0:T(8,128)(2,1)S(1)}, bf16[4096,256]{1,0:T(8,128)(2,1)}, u32[]{:S(2)}) copy-start(bf16[4096,256]{1,0:T(8,128)(2,1)} %copy-done) | copy-start | bytes 6291460
  82.6 19.9 %all-to-all-start.4 = ((f16[16,128,256]{2,1,0:T(8,128)(2,1)}), f16[16,128,256]{2,1,0:T(8,128)(2,1)}, u32[]{:S(2)}, u32[]{:S(2)}) async-start(f16[16,128,256]{2,1,0:T(8,128)(2,1)} %bitcast.13), calls=%async_computation.4 | async-start | bytes 2097152 | tf_op jit(solution)/shard_map/all_to_all | solution.py:408
  91.5 2.0 %collective-permute-start.10 = (f16[32,32,256]{2,1,0:T(8,128)(2,1)S(1)}, f16[32,32,256]{2,1,0:T(8,128)(2,1)S(1)}, u32[]{:S(2)}, u32[]{:S(2)}) collective-permute-start(f16[32,32,256]{2,1,0:T(8,128)(2,1)S(1)} %convert_element_type.18), channel_id=1, source_target_pairs={{0,1},{1,0},{2,3},{3,2},{4,5},{5,4},{6,7},{7,6},{8,9},{9,8},{10,11... | collective-permute-start | bytes 1572872 | tf_op jit(solution)/shard_map/ppermute | solution.py:377
  91.6 21.8 %collective-permute-start.9 = (f32[32,32,256]{2,1,0:T(8,128)}, f32[32,32,256]{2,1,0:T(8,128)}, u32[]{:S(2)}, u32[]{:S(2)}) collective-permute-start(f32[32,32,256]{2,1,0:T(8,128)} %get-tuple-element.24), channel_id=1, source_target_pairs={{0,1},{1,0},{2,3},{3,2},{4,5},{5,4},{6,7},{7,6},{8,9},{9,8},{10,11... | collective-permute-start | bytes 3145736 | tf_op jit(solution)/shard_map/ppermute | solution.py:377
  93.5 19.9 %copy-start.3 = (bf16[32,32,256]{2,1,0:T(8,128)(2,1)S(1)}, bf16[32,32,256]{2,1,0:T(8,128)(2,1)}, u32[]{:S(2)}) copy-start(bf16[32,32,256]{2,1,0:T(8,128)(2,1)} %refs_2_.1) | copy-start | bytes 1572868
  94.5 17.8 %collective-permute-start.11 = (f16[32,32,256]{2,1,0:T(8,128)(2,1)}, f16[32,32,256]{2,1,0:T(8,128)(2,1)}, u32[]{:S(2)}, u32[]{:S(2)}) collective-permute-start(f16[32,32,256]{2,1,0:T(8,128)(2,1)} %add_convert_fusion), channel_id=1, source_target_pairs={{0,2},{2,0},{1,3},{3,1},{4,6},{6,4},{5,7},{7,5},{8,10},{10,8},{9,1... | collective-permute-start | bytes 1572872 | tf_op jit(solution)/shard_map/ppermute | solution.py:373
  104.5 16.1 %all-to-all-start.5 = ((f32[4,32,256]{2,1,0:T(8,128)}), f32[4,32,256]{2,1,0:T(8,128)S(1)}, u32[]{:S(2)}, u32[]{:S(2)}) async-start(f32[4,32,256]{2,1,0:T(8,128)} %bitcast.5), calls=%async_computation.5 | async-start | bytes 262144 | tf_op jit(solution)/shard_map/all_to_all | solution.py:415
  113.4 7.2 %copy-start.10 = (bf16[32,256]{1,0:T(8,128)(2,1)S(1)}, bf16[32,256]{1,0:T(8,128)(2,1)}, u32[]{:S(2)}) copy-start(bf16[32,256]{1,0:T(8,128)(2,1)} %caption_ref.3) | copy-start | bytes 49156
